TPU v7x, 32 devices: a whole 2x2x4 slice. The times are simulated.
32 devices in a mesh: group: 8 (over z, x), fsdp: 4 (over y, core).
Axes of the slice: x: 2, y: 2, z: 4, core: 2. Of those that a mesh axis runs over, the one named last changes fastest.
Arguments:
- tokens: bfloat16 [2, 8, 1024, 2048], P(None, 'group', 'fsdp'), may hold values from -6 to 6
- segment_ids: int32 [2, 8, 1024], P(None, 'group', 'fsdp'), may hold values from 0 to 1023, as said below
- cotangent: bfloat16 [2, 8, 1024, 2048], P(None, 'group', 'fsdp'), may hold values from -6 to 6
- norm_gain: bfloat16 [2048], P('fsdp'), may hold values from 0.099609375 to 1.8984375
- in_weight: bfloat16 [2048, 8512], P('fsdp'), may hold values from -0.125 to 0.125
- conv_weight: bfloat16 [4, 4352], P(None, 'fsdp'), may hold values from -3 to 3
- conv_bias: bfloat16 [4352], P('fsdp'), may hold values from -3 to 3
- dt_bias: bfloat16 [64], P('fsdp'), may hold values from -5 to -2
- a_log: bfloat16 [64], P('fsdp'), may hold values from -4 to 1
- skip_d: bfloat16 [64], P('fsdp'), may hold values from 0.5 to 2
- inner_gain: bfloat16 [4096], P('fsdp'), may hold values from 0.099609375 to 1.8984375
- out_weight: bfloat16 [4096, 2048], P('fsdp'), may hold values from -0.09375 to 0.09375
Outputs:
- mixed: bfloat16 [2, 8, 1024, 2048], P(None, 'group', 'fsdp')
- grad_tokens: bfloat16 [2, 8, 1024, 2048], P(None, 'group', 'fsdp')
- grad_norm_gain: float32 [2048], P('fsdp')
- grad_in_weight: float32 [2048, 8512], P('fsdp')
- grad_conv_weight: float32 [4, 4352], P(None, 'fsdp')
- grad_conv_bias: float32 [4352], P('fsdp')
- grad_dt_bias: float32 [64], P('fsdp')
- grad_a_log: float32 [64], P('fsdp')
- grad_skip_d: float32 [64], P('fsdp')
- grad_inner_gain: float32 [4096], P('fsdp')
- grad_out_weight: float32 [4096, 2048], P('fsdp')
Inputs may be any that keep to these rules, and one draw needn't show every extreme that they name: Within each sequence segment_ids never falls and equals the position of its document's first token; documents hold 200 to 2000 tokens except a sequence's last two, which may be shorter; of the 2 sequences at each index along the second dimension, one drawn from the seed is a single document.
All inputs are finite; a program needn't handle non-finite values.
Results may differ from a plain program's by a relative error of at most 0.0084.
Values may be sent and summed in bfloat16 or wider, within the bound.
No kernel may reach another device: no remote copies, remote signals or barrier semaphores. Data moves between devices by JAX's collectives and lax.ppermute only.
A program may use at most 448 MiB of HBM per device.

v0:
```python
from functools import partial

import jax
import jax.numpy as jnp
from jax import lax
from jax.sharding import PartitionSpec as P

INNER = 4096
HEADS = 64
HEADDIM = 64
STATE = 128
CONV = 4
XBC = 4352


EPSILON = 1e-05
HIGHEST = lax.Precision.HIGHEST


def passed_along(value, axis, steps):
    count = lax.axis_size(axis)
    first, last = (max(0, -steps), min(count, count - steps))
    return lax.ppermute(value, axis, [(source, source + steps) for source in range(first, last)])


def prefix(value, axis, join, neutral, backward):
    count, mine = (lax.axis_size(axis), lax.axis_index(axis))
    pieces = jax.tree.map(lambda part: lax.all_gather(part, axis), value)
    if backward:
        pieces = jax.tree.map(lambda part: part[::-1], pieces)
        mine = count - 1 - mine
    running = jax.tree.map(
        lambda part, zero: jnp.full_like(part, 0) + jnp.asarray(zero, part.dtype), value, neutral
    )

    def turn(position, running):
        longer = join(running, jax.tree.map(lambda part: part[position], pieces))
        return jax.tree.map(lambda new, old: jnp.where(position < mine, new, old), longer, running)

    return lax.fori_loop(0, count - 1, turn, running)


def rms_scale(values, gain):
    return values * lax.rsqrt(jnp.mean(values * values, axis=-1, keepdims=True) + EPSILON) * gain


def rounded(values):
    return lax.optimization_barrier(values.astype(jnp.bfloat16)).astype(jnp.float32)


def conv_part(seg_ids, positions, conv_ext, dt_raw, conv_weight, conv_bias, dt_bias, a_log):
    tok_count = dt_raw.shape[0]
    conv_sum = conv_bias[None, :] + jnp.zeros((tok_count, conv_bias.shape[0]), jnp.float32)
    for offset in range(CONV):
        visible = seg_ids <= positions - (CONV - 1) + offset
        conv_sum = (
            conv_sum
            + conv_weight[offset][None, :]
            * conv_ext[offset : offset + tok_count]
            * visible[:, None]
        )
    step_size = jax.nn.softplus(dt_raw + dt_bias[None, :])
    return (jax.nn.silu(conv_sum), step_size, step_size * (-jnp.exp(a_log))[None, :])


def state_part(seg_ids, start, x_heads, b_input, step_size, log_decay):
    running = jnp.cumsum(log_decay, axis=0)
    outflow = (
        jnp.exp(running[-1][None, :] - running) * (seg_ids == seg_ids[-1])[:, None] * step_size
    )
    fresh = jnp.einsum("shp,sn->hpn", x_heads * outflow[:, :, None], b_input, precision=HIGHEST)
    passing = jnp.exp(running[-1]) * (seg_ids[-1] < start)
    return (fresh, passing)


def tail_part(
    seg_ids,
    positions,
    start,
    x_heads,
    b_input,
    c_output,
    step_size,
    log_decay,
    skip_gain,
    entering,
    gate_branch,
    inner_gain,
):
    tok_count = x_heads.shape[0]
    running = jnp.cumsum(log_decay, axis=0)
    by_head = running.T
    causal = positions[None, :] <= positions[:, None]
    linked = (seg_ids[:, None] == seg_ids[None, :]) & causal
    spread = by_head[:, :, None] - by_head[:, None, :]
    kernel = jnp.where(linked[None], jnp.exp(jnp.where(linked[None], spread, 0.0)), 0.0)
    gram_matrix = jnp.dot(c_output, b_input.T, precision=HIGHEST)
    mixing = gram_matrix[None] * kernel * step_size.T[:, None, :]
    inside = jnp.einsum("hts,shp->thp", mixing, x_heads, precision=HIGHEST)
    inflow = jnp.exp(running) * (seg_ids < start)[:, None]
    carried = jnp.einsum("tn,hpn->thp", c_output, entering, precision=HIGHEST) * inflow[:, :, None]
    ssm_out = (inside + carried + skip_gain[None, :, None] * x_heads).reshape(tok_count, -1)
    return rms_scale(ssm_out * jax.nn.silu(gate_branch), inner_gain)


def chain(earlier, later):
    return (earlier[0] * later[0], later[0][:, None, None] * earlier[1] + later[1])


def on_device(
    tokens,
    segment_ids,
    cotangent,
    norm_gain,
    in_weight,
    conv_weight,
    conv_bias,
    dt_bias,
    a_log,
    skip_d,
    inner_gain,
    out_weight,
):
    micro_count = tokens.shape[0]
    tok_count = tokens.shape[2]
    start = lax.axis_index("fsdp") * tok_count
    positions = start + jnp.arange(tok_count, dtype=jnp.int32)
    shards = (
        norm_gain,
        in_weight,
        conv_weight,
        conv_bias,
        dt_bias,
        a_log,
        skip_d,
        inner_gain,
        out_weight,
    )
    identity = (jnp.ones((HEADS,), jnp.float32), jnp.zeros((HEADS, HEADDIM, STATE), jnp.float32))
    kept = (
        lax.all_gather(shards[0], "fsdp", axis=0, tiled=True),
        lax.all_gather(shards[1], "fsdp", axis=0, tiled=True),
        lax.all_gather(shards[2], "fsdp", axis=1, tiled=True),
        lax.all_gather(shards[3], "fsdp", axis=0, tiled=True),
        lax.all_gather(shards[4], "fsdp", axis=0, tiled=True),
        lax.all_gather(shards[5], "fsdp", axis=0, tiled=True),
        lax.all_gather(shards[6], "fsdp", axis=0, tiled=True),
        lax.all_gather(shards[7], "fsdp", axis=0, tiled=True),
        lax.all_gather(shards[8], "fsdp", axis=0, tiled=True),
    )
    totals = None
    mixed_rows = []
    grad_rows = []
    for micro_index in range(micro_count):
        gain_norm = kept[0].astype(jnp.float32)
        weight_in = kept[1]
        conv_taps = kept[2].astype(jnp.float32)
        conv_shift = kept[3].astype(jnp.float32)
        bias_step = kept[4].astype(jnp.float32)
        rate_log = kept[5].astype(jnp.float32)
        skip_gain = kept[6].astype(jnp.float32)
        gain_inner = kept[7].astype(jnp.float32)
        weight_out = kept[8]
        tok_rows = tokens[micro_index, 0].astype(jnp.float32)
        seg_ids = segment_ids[micro_index, 0]
        normed_in, norm_back = jax.vjp(rms_scale, tok_rows, gain_norm)
        normed_low = normed_in.astype(jnp.bfloat16)
        projected = jnp.dot(normed_low, weight_in, preferred_element_type=jnp.float32)
        gate_branch = projected[:, :INNER]
        conv_low = projected[:, INNER : INNER + XBC].astype(jnp.bfloat16)
        dt_raw = projected[:, INNER + XBC :]
        halo_rows = passed_along(conv_low[tok_count - (CONV - 1) :], "fsdp", 1)
        conv_ext = jnp.concatenate([halo_rows, conv_low], axis=0).astype(jnp.float32)
        (activated, step_size, log_decay), conv_back = jax.vjp(
            partial(conv_part, seg_ids, positions),
            conv_ext,
            dt_raw,
            conv_taps,
            conv_shift,
            bias_step,
            rate_log,
        )
        act_low = rounded(activated)
        x_heads = act_low[:, :INNER].reshape(tok_count, HEADS, HEADDIM)
        b_input = act_low[:, INNER : INNER + STATE]
        c_output = act_low[:, INNER + STATE :]
        (fresh, passing), state_back = jax.vjp(
            partial(state_part, seg_ids, start), x_heads, b_input, step_size, log_decay
        )
        _, entering = prefix((passing, fresh), "fsdp", chain, identity, False)
        gated_out, tail_back = jax.vjp(
            partial(tail_part, seg_ids, positions, start),
            x_heads,
            b_input,
            c_output,
            step_size,
            log_decay,
            skip_gain,
            entering,
            gate_branch,
            gain_inner,
        )
        gated_low = gated_out.astype(jnp.bfloat16)
        mixed_rows.append(
            (tok_rows + jnp.dot(gated_low, weight_out, preferred_element_type=jnp.float32)).astype(
                jnp.bfloat16
            )
        )
        weight_in = kept[1]
        weight_out = kept[8]
        cot_low = cotangent[micro_index, 0]
        grad_gated = rounded(jnp.dot(cot_low, weight_out.T, preferred_element_type=jnp.float32))
        (
            grad_heads,
            grad_input,
            grad_output,
            grad_step,
            grad_decay,
            grad_skip,
            grad_entering,
            grad_gate,
            grad_inner,
        ) = tail_back(grad_gated)
        _, leaving = prefix((passing, grad_entering), "fsdp", chain, identity, True)
        grad_passing = jnp.sum(leaving * entering, axis=(1, 2))
        more_heads, more_input, more_step, more_decay = state_back((leaving, grad_passing))
        grad_act = jnp.concatenate(
            [
                (grad_heads + more_heads).reshape(tok_count, INNER),
                grad_input + more_input,
                grad_output,
            ],
            axis=1,
        )
        grad_ext, grad_dtraw, grad_taps, grad_shift, grad_bias_step, grad_rate_log = conv_back(
            (grad_act, grad_step + more_step, grad_decay + more_decay)
        )
        returned = passed_along(grad_ext[: CONV - 1].astype(jnp.bfloat16), "fsdp", -1).astype(
            jnp.float32
        )
        grad_conv = grad_ext[CONV - 1 :].at[tok_count - (CONV - 1) :].add(returned)
        grad_proj = jnp.concatenate([grad_gate, grad_conv, grad_dtraw], axis=1).astype(jnp.bfloat16)
        grad_normed = jnp.dot(grad_proj, weight_in.T, preferred_element_type=jnp.float32)
        normed_cols, gated_cols = (
            lax.all_to_all(normed_low, "fsdp", split_axis=1, concat_axis=0, tiled=True),
            lax.all_to_all(gated_low, "fsdp", split_axis=1, concat_axis=0, tiled=True),
        )
        grad_inw = jnp.dot(
            normed_cols.T,
            lax.all_gather(grad_proj, "fsdp", axis=0, tiled=True),
            preferred_element_type=jnp.float32,
        )
        grad_outw = jnp.dot(
            gated_cols.T,
            lax.all_gather(cot_low, "fsdp", axis=0, tiled=True),
            preferred_element_type=jnp.float32,
        )
        grad_from_norm, grad_gain_norm = norm_back(grad_normed)
        grad_rows.append((cot_low.astype(jnp.float32) + grad_from_norm).astype(jnp.bfloat16))
        local_grads = (
            grad_gain_norm,
            grad_inw,
            grad_taps,
            grad_shift,
            grad_bias_step,
            grad_rate_log,
            grad_skip,
            grad_inner,
            grad_outw,
        )
        totals = local_grads if totals is None else jax.tree.map(jnp.add, totals, local_grads)
    totals = lax.psum(
        (
            lax.psum_scatter(totals[0], "fsdp", scatter_dimension=0, tiled=True),
            totals[1],
            lax.psum_scatter(totals[2], "fsdp", scatter_dimension=1, tiled=True),
            lax.psum_scatter(totals[3], "fsdp", scatter_dimension=0, tiled=True),
            lax.psum_scatter(totals[4], "fsdp", scatter_dimension=0, tiled=True),
            lax.psum_scatter(totals[5], "fsdp", scatter_dimension=0, tiled=True),
            lax.psum_scatter(totals[6], "fsdp", scatter_dimension=0, tiled=True),
            lax.psum_scatter(totals[7], "fsdp", scatter_dimension=0, tiled=True),
            totals[8],
        ),
        "group",
    )
    mixed_out = jnp.stack(mixed_rows, axis=0)[:, None]
    grad_tok = jnp.stack(grad_rows, axis=0)[:, None]
    return (
        mixed_out,
        grad_tok,
        totals[0],
        totals[1],
        totals[2],
        totals[3],
        totals[4],
        totals[5],
        totals[6],
        totals[7],
        totals[8],
    )


def solution(mesh):
    in_specs = (
        P(None, "group", "fsdp", None),
        P(None, "group", "fsdp"),
        P(None, "group", "fsdp", None),
        P("fsdp"),
        P("fsdp", None),
        P(None, "fsdp"),
        P("fsdp"),
        P("fsdp"),
        P("fsdp"),
        P("fsdp"),
        P("fsdp"),
        P("fsdp", None),
    )
    out_specs = (
        P(None, "group", "fsdp", None),
        P(None, "group", "fsdp", None),
        P("fsdp"),
        P("fsdp", None),
        P(None, "fsdp"),
        P("fsdp"),
        P("fsdp"),
        P("fsdp"),
        P("fsdp"),
        P("fsdp"),
        P("fsdp", None),
    )
    return jax.shard_map(
        on_device, mesh=mesh, in_specs=in_specs, out_specs=out_specs, check_vma=False
    )
```

profile of v0, /device:TPU:0, one launch (start us, length us, event | category | flops | bytes accessed | tf_op | source)
XLA Modules:
  0.0 1908.0 jit_solution(6642374672870304193)
XLA Ops:
  40.8 182.9 %all-gather.21.cloned.1.call-done = bf16[2048,8512]{0,1:T(8,128)(2,1)} async-done(((bf16[512,8512]{0,1:T(8,128)(2,1)}), bf16[2048,8512]{0,1:T(8,128)(2,1)}) %all-gather.21.cloned.1.call-update) | async-done | bytes 34865168 | tf_op jit(solution)/shard_map/all_gather | solution.py:142
  223.8 20.3 %fusion.247 = (bf16[256,8512]{0,1:T(8,128)(2,1)}, f32[256,8512]{0,1:T(8,128)S(1)}) fusion(bf16[2048,8512]{0,1:T(8,128)(2,1)} %all-gather.21.cloned.1.call-done, f32[256]{0:T(256)S(1)} %fusion.216, f32[2048]{0:T(1024)S(1)} %bitcast.510, bf16[2,1,256,2048]{3,2,1,0:T(8,128)(2,1)S(1)} %copy-done.21), kind=kOutput, calls=%fused_computation.409 | convolution fusion | flops 8929755136 | bytes 48997376 | tf_op jit(solution)/shard_map/dot_general | solution.py:168
  244.2 23.3 %fusion.248 = (bf16[256,8512]{0,1:T(8,128)(2,1)}, f32[256,8512]{0,1:T(8,128)}) fusion(bf16[2048,8512]{0,1:T(8,128)(2,1)} %all-gather.21.cloned.1.call-done, f32[2048]{0:T(1024)S(1)} %bitcast.511, f32[256]{0:T(256)S(1)} %fusion.214, bf16[2,1,256,2048]{3,2,1,0:T(8,128)(2,1)S(1)} %copy-done.21), kind=kOutput, calls=%fused_computation.410 | convolution fusion | flops 8929755136 | bytes 48997376 | tf_op jit(solution)/shard_map/dot_general | solution.py:168
  367.3 24.6 %all-gather.29.cloned.1.call-done = f32[256,64,128]{2,1,0:T(8,128)} async-done(((f32[64,64,128]{2,1,0:T(8,128)}), f32[256,64,128]{2,1,0:T(8,128)}) %all-gather.29.cloned.1.call-update) | async-done | bytes 8388624 | tf_op jit(solution)/shard_map/all_gather | solution.py:28
  430.3 22.0 %all-gather.31.cloned.1.call-done = f32[256,64,128]{2,1,0:T(8,128)} async-done(((f32[64,64,128]{2,1,0:T(8,128)}), f32[256,64,128]{2,1,0:T(8,128)}) %all-gather.31.cloned.1.call-update) | async-done | bytes 8388624 | tf_op jit(solution)/shard_map/all_gather | solution.py:28
  463.5 13.9 fusion.70
  531.4 21.2 %fusion.19 = (f32[64,256]{1,0:T(8,128)S(1)}, f32[64,256]{1,0:T(8,128)S(1)}, f32[64,256]{1,0:T(8,128)}, f32[256,256]{1,0:T(8,128)S(1)}) fusion(f32[64,256]{1,0:T(8,128)S(1)} %copy-done.112, f32[64,256]{1,0:T(8,128)S(1)} %copy-done.98, f32[256,256]{1,0:T(8,128)S(1)} %copy-done.79, pred[256,256]{1,0:T(8,128)(4,1)S(1)} %get-tuple-element.722, ...), kind=kOutput, calls=%fused_computation.32 | convolution fusion | flops 3284025344 | bytes 7208960 | tf_op jit(solution)/shard_map/transpose(jvp(hts,shp->thp))/dot_general | solution.py:99
  552.6 21.2 %fusion.21 = (f32[64,256]{1,0:T(8,128)S(1)}, f32[64,256]{1,0:T(8,128)S(1)}, f32[64,256]{1,0:T(8,128)}, f32[256,256]{1,0:T(8,128)S(1)}) fusion(f32[64,256]{1,0:T(8,128)S(1)} %copy-done.109, f32[64,256]{1,0:T(8,128)S(1)} %copy-done.101, f32[256,256]{1,0:T(8,128)S(1)} %fusion.194, pred[256,256]{1,0:T(8,128)(4,1)S(1)} %copy-done.104, ...), kind=kOutput, calls=%fused_computation.34 | convolution fusion | flops 3284025344 | bytes 7208960 | tf_op jit(solution)/shard_map/transpose(jvp(hts,shp->thp))/dot_general | solution.py:99
  648.7 16.2 fusion.69
  666.7 16.6 fusion.68
  691.1 20.4 %multiply_reduce_fusion.11 = (f32[4352]{0:T(1024)}, f32[4352]{0:T(1024)}, f32[4352]{0:T(1024)}, f32[4352]{0:T(1024)S(1)}, f32[4352]{0:T(1024)}, /*index=5*/f32[256,4352]{0,1:T(8,128)}) fusion(f32[259,4352]{0,1:T(8,128)} %copy-done, f32[256]{0:T(256)} %get-tuple-element.718, f32[256]{0:T(256)} %get-tuple-element.719, f32[256]{0:T(256)} %get-tuple-element.720, ...), kind=kLoop, calls=%fused_computation.90 | loop fusion | flops 26716928 | bytes 31286272 | tf_op jit(solution)/shard_map/transpose(jvp())/reduce_sum | solution.py:58
  711.6 19.5 %multiply_reduce_fusion.7 = (f32[4352]{0:T(1024)}, f32[4352]{0:T(1024)}, f32[4352]{0:T(1024)S(1)}, f32[4352]{0:T(1024)S(1)}, f32[4352]{0:T(1024)}, /*index=5*/f32[256,4352]{0,1:T(8,128)}) fusion(f32[259,4352]{0,1:T(8,128)} %copy-done.1, f32[256]{0:T(256)} %copy-done.130, f32[256]{0:T(256)} %copy-done.132, f32[256]{0:T(256)} %copy-done.134, ...), kind=kLoop, calls=%fused_computation.86 | loop fusion | flops 26716928 | bytes 31286272 | tf_op jit(solution)/shard_map/transpose(jvp())/reduce_sum | solution.py:58
  774.6 15.2 pad_maximum_fusion.2
  824.2 15.1 pad_maximum_fusion.3
  852.2 45.6 %all-to-all-done.3 = bf16[256,4,1024]{2,0,1:T(8,128)(2,1)} async-done(((bf16[256,4,1024]{2,0,1:T(8,128)(2,1)}), bf16[256,4,1024]{2,0,1:T(8,128)(2,1)}, u32[]{:S(2)}, u32[]{:S(2)}) %all-to-all-start.3) | async-done | bytes 2097184 | tf_op jit(solution)/shard_map/all_to_all | solution.py:246
  928.2 19.0 all-to-all-done.2
  950.8 14.7 fusion.90
  972.7 16.6 fusion.249
  998.4 76.7 %all-gather.27.cloned.1.call-done = bf16[1024,8512]{0,1:T(8,128)(2,1)} async-done(((bf16[256,8512]{0,1:T(8,128)(2,1)}), bf16[1024,8512]{0,1:T(8,128)(2,1)}) %all-gather.27.cloned.1.call-update) | async-done | bytes 17432592 | tf_op jit(solution)/shard_map/all_gather | solution.py:250
  1075.1 21.3 %convolution_add_fusion = f32[512,8512]{0,1:T(8,128)} fusion(f32[512,8512]{0,1:T(8,128)} %fusion.249, bf16[1024,8512]{0,1:T(8,128)(2,1)} %all-gather.27.cloned.1.call-done, bf16[1024,512]{1,0:T(8,128)(2,1)} %bitcast.79), kind=kOutput, calls=%fused_computation.30 | convolution fusion | flops 8929837056 | bytes 53346304 | tf_op jit(solution)/shard_map/dot_general | solution.py:248
  1120.8 19.0 fusion.229
  1139.9 19.3 %fusion.118 = (f32[2048]{0:T(1024)S(1)}, f32[256]{0:T(256)S(1)}, f32[256]{0:T(256)S(1)}, f32[2048]{0:T(1024)S(1)}, f32[256,2048]{1,0:T(8,128)}) fusion(f32[256]{0:T(256)S(1)} %copy-done.159, bf16[2,1,256,2048]{3,2,1,0:T(8,128)(2,1)S(1)} %copy-done.22, f32[2048]{0:T(1024)S(1)} %bitcast.512, f32[256,2048]{1,0:T(8,128)} %fusion.229, f32[256]{0:T(256)S(1)} %copy-done.157, ...), kind=kOutput, calls=%fused_computation.201 | convolution fusion | flops 8945889280 | bytes 45543424 | tf_op jit(solution)/shard_map/dot_general | solution.py:243
  1177.7 40.6 %all-reduce.30 = (f32[512]{0:T(512)}, f32[4,1088]{1,0:T(4,128)}, f32[1088]{0:T(1024)}, f32[16]{0:T(128)}, f32[16]{0:T(128)}, /*index=5*/f32[16]{0:T(128)}, f32[1024]{0:T(1024)}) all-reduce(f32[512]{0:T(512)S(1)} %dynamic-slice.21, f32[4,1088]{1,0:T(4,128)S(1)} %copy.177, ...), channel_id=1, replica_groups=mesh['group'=8,'fsdp'=4] {'group'}, use_global_device_ids=true, to_apply=%region_47.49 | all-reduce | flops 7024 | bytes 56192 | tf_op jit(solution)/shard_map/psum | solution.py:272
  1218.3 664.8 %all-reduce.36.cloned.1.call-done = (f32[512,8512]{0,1:T(8,128)}, f32[1024,2048]{1,0:T(8,128)}) async-done(((f32[512,8512]{0,1:T(8,128)}, f32[1024,2048]{1,0:T(8,128)}), (f32[512,8512]{0,1:T(8,128)}, f32[1024,2048]{1,0:T(8,128)})) %all-reduce.36.cloned.1.call-update) | async-done | bytes 25821200 | tf_op jit(solution)/shard_map/psum | solution.py:272
  (659 shorter events, 551.1 us)
Async XLA Ops:
  7.2 216.6 %all-gather.21.cloned.1.call-start = ((), (), s32[]{:S(2)}) async-start(), calls=%async_computation.5 | async-start | bytes 43581440 | tf_op jit(solution)/shard_map/all_gather | solution.py:142
  8.0 325.9 %all-gather.23.cloned.1.call-start = ((), (), s32[]{:S(2)}) async-start(), calls=%async_computation.6 | async-start | bytes 20971520 | tf_op jit(solution)/shard_map/all_gather | solution.py:149
  8.8 383.2 %all-gather.29.cloned.1.call-start = ((), (), s32[]{:S(2)}) async-start(), calls=%async_computation.9 | async-start | bytes 10485760 | tf_op jit(solution)/shard_map/all_gather | solution.py:28
  25.0 251.2 %copy-start.148 = (f32[64]{0:T(128)}, f32[64]{0:T(128)S(1)}, u32[]{:S(2)}) copy-start(f32[64]{0:T(128)S(1)} %convert_element_type.240) | copy-start | bytes 772
  38.4 243.9 %copy-start.59 = (f32[4352]{0:T(1024)}, f32[4352]{0:T(1024)S(1)}, u32[]{:S(2)}) copy-start(f32[4352]{0:T(1024)S(1)} %get-tuple-element.569) | copy-start | bytes 52228
  38.4 243.9 %copy-start.62 = (f32[4352]{0:T(1024)}, f32[4352]{0:T(1024)S(1)}, u32[]{:S(2)}) copy-start(f32[4352]{0:T(1024)S(1)} %get-tuple-element.570) | copy-start | bytes 52228
  38.4 243.9 %copy-start.65 = (f32[4352]{0:T(1024)}, f32[4352]{0:T(1024)S(1)}, u32[]{:S(2)}) copy-start(f32[4352]{0:T(1024)S(1)} %get-tuple-element.571) | copy-start | bytes 52228
  272.0 7.6 collective-permute-start
  298.3 154.0 %all-gather.31.cloned.1.call-start = ((), (), s32[]{:S(2)}) async-start(), calls=%async_computation.10 | async-start | bytes 10485760 | tf_op jit(solution)/shard_map/all_gather | solution.py:28
  302.6 7.1 collective-permute-start.1
  328.2 254.7 %all-gather.33.cloned.1.call-start = ((), (), s32[]{:S(2)}) async-start(), calls=%async_computation.11 | async-start | bytes 10485760 | tf_op jit(solution)/shard_map/all_gather | solution.py:28
  504.0 118.2 %all-gather.35.cloned.1.call-start = ((), (), s32[]{:S(2)}) async-start(), calls=%async_computation.12 | async-start | bytes 10485760 | tf_op jit(solution)/shard_map/all_gather | solution.py:28
  509.8 407.6 %all-gather.39.cloned.1.call-start = ((), (), s32[]{:S(2)}) async-start(), calls=%async_computation.14 | async-start | bytes 5242880 | tf_op jit(solution)/shard_map/all_gather | solution.py:255
  513.3 437.5 %all-gather.37.cloned.1.call-start = ((), (), s32[]{:S(2)}) async-start(), calls=%async_computation.13 | async-start | bytes 5242880 | tf_op jit(solution)/shard_map/all_gather | solution.py:255
  514.0 458.6 %all-gather.25.cloned.1.call-start = ((), (), s32[]{:S(2)}) async-start(), calls=%async_computation.7 | async-start | bytes 21790720 | tf_op jit(solution)/shard_map/all_gather | solution.py:250
  754.3 6.9 collective-permute-start.2
  789.8 285.4 %all-gather.27.cloned.1.call-start = ((), (), s32[]{:S(2)}) async-start(), calls=%async_computation.8 | async-start | bytes 21790720 | tf_op jit(solution)/shard_map/all_gather | solution.py:250
  802.9 6.7 collective-permute-start.3
  843.3 54.5 %all-to-all-start.3 = ((bf16[256,4,1024]{2,0,1:T(8,128)(2,1)}), bf16[256,4,1024]{2,0,1:T(8,128)(2,1)}, u32[]{:S(2)}, u32[]{:S(2)}) async-start(bf16[256,4,1024]{2,0,1:T(8,128)(2,1)} %copy.155), calls=%async_computation.3 | async-start | bytes 4194304 | tf_op jit(solution)/shard_map/all_to_all | solution.py:246
  897.8 49.4 %all-to-all-start.2 = ((bf16[256,4,1024]{2,0,1:T(8,128)(2,1)}), bf16[256,4,1024]{2,0,1:T(8,128)(2,1)}, u32[]{:S(2)}, u32[]{:S(2)}) async-start(bf16[256,4,1024]{2,0,1:T(8,128)(2,1)} %copy.154), calls=%async_computation.2 | async-start | bytes 4194304 | tf_op jit(solution)/shard_map/all_to_all | solution.py:246
  947.2 20.9 %all-to-all-start = ((bf16[256,4,512]{2,0,1:T(8,128)(2,1)}), bf16[256,4,512]{2,0,1:T(8,128)(2,1)S(1)}, u32[]{:S(2)}, u32[]{:S(2)}) async-start(bf16[256,4,512]{2,0,1:T(8,128)(2,1)} %get-tuple-element.709), calls=%async_computation | async-start | bytes 2097152 | tf_op jit(solution)/shard_map/all_to_all | solution.py:245
  950.7 225.7 %reduce-scatter.4.cloned.1.call-start = ((), (), s32[]{:S(2)}) async-start(), calls=%async_computation.15 | async-start | bytes 2785280
  968.1 30.4 %all-to-all-start.1 = ((bf16[256,4,512]{2,0,1:T(8,128)(2,1)}), bf16[256,4,512]{2,0,1:T(8,128)(2,1)}, u32[]{:S(2)}, u32[]{:S(2)}) async-start(bf16[256,4,512]{2,0,1:T(8,128)(2,1)} %get-tuple-element.708), calls=%async_computation.1 | async-start | bytes 2097152 | tf_op jit(solution)/shard_map/all_to_all | solution.py:245
  972.4 910.7 %all-reduce.36.cloned.1.call-start = ((), (), s32[]{:S(2)}) async-start(), calls=%async_computation.16 | async-start | bytes 51642368 | tf_op jit(solution)/shard_map/psum | solution.py:272
  (191 other events, 4927.7 us)
Sparse Core Ops, SparseCore 0:
  9.6 214.1 all-gather.20
  225.3 105.9 all-gather.22
  332.9 59.0 all-gather.28
  393.9 58.2 all-gather.30
  504.1 58.2 all-gather.32
  563.8 58.2 all-gather.34
  623.7 34.4 all-gather.38
  659.8 34.4 all-gather.36
  789.9 158.2 all-gather.24
  949.6 125.5 all-gather.26
  1077.7 32.2 reduce-scatter.3
  1116.1 767.0 all-reduce.35
where the time goes:
time: 1920 us; the launch traced here: 1910 us
  waiting for transfers between devices  1060 us (55%)
  matrix products  347 us (18%)
  other arithmetic  234 us (12%)
  local copies, waits for them, and re-layouts  130 us (7%)
  blocking collectives  91.8 us (5%)
  starting transfers between devices  26.2 us (1%)
  between operations  22.3 us (1%)
    psum x1, waiting for transfers between devices, on_device(): lax.psum((lax.psum_scatter(totals[0], 'fsdp', scatter_dimension=0, tiled=...  665 us
    all_gather x1, waiting for transfers between devices, on_device(): lax.all_gather(shards[1], 'fsdp', axis=0, tiled=True)  183 us
    dot_general x6, matrix products, tail_part(): inside = jnp.einsum('hts,shp->thp', mixing, x_heads, precision=HIGHEST)  103 us
    all_gather x2, waiting for transfers between devices, on_device(): lax.all_gather(grad_proj, 'fsdp', axis=0, tiled=True)  76.7 us
    all_to_all x2, waiting for transfers between devices, on_device(): lax.all_to_all(gated_low, 'fsdp', split_axis=1, concat_axis=0, tiled=True)  64.7 us
    all_gather x4, waiting for transfers between devices, prefix(): pieces = jax.tree.map(lambda part: lax.all_gather(part, axis), value)  55.1 us
    unnamed x411, local copies, waits for them, and re-layouts  50.7 us
    dot_general x2, matrix products, on_device(): jnp.dot(normed_low, weight_in, preferred_element_type=jnp.float32)  43.6 us
  transfers between devices with their start and end apart: 20, of which 9 were waited for; matrix products, arithmetic and copies ran while one was open for 32% of the time, Pallas kernels for 0%

commit v1 on v0

v1 whole, which is shorter than its diff:
```python
from functools import partial

import jax
import jax.numpy as jnp
from jax import lax
from jax.experimental import pallas as pl
from jax.experimental.pallas import tpu as pltpu
from jax.sharding import PartitionSpec as P

INNER = 4096
HEADS = 64
HEADDIM = 64
STATE = 128
CONV = 4
XBC = 4352
LANES = 128
EPSILON = 1e-05
FAR = -1e30
HIGHEST = lax.Precision.HIGHEST
VMEM = 48 * 1024 * 1024
F32 = jnp.float32
BF16 = jnp.bfloat16


def swap(value, axis, bit):
    count = lax.axis_size(axis)
    return lax.ppermute(value, axis, [(i, i ^ bit) for i in range(count)])


def bits_of(count):
    return [1 << k for k in reversed(range(count.bit_length() - 1))]


def gathered(piece):
    held = {0: piece}
    for bit in bits_of(lax.axis_size("fsdp")):
        for r, part in list(held.items()):
            held[r ^ bit] = swap(part, "fsdp", bit)
    return [held[r] for r in range(len(held))]


def swap_shared(value, bit):
    if bit == 1:
        return swap(value, "fsdp", bit)
    half = value.shape[1] // 2
    side = lax.axis_index("group") & 1
    mine = swap(lax.dynamic_slice_in_dim(value, side * half, half, 1), "fsdp", bit)
    other = swap(mine, "group", 1)
    return jnp.concatenate(
        [jnp.where(side == 0, mine, other), jnp.where(side == 0, other, mine)], axis=1
    )


def traded_shared(blocks):
    held = {r: {0: block} for r, block in enumerate(blocks)}
    for bit in bits_of(len(blocks)):
        going = [r for r in sorted(held) if r & bit]
        sources = sorted(held[going[0]])
        stacked = jnp.stack([held[r][s] for r in going for s in sources])
        got = swap_shared(stacked, bit)
        place = 0
        for r in going:
            for s in sources:
                held[r ^ bit][s ^ bit] = got[place]
                place += 1
            del held[r]
    return [held[0][s] for s in sorted(held[0])]


def traded(blocks):
    held = {r: {0: block} for r, block in enumerate(blocks)}
    for bit in bits_of(len(blocks)):
        going = [r for r in sorted(held) if r & bit]
        sources = sorted(held[going[0]])
        got = swap(jnp.stack([held[r][s] for r in going for s in sources]), "fsdp", bit)
        place = 0
        for r in going:
            for s in sources:
                held[r ^ bit][s ^ bit] = got[place]
                place += 1
            del held[r]
    return [held[0][s] for s in sorted(held[0])]


def scattered(value):
    count = value.shape[0]
    bit = 1
    while bit < count:
        pairs = value.reshape((value.shape[0] // 2, 2) + value.shape[1:])
        got = swap(pairs[:, 1].astype(BF16), "fsdp", bit)
        value = pairs[:, 0].astype(F32) + got.astype(F32)
        bit *= 2
    return value[0]


def absolute(blocks):
    own = lax.axis_index("fsdp")
    stacked = jnp.stack(blocks)
    return [
        lax.dynamic_index_in_dim(stacked, own ^ i, 0, keepdims=False) for i in range(len(blocks))
    ]


def summed(value, axis):
    for bit in bits_of(lax.axis_size(axis)):
        value = value + swap(value, axis, bit)
    return value


def lines():
    count = lax.axis_size("group")
    return [list(range(side, count, 2)) for side in (0, 1)]


def group_scatter(value):
    side = lax.axis_index("group") & 1
    away = lax.dynamic_index_in_dim(value, 1 - side, 0, keepdims=False).astype(BF16)
    keep = lax.dynamic_index_in_dim(value, side, 0, keepdims=False)
    half = (keep.astype(F32) + swap(away, "group", 1).astype(F32)).astype(BF16)
    return lax.psum_scatter(
        half, "group", scatter_dimension=0, tiled=False, axis_index_groups=lines()
    )


def group_gather(part):
    side = lax.axis_index("group") & 1
    half = lax.all_gather(part, "group", axis=0, tiled=False, axis_index_groups=lines())
    other = swap(half, "group", 1)
    return jnp.stack([jnp.where(side == 0, half, other), jnp.where(side == 0, other, half)])


def dot(a, b, contract=((1,), (0,)), precision=None):
    return lax.dot_general(a, b, (contract, ((), ())), precision=precision, preferred_element_type=F32)


def steps(dt_ref, head_ref, tri):
    raw = dt_ref[...] + head_ref[0:1, :]
    size = jnp.maximum(raw, 0.0) + jnp.log1p(jnp.exp(-jnp.abs(raw)))
    log_decay = size * head_ref[1:2, :]
    running = dot(tri, log_decay, precision=HIGHEST)
    return raw, size, log_decay, running


def forward_kernel(
    chunk,
    own_ref,
    pre_ref,
    gate_ref,
    dt_ref,
    back_ref,
    col_ref,
    row_ref,
    taps_ref,
    head_ref,
    skip_ref,
    gain_ref,
    act_ref,
    slope_ref,
    out_ref,
    gained_ref,
    enter_ref,
    stat_ref,
    state,
    window,
):
    where = pl.program_id(1)
    inner = gate_ref.shape[1]
    channels = pre_ref.shape[1]

    @pl.when(where == 0)
    def _():
        state[...] = jnp.zeros_like(state)
        window[0:8, :] = jnp.zeros((8, channels), F32)

    window[8:, :] = pre_ref[...].astype(F32)
    for at in range(0, channels, LANES):
        lanes = slice(at, at + LANES)
        total = taps_ref[4:5, lanes] + taps_ref[3:4, lanes] * window[8 : 8 + chunk, lanes]
        for back in range(1, CONV):
            total += taps_ref[3 - back : 4 - back, lanes] * (
                window[8 - back : 8 - back + chunk, lanes] * col_ref[:, back : back + 1]
            )
        sig = jax.nn.sigmoid(total)
        act_ref[:, lanes] = (total * sig).astype(BF16)
        slope_ref[:, lanes] = (sig * (1.0 + total * (1.0 - sig))).astype(BF16)
    window[0:8, :] = window[chunk : chunk + 8, :]

    start = (where * chunk).astype(F32)
    seg_col = col_ref[:, 0:1]
    seg_row = row_ref[...]
    seg_last = seg_row[:, chunk - 1 : chunk]
    down = lax.broadcasted_iota(jnp.int32, (chunk, chunk), 0)
    across = lax.broadcasted_iota(jnp.int32, (chunk, chunk), 1)
    tri = (across <= down).astype(F32)
    _, size, _, running = steps(dt_ref, head_ref, tri)
    running_t = running.T
    size_t = size.T
    b_input = act_ref[:, inner : inner + STATE]
    c_output = act_ref[:, inner + STATE :]
    gram = dot(c_output, b_input, ((1,), (1,)))
    veil = jnp.where((seg_col == seg_row) & (across <= down), 0.0, FAR)
    crossing = (seg_col < start).astype(F32)
    ending = (seg_col == seg_last).astype(F32)
    passing = (seg_last < start).astype(F32)
    last = running[chunk - 1 : chunk, :]
    low = lax.broadcasted_iota(jnp.int32, (chunk, LANES), 1) < HEADDIM
    low_row = low[0:1, :]
    squares = jnp.zeros((chunk, LANES), F32)
    products = jnp.zeros((chunk, LANES), F32)
    for pair in range(inner // LANES):
        lanes = slice(pair * LANES, (pair + 1) * LANES)
        heads = (2 * pair, 2 * pair + 1)
        x_low = act_ref[:, lanes]
        x_pair = x_low.astype(F32)
        masked = (jnp.where(low, x_pair, 0.0), jnp.where(low, 0.0, x_pair))
        run = [running[:, h : h + 1] for h in heads]
        inside = jnp.zeros((chunk, LANES), F32)
        for k, h in enumerate(heads):
            mixing = jnp.exp(run[k] - running_t[h : h + 1, :] + veil) * gram * size_t[h : h + 1, :]
            inside += dot(mixing.astype(BF16), masked[k].astype(BF16))
        run_pair = jnp.where(low, run[0], run[1])
        size_pair = jnp.where(low, size[:, heads[0] : heads[0] + 1], size[:, heads[1] : heads[1] + 1])
        last_pair = jnp.where(
            low_row, last[:, heads[0] : heads[0] + 1], last[:, heads[1] : heads[1] + 1]
        )
        entering = state[:, lanes]
        entering_low = entering.astype(BF16)
        enter_ref[:, lanes] = entering_low
        ssm = (
            inside
            + dot(c_output, entering_low) * (jnp.exp(run_pair) * crossing)
            + skip_ref[:, lanes] * x_pair
        )
        outflow = jnp.exp(last_pair - run_pair) * ending * size_pair
        fresh = dot(b_input, (x_pair * outflow).astype(BF16), ((0,), (0,)))
        state[:, lanes] = (jnp.exp(last_pair) * passing) * entering + fresh
        gate = gate_ref[:, lanes]
        gated = ssm * (gate * jax.nn.sigmoid(gate))
        gained = gated * gain_ref[:, lanes]
        out_ref[:, lanes] = ssm
        gained_ref[:, lanes] = gained.astype(BF16)
        squares += gated * gated
        products += gained * back_ref[:, lanes].astype(F32)
    stat_ref[0:1, :] = jnp.sum(squares.T, axis=0, keepdims=True)
    stat_ref[1:2, :] = jnp.sum(products.T, axis=0, keepdims=True)
    stat_ref[2:8, :] = jnp.zeros((6, chunk), F32)


def gate_kernel(
    chunk,
    own_ref,
    out_ref,
    gate_ref,
    back_ref,
    stat_ref,
    gain_ref,
    grad_ssm_ref,
    grad_gate_ref,
    gated_ref,
    grad_gain_ref,
):
    inner = gate_ref.shape[1]

    @pl.when((pl.program_id(0) == 0) & (pl.program_id(1) == 0))
    def _():
        grad_gain_ref[...] = jnp.zeros_like(grad_gain_ref)

    scale = lax.rsqrt(stat_ref[0:1, :] * (1.0 / INNER) + EPSILON)
    shift = scale * scale * scale * stat_ref[1:2, :] * (1.0 / INNER)
    scale = jnp.broadcast_to(scale, (LANES, chunk)).T
    shift = jnp.broadcast_to(shift, (LANES, chunk)).T
    for at in range(0, inner, LANES):
        lanes = slice(at, at + LANES)
        ssm = out_ref[:, lanes]
        gate = gate_ref[:, lanes]
        back = back_ref[:, lanes].astype(F32)
        sig = jax.nn.sigmoid(gate)
        silu = gate * sig
        gated = ssm * silu
        scaled = gated * scale
        gain = gain_ref[:, lanes]
        grad_gated = scale * (gain * back) - gated * shift
        grad_ssm_ref[:, lanes] = (grad_gated * silu).astype(BF16)
        grad_gate_ref[:, lanes] = (
            grad_gated * ssm * (sig * (1.0 + gate * (1.0 - sig)))
        ).astype(BF16)
        gated_ref[:, lanes] = (scaled * gain).astype(BF16)
        grad_gain_ref[0:1, lanes] += jnp.sum(scaled * back, axis=0, keepdims=True)


def backward_kernel(
    chunk,
    own_ref,
    act_ref,
    slope_ref,
    pre_ref,
    dt_ref,
    grad_ref,
    enter_ref,
    col_ref,
    row_ref,
    taps_ref,
    head_ref,
    skip_ref,
    grad_pre_ref,
    grad_dt_ref,
    grad_taps_ref,
    grad_skip_ref,
    grad_head_ref,
    leaving,
    window,
    grad_act,
    row_sums,
):
    count = pl.num_programs(1)
    where = count - 1 - pl.program_id(1)
    inner = grad_ref.shape[1]
    channels = pre_ref.shape[1]

    @pl.when(pl.program_id(1) == 0)
    def _():
        leaving[...] = jnp.zeros_like(leaving)
        window[chunk:, :] = jnp.zeros((8, channels), F32)

    @pl.when((pl.program_id(0) == 0) & (pl.program_id(1) == 0))
    def _():
        grad_taps_ref[...] = jnp.zeros_like(grad_taps_ref)
        grad_skip_ref[...] = jnp.zeros_like(grad_skip_ref)
        grad_head_ref[...] = jnp.zeros_like(grad_head_ref)
        row_sums[...] = jnp.zeros_like(row_sums)

    start = (where * chunk).astype(F32)
    seg_col = col_ref[:, 0:1]
    seg_row = row_ref[...]
    seg_last = seg_row[:, chunk - 1 : chunk]
    down = lax.broadcasted_iota(jnp.int32, (chunk, chunk), 0)
    across = lax.broadcasted_iota(jnp.int32, (chunk, chunk), 1)
    tri = (across <= down).astype(F32)
    raw, size, log_decay, running = steps(dt_ref, head_ref, tri)
    running_t = running.T
    b_input = act_ref[:, inner : inner + STATE]
    c_output = act_ref[:, inner + STATE :]
    gram = dot(b_input, c_output, ((1,), (1,)))
    veil = jnp.where((seg_col == seg_row) & (down <= across), 0.0, FAR)
    crossing = (seg_col < start).astype(F32)
    ending = (seg_col == seg_last).astype(F32)
    passing = (seg_last < start).astype(F32)
    last = running[chunk - 1 : chunk, :]
    lane = lax.broadcasted_iota(jnp.int32, (chunk, LANES), 1)
    low = lane < HEADDIM
    low_row = low[0:1, :]
    lane_row = lane[0:1, :]
    grad_gram = jnp.zeros((chunk, chunk), F32)
    grad_b = jnp.zeros((chunk, STATE), F32)
    grad_c = jnp.zeros((chunk, STATE), F32)
    size_grad = jnp.zeros((chunk, LANES), F32)
    carry_grad = jnp.zeros((chunk, LANES), F32)
    total_grad = jnp.zeros((1, LANES), F32)
    for pair in range(inner // LANES):
        lanes = slice(pair * LANES, (pair + 1) * LANES)
        heads = (2 * pair, 2 * pair + 1)
        x_pair = act_ref[:, lanes].astype(F32)
        grad_low = grad_ref[:, lanes]
        grad = grad_low.astype(F32)
        halves = (low, jnp.logical_not(low))
        run = [running[:, h : h + 1] for h in heads]
        sizes = [size[:, h : h + 1] for h in heads]
        run_pair = jnp.where(low, run[0], run[1])
        size_pair = jnp.where(low, sizes[0], sizes[1])
        last_pair = jnp.where(
            low_row, last[:, heads[0] : heads[0] + 1], last[:, heads[1] : heads[1] + 1]
        )
        entering = enter_ref[:, lanes]
        left = leaving[:, lanes]
        left_low = left.astype(BF16)
        inflow = jnp.exp(run_pair) * crossing
        outflow = jnp.exp(last_pair - run_pair) * ending
        into = grad * inflow
        into_low = into.astype(BF16)
        carried = into * dot(c_output, entering)
        fresh_back = dot(b_input, left_low) * outflow
        flown = x_pair * fresh_back
        whole = jnp.exp(last_pair) * passing
        kept = whole * jnp.sum(left * entering.astype(F32), axis=0, keepdims=True)
        kept += jnp.sum(flown * size_pair, axis=0, keepdims=True)
        leaving[:, lanes] = whole * left + dot(c_output, into_low, ((0,), (0,)))
        grad_c += dot(into_low, entering, ((1,), (1,)))
        grad_b += dot((x_pair * outflow * size_pair).astype(BF16), left_low, ((1,), (1,)))
        grad_x = fresh_back * size_pair + skip_ref[:, lanes] * grad
        for k, h in enumerate(heads):
            mine = halves[k]
            decay = jnp.exp(running_t[h : h + 1, :] - run[k] + veil)
            weight = decay * gram
            back = dot(jnp.where(mine, x_pair, 0.0).astype(BF16), grad_low, ((1,), (1,)))
            grad_x += dot(
                (weight * sizes[k]).astype(BF16), jnp.where(mine, grad, 0.0).astype(BF16)
            )
            grad_gram += back * decay * sizes[k]
            straight = back * weight
            row_sums[h : h + 1, :] = jnp.sum(straight * sizes[k], axis=0, keepdims=True)
            size_here = jnp.sum(straight, axis=1, keepdims=True) + jnp.sum(
                jnp.where(mine, flown, 0.0), axis=1, keepdims=True
            )
            carry_here = jnp.sum(jnp.where(mine, carried, 0.0), axis=1, keepdims=True)
            here = lane == h
            size_grad = jnp.where(here, size_here, size_grad)
            carry_grad = jnp.where(here, carry_here, carry_grad)
            total_here = jnp.sum(jnp.where(mine[0:1, :], kept, 0.0), axis=1, keepdims=True)
            total_grad = jnp.where(lane_row == h, total_here, total_grad)
        grad_skip_ref[0:1, lanes] += jnp.sum(grad * x_pair, axis=0, keepdims=True)
        grad_act[:, lanes] = grad_x
    grad_gram_low = grad_gram.astype(BF16)
    grad_act[:, inner : inner + STATE] = grad_b + dot(grad_gram_low, c_output)
    grad_act[:, inner + STATE :] = grad_c + dot(grad_gram_low, b_input, ((0,), (0,)))
    row_t = row_sums[...].T
    grad_run = row_t + carry_grad - size * size_grad
    upper = (across >= down).astype(F32)
    grad_decay = dot(upper, grad_run, precision=HIGHEST) + total_grad
    grad_size = grad_decay * head_ref[1:2, :] + size_grad
    grad_raw = jnp.where(lane < inner // HEADDIM, grad_size * jax.nn.sigmoid(raw), 0.0)
    grad_dt_ref[...] = grad_raw.astype(BF16)
    grad_head_ref[0:1, :] += jnp.sum(grad_raw, axis=0, keepdims=True)
    grad_head_ref[1:2, :] += jnp.sum(grad_decay * log_decay, axis=0, keepdims=True)

    for at in range(0, channels, LANES):
        lanes = slice(at, at + LANES)
        grad_sum = grad_act[:, lanes] * slope_ref[:, lanes].astype(F32)
        window[0:chunk, lanes] = grad_sum
        pre = pre_ref[:, lanes].astype(F32)
        grad_pre = taps_ref[3:4, lanes] * grad_sum
        grad_taps_ref[3:4, lanes] += jnp.sum(pre * grad_sum, axis=0, keepdims=True)
        grad_taps_ref[4:5, lanes] += jnp.sum(grad_sum, axis=0, keepdims=True)
        for ahead in range(1, CONV):
            later = window[ahead : ahead + chunk, lanes] * col_ref[:, 3 + ahead : 4 + ahead]
            grad_pre += taps_ref[3 - ahead : 4 - ahead, lanes] * later
            grad_taps_ref[3 - ahead : 4 - ahead, lanes] += jnp.sum(
                pre * later, axis=0, keepdims=True
            )
        grad_pre_ref[:, lanes] = grad_pre.astype(BF16)
    window[chunk:, :] = window[0:8, :]


def scan_calls(micro, parts, tok_count, inner):
    chunk = min(LANES, tok_count)
    per_part = tok_count // chunk
    count = parts * per_part
    channels = inner + 2 * STATE
    tokens = micro * parts * tok_count

    def blocks(flip):
        def time(step):
            return count - 1 - step if flip else step

        def place(m, step, own):
            t = time(step)
            part = lax.bitwise_xor(t // per_part, own[0])
            return ((part * micro + m) * per_part + t % per_part, 0)

        def tok(width):
            return pl.BlockSpec((chunk, width), place)

        col = pl.BlockSpec((None, chunk, 8), lambda m, step, own: (m, time(step), 0))
        row = pl.BlockSpec((None, None, 1, chunk), lambda m, step, own: (m, time(step), 0, 0))
        stat = pl.BlockSpec((None, None, 8, chunk), lambda m, step, own: (m, time(step), 0, 0))
        states = pl.BlockSpec((None, None, STATE, inner), lambda m, step, own: (m, time(step), 0, 0))

        def const(rows, width):
            return pl.BlockSpec((rows, width), lambda m, step, own: (0, 0))

        return tok, col, row, stat, states, const

    def call(kernel, flip, ins, outs, shapes, scratch, flops, moved):
        return pl.pallas_call(
            partial(kernel, chunk),
            grid_spec=pltpu.PrefetchScalarGridSpec(
                num_scalar_prefetch=1,
                grid=(micro, count),
                in_specs=ins,
                out_specs=outs,
                scratch_shapes=scratch,
            ),
            out_shape=shapes,
            compiler_params=pltpu.CompilerParams(
                dimension_semantics=("arbitrary", "arbitrary"), vmem_limit_bytes=VMEM
            ),
            cost_estimate=pl.CostEstimate(flops=flops, bytes_accessed=moved, transcendentals=0),
        )

    struct = jax.ShapeDtypeStruct
    tok, col, row, stat, states, const = blocks(False)
    forward = call(
        forward_kernel,
        False,
        [tok(channels), tok(inner), tok(LANES), tok(inner), col, row]
        + [const(8, channels), const(8, LANES), const(1, inner), const(1, inner)],
        [tok(channels), tok(channels), tok(inner), tok(inner), states, stat],
        [
            struct((tokens, channels), BF16),
            struct((tokens, channels), BF16),
            struct((tokens, inner), F32),
            struct((tokens, inner), BF16),
            struct((micro, count, STATE, inner), BF16),
            struct((micro, count, 8, chunk), F32),
        ],
        [pltpu.VMEM((STATE, inner), F32), pltpu.VMEM((chunk + 8, channels), F32)],
        tokens * inner * 8 * chunk,
        tokens * inner * 60,
    )
    gating = call(
        gate_kernel,
        False,
        [tok(inner), tok(inner), tok(inner), stat, const(1, inner)],
        [tok(inner), tok(inner), tok(inner), const(8, inner)],
        [struct((tokens, inner), BF16)] * 3 + [struct((8, inner), F32)],
        [],
        tokens * inner * 30,
        tokens * inner * 16,
    )
    tok, col, row, stat, states, const = blocks(True)
    backward = call(
        backward_kernel,
        True,
        [tok(channels), tok(channels), tok(channels), tok(LANES), tok(inner), states, col, row]
        + [const(8, channels), const(8, LANES), const(1, inner)],
        [tok(channels), tok(LANES), const(8, channels), const(8, inner), const(8, LANES)],
        [
            struct((tokens, channels), BF16),
            struct((tokens, LANES), BF16),
            struct((8, channels), F32),
            struct((8, inner), F32),
            struct((8, LANES), F32),
        ],
        [
            pltpu.VMEM((STATE, inner), F32),
            pltpu.VMEM((chunk + 8, channels), F32),
            pltpu.VMEM((chunk, channels), F32),
            pltpu.VMEM((LANES, chunk), F32),
        ],
        tokens * inner * 20 * chunk,
        tokens * inner * 100,
    )
    return forward, gating, backward


def padded(row, width):
    return jnp.pad(row, ((0, 0), (0, width - row.shape[1])))


def on_device(
    tokens,
    segment_ids,
    cotangent,
    norm_gain,
    in_weight,
    conv_weight,
    conv_bias,
    dt_bias,
    a_log,
    skip_d,
    inner_gain,
    out_weight,
):
    micro, _, tok_count, width = tokens.shape
    parts = lax.axis_size("fsdp")
    groups = lax.axis_size("group")
    own = lax.axis_index("fsdp")
    inner = INNER // parts
    heads = HEADS // parts
    channels = inner + 2 * STATE
    rows = width // parts
    seq = tok_count * parts
    tok_all = micro * seq

    taps_here = jnp.concatenate([conv_weight, conv_bias[None]], axis=0).astype(F32)
    packed = jnp.concatenate(
        [
            norm_gain.astype(F32),
            taps_here.reshape(-1),
            segment_ids.astype(F32).reshape(-1),
        ]
    )
    packed = lax.all_gather(packed, "fsdp", axis=0, tiled=False)
    cut = norm_gain.shape[0]
    gain_norm = packed[:, :cut].reshape(-1)
    taps_size = taps_here.size
    taps = packed[:, cut : cut + taps_size].reshape(parts, CONV + 1, -1)
    taps = taps.transpose(1, 0, 2).reshape(CONV + 1, XBC)
    seg = packed[:, cut + taps_size :].reshape(parts, micro, tok_count)
    seg = seg.transpose(1, 0, 2).reshape(micro, seq)
    taps = jnp.concatenate(
        [lax.dynamic_slice_in_dim(taps, own * inner, inner, 1), taps[:, INNER:]], axis=1
    )
    taps = jnp.pad(taps, ((0, 8 - CONV - 1), (0, 0)))
    times = jnp.arange(seq, dtype=F32)[None]
    cols = [seg]
    for back in range(1, CONV):
        cols.append((seg <= times - back).astype(F32))
    for ahead in range(1, CONV):
        later = jnp.pad(seg[:, ahead:], ((0, 0), (0, ahead)), constant_values=-1.0)
        cols.append((later == seg).astype(F32))
    cols.append(jnp.zeros_like(seg))
    cols = jnp.stack(cols, axis=-1)
    chunk = min(LANES, tok_count)
    seg_row = seg.reshape(micro, -1, 1, chunk)
    head_row = jnp.concatenate(
        [dt_bias.astype(F32)[None], -jnp.exp(a_log.astype(F32))[None]], axis=0
    )
    head_row = jnp.pad(head_row, ((0, 6), (0, LANES - heads)))
    skip_row = jnp.repeat(skip_d.astype(F32), HEADDIM)[None]
    gain_row = inner_gain.astype(F32)[None]

    blocks = []
    for r in range(parts):
        at = (own ^ r) * inner
        blocks.append(
            jnp.concatenate(
                [
                    lax.dynamic_slice_in_dim(in_weight, at, inner, 1),
                    lax.dynamic_slice_in_dim(in_weight, INNER + at, inner, 1),
                ],
                axis=1,
            )
        )
    tail = lax.all_gather(in_weight[:, 2 * INNER :], "fsdp", axis=0, tiled=True)
    mine = jnp.concatenate(absolute(traded_shared(blocks)), axis=0)
    weight_gate = mine[:, :inner]
    weight_xbc = jnp.concatenate([mine[:, inner:], tail[:, : 2 * STATE]], axis=1)
    weight_dt = padded(lax.dynamic_slice_in_dim(tail, 2 * STATE + own * heads, heads, 1), LANES)

    tok_rows = tokens[:, 0].astype(F32)
    inverse = lax.rsqrt(jnp.mean(tok_rows * tok_rows, axis=-1, keepdims=True) + EPSILON)
    normed = (tok_rows * inverse * gain_norm).astype(BF16)
    cot_here = cotangent[:, 0]
    normed_all = jnp.stack(gathered(normed)).reshape(tok_all, width)
    cot_all = jnp.stack(gathered(cot_here)).reshape(tok_all, width)

    gate = jnp.dot(normed_all, weight_gate, preferred_element_type=F32)
    pre = jnp.dot(normed_all, weight_xbc, preferred_element_type=F32).astype(BF16)
    dt_raw = jnp.dot(normed_all, weight_dt, preferred_element_type=F32)
    back = dot(cot_all, out_weight, ((1,), (1,))).astype(BF16)

    forward, gating, backward = scan_calls(micro, parts, tok_count, inner)
    own_arg = own.astype(jnp.int32)[None]
    act, slope, ssm, gained, entering, stat = forward(
        own_arg, pre, gate, dt_raw, back, cols, seg_row, taps, head_row, skip_row, gain_row
    )
    stat = jnp.pad(lax.psum(stat[:, :, :2], "fsdp"), ((0, 0), (0, 0), (0, 6), (0, 0)))
    grad_ssm, grad_gate, gated, grad_inner = gating(own_arg, ssm, gate, back, stat, gain_row)

    mixed = jnp.dot(gained, out_weight, preferred_element_type=F32).astype(BF16)
    mixed = scattered(mixed.reshape(parts, micro, tok_count, width))
    own_stat = lax.dynamic_slice_in_dim(
        stat[:, :, 0].reshape(micro, seq), own * tok_count, tok_count, 1
    )
    own_scale = lax.rsqrt(own_stat * (1.0 / INNER) + EPSILON)[:, :, None]
    mixed = (tok_rows + mixed * own_scale).astype(BF16)

    grad_out = dot(gated, cot_all, ((0,), (0,))).astype(BF16)
    sides = (2, groups // 2)
    grad_out = group_gather(group_scatter(grad_out.reshape(sides + (inner // groups, width))))
    grad_out = grad_out.reshape(inner, width).astype(F32)

    def in_piece(value):
        wide = value.shape[1]
        value = value.reshape((parts,) + sides + (rows // groups, wide))
        return group_scatter(value.transpose(1, 2, 0, 3, 4))

    piece_gate = in_piece(dot(normed_all, grad_gate, ((0,), (0,))).astype(BF16))
    grad_pre, grad_dt, grad_taps, grad_skip, grad_head = backward(
        own_arg,
        act,
        slope,
        pre,
        dt_raw,
        grad_ssm,
        entering,
        cols,
        seg_row,
        taps,
        head_row,
        skip_row,
    )
    grad_rest = jnp.concatenate([grad_pre, grad_dt], axis=1)
    piece_rest = in_piece(dot(normed_all, grad_rest, ((0,), (0,))).astype(BF16))

    def finish(piece):
        part = piece.shape[1]
        here = [lax.dynamic_index_in_dim(piece, own ^ r, 0, keepdims=False) for r in range(parts)]
        return jnp.stack(absolute(traded(here)), axis=1)

    gate_cols = group_gather(finish(piece_gate)).reshape(rows, INNER)
    rest = finish(piece_rest)
    shared = jnp.sum(rest[:, :, inner:channels].astype(F32), axis=1).astype(BF16)
    step_cols = rest[:, :, channels : channels + heads].reshape(-1, HEADS)
    rest = jnp.concatenate([rest[:, :, :inner].reshape(-1, INNER), shared, step_cols], axis=1)
    rest_cols = group_gather(rest).reshape(rows, -1)
    grad_in = jnp.concatenate([gate_cols, rest_cols], axis=1).astype(F32)

    weight_rest = jnp.concatenate([weight_xbc, weight_dt], axis=1)
    grad_normed = dot(grad_gate, weight_gate, ((1,), (1,))) + dot(
        grad_rest, weight_rest, ((1,), (1,))
    )
    grad_normed = scattered(grad_normed.reshape(parts, micro, tok_count, width))
    hat = tok_rows * inverse
    through = grad_normed * gain_norm
    grad_tok = inverse * (through - hat * jnp.mean(hat * through, axis=-1, keepdims=True))
    grad_tok = (cot_here.astype(F32) + grad_tok).astype(BF16)
    grad_norm = jnp.sum(grad_normed * hat, axis=(0, 1))

    taps_all = jnp.zeros((CONV + 1, XBC), F32)
    taps_all = lax.dynamic_update_slice_in_dim(
        taps_all, grad_taps[: CONV + 1, :inner], own * inner, 1
    )
    taps_all = taps_all.at[:, INNER:].set(grad_taps[: CONV + 1, inner:])
    joint = summed(jnp.concatenate([taps_all.reshape(-1), grad_norm]), "fsdp")
    skip_sum = jnp.sum(grad_skip[0].reshape(heads, HEADDIM), axis=1)
    joint = summed(
        jnp.concatenate(
            [joint, grad_inner[0], grad_head[0, :heads], grad_head[1, :heads], skip_sum]
        ),
        "group",
    )
    at = (CONV + 1) * XBC
    share = XBC // parts
    taps_all = lax.dynamic_slice_in_dim(
        joint[:at].reshape(CONV + 1, XBC), own * share, share, 1
    )
    grad_norm = lax.dynamic_slice_in_dim(joint, at + own * rows, rows, 0)
    at += width
    grad_inner = joint[at : at + inner]
    at += inner
    grad_bias, grad_rate, grad_skip = (
        joint[at + k * heads : at + (k + 1) * heads] for k in range(3)
    )
    return (
        mixed[:, None],
        grad_tok[:, None],
        grad_norm,
        grad_in,
        taps_all[:CONV],
        taps_all[CONV],
        grad_bias,
        grad_rate,
        grad_skip,
        grad_inner,
        grad_out,
    )


def solution(mesh):
    rows = P(None, "group", "fsdp", None)
    shard = P("fsdp")
    in_specs = (rows, P(None, "group", "fsdp"), rows, shard, P("fsdp", None), P(None, "fsdp"))
    in_specs += (shard,) * 5 + (P("fsdp", None),)
    out_specs = (rows, rows, shard, P("fsdp", None), P(None, "fsdp")) + (shard,) * 5
    out_specs += (P("fsdp", None),)
    return jax.shard_map(
        on_device, mesh=mesh, in_specs=in_specs, out_specs=out_specs, check_vma=False
    )
```

time: 1920 us -> 940 us (0.49)
  waiting for transfers between devices: 1060 us -> 410 us
  matrix products: 347 us -> 129 us
  other arithmetic: 234 us -> 99.9 us
  Pallas kernels: 0 us -> 134 us
  blocking collectives: 91.8 us -> 11.6 us
  local copies, waits for them, and re-layouts: 130 us -> 109 us
    psum x1 -> x0, waiting for transfers between devices: 665 us -> none  [on_device(): lax.psum((lax.psum_scatter(totals[0], 'fsdp', scatter_dimension=0, tiled=...]
    all_gather x10 -> x4, waiting for transfers between devices: 315 us -> 42.7 us  [the longest x3 42.7 us: group_gather(): lax.all_gather(part, 'group', axis=0, tiled=False, axis_index_groups=line...]
    dot_general x36 -> x10, matrix products: 347 us -> 129 us  [the longest x6 87.5 us: dot(): lax.dot_general(a, b, (contract, ((), ())), precision=precision, preferre...]
    ppermute x4 -> x28, waiting for transfers between devices: 0.01 us -> 201 us  [swap(): return lax.ppermute(value, axis, [(i, i ^ bit) for i in range(count)])]
    unnamed x13 -> x9, waiting for transfers between devices: 2.22 us -> 166 us
    pallas_call x0 -> x3, Pallas kernels: none -> 134 us  [the longest x1 75.9 us: on_device(): backward(own_arg, act, slope, pre, dt_raw, grad_ssm, entering, cols, seg_...]
    all_to_all x4 -> x0, waiting for transfers between devices: 73.9 us -> none  [the longest x2 64.7 us: on_device(): lax.all_to_all(gated_low, 'fsdp', split_axis=1, concat_axis=0, tiled=True)]
    reduce_sum x15 -> x4, other arithmetic: 77.8 us -> 5.06 us  [the longest x1 4.43 us: on_device(): grad_norm = jnp.sum(grad_normed * hat, axis=(0, 1))]
  transfers between devices with their start and end apart: 20 -> 35, of which waited for: 9 -> 15; matrix products, arithmetic and copies ran while one was open for 32% -> 25% of each run, Pallas kernels for 0% -> 8%
where the time goes in v1:
time: 940 us; the launch traced here: 933 us
  waiting for transfers between devices  410 us (44%)
  Pallas kernels  134 us (14%)
  matrix products  129 us (14%)
  local copies, waits for them, and re-layouts  109 us (12%)
  other arithmetic  99.9 us (11%)
  starting transfers between devices  23.8 us (3%)
  between operations  17 us (2%)
  blocking collectives  11.6 us (1%)
    ppermute x28, waiting for transfers between devices, swap(): return lax.ppermute(value, axis, [(i, i ^ bit) for i in range(count)])  201 us
    unnamed x9, waiting for transfers between devices  166 us
    dot_general x6, matrix products, dot(): lax.dot_general(a, b, (contract, ((), ())), precision=precision, preferre...  87.5 us
    pallas_call x1, Pallas kernels, on_device(): backward(own_arg, act, slope, pre, dt_raw, grad_ssm, entering, cols, seg_...  75.9 us
    all_gather x3, waiting for transfers between devices, group_gather(): lax.all_gather(part, 'group', axis=0, tiled=False, axis_index_groups=line...  42.7 us
    unnamed x93, local copies, waits for them, and re-layouts  42 us
    pallas_call x1, Pallas kernels, on_device(): forward(own_arg, pre, gate, dt_raw, back, cols, seg_row, taps, head_row,...  40.1 us
    ppermute x28, starting transfers between devices, swap(): return lax.ppermute(value, axis, [(i, i ^ bit) for i in range(count)])  23.5 us
  transfers between devices with their start and end apart: 35, of which 15 were waited for; matrix products, arithmetic and copies ran while one was open for 25% of the time, Pallas kernels for 8%

profile of v1, /device:TPU:0, one launch (start us, length us, event | category | flops | bytes accessed | tf_op | source)
XLA Modules:
  0.0 933.2 jit_solution(10675929359590310969)
XLA Ops:
  29.1 17.1 %all-reduce.14.cloned.1.call-done = f32[25856]{0:T(1024)} async-done(((f32[25856]{0:T(1024)}), f32[25856]{0:T(1024)}) %all-reduce.14.cloned.1.call-update) | async-done | bytes 103440
  51.5 27.5 %collective-permute-done.3 = bf16[2,256,2048]{1,2,0:T(8,128)(2,1)} collective-permute-done((bf16[2,256,2048]{1,2,0:T(8,128)(2,1)}, bf16[2,256,2048]{1,2,0:T(8,128)(2,1)}, u32[]{:S(2)}, u32[]{:S(2)}) %collective-permute-start.3) | collective-permute-done | bytes 2097184 | tf_op jit(solution)/shard_map/ppermute | solution.py:27
  87.5 36.4 %collective-permute-done.7 = bf16[2,256,2048]{2,1,0:T(8,128)(2,1)} collective-permute-done((bf16[2,256,2048]{2,1,0:T(8,128)(2,1)}, bf16[2,256,2048]{2,1,0:T(8,128)(2,1)}, u32[]{:S(2)}, u32[]{:S(2)}) %collective-permute-start.7) | collective-permute-done | bytes 2097184 | tf_op jit(solution)/shard_map/ppermute | solution.py:27
  140.6 27.6 %collective-permute-done.1 = bf16[2,256,2048]{2,1,0:T(8,128)(2,1)} collective-permute-done((bf16[2,256,2048]{2,1,0:T(8,128)(2,1)}, bf16[2,256,2048]{2,1,0:T(8,128)(2,1)}, u32[]{:S(2)}, u32[]{:S(2)}) %collective-permute-start.1) | collective-permute-done | bytes 2097184 | tf_op jit(solution)/shard_map/ppermute | solution.py:27
  177.6 13.8 %convolution_convert_fusion.4.back_ref = bf16[2048,1024]{1,0:T(8,128)(2,1)} fusion(bf16[2048,2048]{1,0:T(8,128)(2,1)S(1)} %bitcast.292, bf16[1024,2048]{1,0:T(8,128)(2,1)} %param.25), kind=kOutput, calls=%fused_computation.81 | convolution fusion | flops 8592031744 | bytes 16777216 | tf_op jit(solution)/shard_map/dot_general | solution.py:133
  212.1 11.6 %fusion.45.gate_ref = f32[2048,1024]{1,0:T(8,128)} fusion(bf16[2048,2048]{1,0:T(8,128)(2,1)S(1)} %bitcast.286, bf16[2048,2048]{0,1:T(8,128)(2,1)S(1)} %pad_maximum_fusion.1), kind=kOutput, calls=%fused_computation.85 | convolution fusion | flops 8589934592 | bytes 20971520 | tf_op jit(solution)/shard_map/dot_general | solution.py:637
  226.0 15.0 %convolution_convert_fusion.2.pre_ref = bf16[2048,1280]{1,0:T(8,128)(2,1)} fusion(bf16[2048,2048]{1,0:T(8,128)(2,1)S(1)} %bitcast.287, bf16[2048,256]{0,1:T(8,128)(2,1)S(1)} %slice.223, bf16[2048,1024]{0,1:T(8,128)(2,1)} %slice.222), kind=kOutput, calls=%fused_computation.21 | convolution fusion | flops 10750525440 | bytes 18874368 | tf_op jit(solution)/shard_map/dot_general | solution.py:638
  241.0 40.1 %shard_map.203 = (bf16[2048,1280]{1,0:T(8,128)(2,1)}, bf16[2048,1280]{1,0:T(8,128)(2,1)}, f32[2048,1024]{1,0:T(8,128)}, bf16[2048,1024]{1,0:T(8,128)(2,1)}, bf16...) custom-call(s32[1]{0:T(128)} %bitcast.own_ref, bf16[2048,1280]{1,0:T(8,128)(2,1)} %convolution_convert_fusion.2.pre_ref, ...), custom_call_target="tpu_custom_call" | custom-call | flops 2147483648 | bytes 125829120 | tf_op jit(solution)/shard_map/pallas_call | solution.py:644
  281.0 11.6 %psum.7 = f32[2,8,2,128]{3,2,1,0:T(2,128)S(1)} all-reduce(f32[2,8,2,128]{3,2,1,0:T(2,128)S(1)} %slice.187), channel_id=1, replica_groups=mesh['group'=8,'fsdp'=4] {'fsdp'}, use_global_device_ids=true, to_apply=%region_1.2 | all-reduce | flops 4096 | bytes 32768 | tf_op jit(solution)/shard_map/psum | solution.py:647
  293.2 17.6 %shard_map.204 = (bf16[2048,1024]{1,0:T(8,128)(2,1)S(1)}, bf16[2048,1024]{1,0:T(8,128)(2,1)}, bf16[2048,1024]{1,0:T(8,128)(2,1)}, f32[8,1024]{1,0:T(8,128)S(1)}) custom-call(s32[1]{0:T(128)} %bitcast.own_ref, f32[2048,1024]{1,0:T(8,128)} %get-tuple-element.40.out_ref, f32[2048,1024]{1,0:T(8,128)} %fusion.45.gate_ref, ...), custom_call_target="tpu_custom_call" | custom-call | flops 62914560 | bytes 33554432 | tf_op jit(solution)/shard_map/pallas_call | solution.py:648
  310.8 14.2 %convolution_convert_fusion.3 = bf16[1024,2048]{1,0:T(8,128)(2,1)S(1)} fusion(bf16[2048,1024]{1,0:T(8,128)(2,1)} %get-tuple-element.52, bf16[2048,2048]{1,0:T(8,128)(2,1)} %bitcast.293), kind=kOutput, calls=%fused_computation.80 | convolution fusion | flops 8592031744 | bytes 16777216 | tf_op jit(solution)/shard_map/dot_general | solution.py:133
  341.9 75.9 %shard_map.205 = (bf16[2048,1280]{1,0:T(8,128)(2,1)}, bf16[2048,128]{1,0:T(8,128)(2,1)S(1)}, f32[8,1280]{1,0:T(8,128)S(1)}, f32[8,1024]{1,0:T(8,128)S(1)}, f32[8,128]{1,0:T(8,128)S(1)}) custom-call(s32[1]{0:T(128)} %bitcast.own_ref, bf16[2048,1280]{1,0:T(8,128)(2,1)} %get-tuple-element.42.act_ref, bf16[2048,1280]{1,0:T(8,128)(2,1)} %get-tuple-element.43.slope_ref, ...), custom_call_target="tpu_custom_call" | custom-call | flops 5368709120 | bytes 209715200 | tf_op jit(solution)/shard_map/pallas_call | solution.py:669
  423.9 15.5 %convolution_convert_fusion.1 = bf16[2048,1408]{1,0:T(8,128)(2,1)S(1)} fusion(bf16[2048,2048]{1,0:T(8,128)(2,1)S(1)} %bitcast.291, bf16[2048,1408]{1,0:T(8,128)(2,1)} %constant_dynamic-update-slice_fusion.1), kind=kOutput, calls=%fused_computation.20 | convolution fusion | flops 11814043648 | bytes 19922944 | tf_op jit(solution)/shard_map/dot_general | solution.py:133
  444.7 11.9 %fusion.43 = f32[2048,2048]{1,0:T(8,128)} fusion(bf16[2048,1024]{1,0:T(8,128)(2,1)S(1)} %copy-done.29, bf16[2048,2048]{0,1:T(8,128)(2,1)S(1)} %bitcast.277), kind=kOutput, calls=%fused_computation.83 | convolution fusion | flops 8589934592 | bytes 25165824 | tf_op jit(solution)/shard_map/dot_general | solution.py:133
  460.5 22.7 %convolution_add_fusion = f32[2048,2048]{1,0:T(8,128)} fusion(f32[2048,2048]{1,0:T(8,128)} %fusion.43, bf16[2048,1408]{1,0:T(8,128)(2,1)} %constant_dynamic-update-slice_fusion.1, bf16[2048,128]{0,1:T(8,128)(2,1)S(1)} %copy-done.18, bf16[2048,256]{0,1:T(8,128)(2,1)} %copy-done.17, bf16[2048,1024]{0,1:T(8,128)(2,1)} %slice.222), kind=kOutput, calls=%fused_computation.18 | convolution fusion | flops 11832655872 | bytes 45088768 | tf_op jit(solution)/shard_map/dot_general | solution.py:133
  506.6 12.2 %convolution_convert_fusion = bf16[2048,2048]{1,0:T(8,128)(2,1)S(1)} fusion(bf16[2048,1024]{1,0:T(8,128)(2,1)} %get-tuple-element.38, bf16[1024,2048]{1,0:T(8,128)(2,1)} %param.25), kind=kOutput, calls=%fused_computation.19 | convolution fusion | flops 8594128896 | bytes 16777216 | tf_op jit(solution)/shard_map/dot_general | solution.py:650
  524.7 10.2 %fusion.7 = f32[1,2,2,256,2048]{4,3,2,1,0:T(8,128)} fusion(bf16[2,2,256,2048]{3,2,1,0:T(8,128)(2,1)} %collective-permute-done.11, f32[2,2,2,256,2048]{4,3,2,1,0:T(8,128)} %bitcast.282), kind=kLoop, calls=%fused_computation.12 | loop fusion | flops 4194304 | bytes 20971520 | tf_op jit(solution)/shard_map/reshape | solution.py:89
  540.1 148.3 %all-reduce.16.cloned.1.call-done = (bf16[4,4,64,1408]{3,2,0,1:T(8,128)(2,1)}, bf16[4,4,64,1024]{3,2,0,1:T(8,128)(2,1)}) async-done(((bf16[4,4,64,1408]{3,2,0,1:T(8,128)(2,1)}, bf16[4,4,64,1024]{3,2,0,1:T(8,128)(2,1)}), (bf16[4,4,64,1408]{3,2,0,1:T(8,128)(2,1)}, bf16[4,4,64,1024]{3,2,0,1:T(8,128)(2,1)})) %all-reduce.16.cloned.1.call-update) | async-done | bytes 4980752
  736.2 30.3 %collective-permute-done.13 = f32[23808]{0:T(1024)S(1)} collective-permute-done((f32[23808]{0:T(1024)S(1)}, f32[23808]{0:T(1024)S(1)}, u32[]{:S(2)}, u32[]{:S(2)}) %collective-permute-start.13) | collective-permute-done | bytes 95264 | tf_op jit(solution)/shard_map/ppermute | solution.py:27
  769.4 12.9 %collective-permute-done.15 = f32[24880]{0:T(1024)S(1)} collective-permute-done((f32[24880]{0:T(1024)S(1)}, f32[24880]{0:T(1024)S(1)}, u32[]{:S(2)}, u32[]{:S(2)}) %collective-permute-start.15) | collective-permute-done | bytes 99552 | tf_op jit(solution)/shard_map/ppermute | solution.py:27
  800.9 34.0 %all-gather.14.cloned.1.call-done = bf16[256,4416]{1,0:T(8,128)(2,1)} async-done(((bf16[64,4416]{1,0:T(8,128)(2,1)}), bf16[256,4416]{1,0:T(8,128)(2,1)}) %all-gather.14.cloned.1.call-update) | async-done | bytes 2261008 | tf_op jit(solution)/shard_map/all_gather | solution.py:127
  856.8 37.2 %collective-permute-done.25 = bf16[4,64,4416]{2,1,0:T(8,128)(2,1)S(1)} collective-permute-done((bf16[4,64,4416]{2,1,0:T(8,128)(2,1)}, bf16[4,64,4416]{2,1,0:T(8,128)(2,1)S(1)}, u32[]{:S(2)}, u32[]{:S(2)}) %collective-permute-start.25) | collective-permute-done | bytes 2261024 | tf_op jit(solution)/shard_map/ppermute | solution.py:27
  897.1 11.0 %maximum_convert_fusion = f32[512,8512]{1,0:T(8,128)} fusion(bf16[512,4416]{1,0:T(8,128)(2,1)} %bitcast.278, bf16[512,4096]{1,0:T(8,128)(2,1)} %bitcast.279), kind=kLoop, calls=%fused_computation.5 | loop fusion | flops 17432576 | bytes 26148864 | tf_op jit(solution)/shard_map/convert_element_type | solution.py:697
  908.0 17.9 %copy.166 = f32[512,8512]{0,1:T(8,128)} copy(f32[512,8512]{1,0:T(8,128)} %maximum_convert_fusion) | data formatting | bytes 34865152
  (295 shorter events, 243.9 us)
Async XLA Ops:
  7.2 39.1 %all-reduce.14.cloned.1.call-start = ((), (), s32[]{:S(2)}) async-start(), calls=%async_computation.6 | async-start | bytes 212992
  13.3 124.3 %all-gather.8.cloned.1.call-start = ((), (), s32[]{:S(2)}) async-start(), calls=%async_computation.1 | async-start | bytes 1638400 | tf_op jit(solution)/shard_map/all_gather | solution.py:624
  20.8 58.2 %collective-permute-start.3 = (bf16[2,256,2048]{1,2,0:T(8,128)(2,1)}, bf16[2,256,2048]{1,2,0:T(8,128)(2,1)}, u32[]{:S(2)}, u32[]{:S(2)}) collective-permute-start(bf16[2,256,2048]{1,2,0:T(8,128)(2,1)} %fusion.48), channel_id=1, source_target_pairs={{0,2},{1,3},{2,0},{3,1},{4,6},{5,7},{6,4},{7,5},{8,10},{9,11},{10,... | collective-permute-start | bytes 6291464 | tf_op jit(solution)/shard_map/ppermute | solution.py:27
  23.7 100.2 %collective-permute-start.7 = (bf16[2,256,2048]{2,1,0:T(8,128)(2,1)}, bf16[2,256,2048]{2,1,0:T(8,128)(2,1)}, u32[]{:S(2)}, u32[]{:S(2)}) collective-permute-start(bf16[2,256,2048]{2,1,0:T(8,128)(2,1)} %bitcast.18), channel_id=1, source_target_pairs={{0,2},{1,3},{2,0},{3,1},{4,6},{5,7},{6,4},{7,5},{8,10},{9,11},{10,... | collective-permute-start | bytes 6291464 | tf_op jit(solution)/shard_map/ppermute | solution.py:27
  23.8 149.5 %collective-permute-start.6 = (bf16[2,256,2048]{2,1,0:T(8,128)(2,1)}, bf16[2,256,2048]{2,1,0:T(8,128)(2,1)}, u32[]{:S(2)}, u32[]{:S(2)}) collective-permute-start(bf16[2,256,2048]{2,1,0:T(8,128)(2,1)} %bitcast.18), channel_id=1, source_target_pairs={{0,1},{1,0},{2,3},{3,2},{4,5},{5,4},{6,7},{7,6},{8,9},{9,8},{10,11... | collective-permute-start | bytes 6291464 | tf_op jit(solution)/shard_map/ppermute | solution.py:27
  25.5 509.3 %reduce-scatter.8.cloned.1.call-start = ((), (), s32[]{:S(2)}) async-start(), calls=%async_computation.2 | async-start | bytes 2621440 | tf_op jit(solution)/shard_map/reduce_scatter | solution.py:120
  49.2 118.9 %collective-permute-start.1 = (bf16[2,256,2048]{2,1,0:T(8,128)(2,1)}, bf16[2,256,2048]{2,1,0:T(8,128)(2,1)}, u32[]{:S(2)}, u32[]{:S(2)}) collective-permute-start(bf16[2,256,2048]{2,1,0:T(8,128)(2,1)} %fusion.23), channel_id=1, source_target_pairs={{0,2},{1,3},{2,0},{3,1},{4,6},{5,7},{6,4},{7,5},{8,10},{9,11},{10,... | collective-permute-start | bytes 6291464 | tf_op jit(solution)/shard_map/ppermute | solution.py:27
  79.0 89.2 %collective-permute-start.4 = (bf16[2,256,2048]{1,2,0:T(8,128)(2,1)}, bf16[2,256,2048]{1,2,0:T(8,128)(2,1)}, u32[]{:S(2)}, u32[]{:S(2)}) collective-permute-start(bf16[2,256,2048]{1,2,0:T(8,128)(2,1)} %collective-permute-done.3), channel_id=1, source_target_pairs={{0,4},{4,0},{8,12},{12,8},{16,20},{20,16},{24,28},{28,24},{1,5},{5... | collective-permute-start | bytes 6291464 | tf_op jit(solution)/shard_map/ppermute | solution.py:27
  83.9 107.5 %collective-permute-start = (bf16[2,256,2048]{2,1,0:T(8,128)(2,1)}, bf16[2,256,2048]{2,1,0:T(8,128)(2,1)}, u32[]{:S(2)}, u32[]{:S(2)}) collective-permute-start(bf16[2,256,2048]{2,1,0:T(8,128)(2,1)} %fusion.23), channel_id=1, source_target_pairs={{0,1},{1,0},{2,3},{3,2},{4,5},{5,4},{6,7},{7,6},{8,9},{9,8},{10,11... | collective-permute-start | bytes 6291464 | tf_op jit(solution)/shard_map/ppermute | solution.py:27
  123.9 49.3 %collective-permute-start.8 = (bf16[2,256,2048]{2,1,0:T(8,128)(2,1)}, bf16[2,256,2048]{2,1,0:T(8,128)(2,1)}, u32[]{:S(2)}, u32[]{:S(2)}) collective-permute-start(bf16[2,256,2048]{2,1,0:T(8,128)(2,1)} %collective-permute-done.7), channel_id=1, source_target_pairs={{0,1},{1,0},{2,3},{3,2},{4,5},{5,4},{6,7},{7,6},{8,9},{9,8},{10,11... | collective-permute-start | bytes 6291464 | tf_op jit(solution)/shard_map/ppermute | solution.py:27
  326.6 130.0 %collective-permute-start.26 = (bf16[4,128,2048]{2,1,0:T(8,128)(2,1)}, bf16[4,128,2048]{2,1,0:T(8,128)(2,1)}, u32[]{:S(2)}, u32[]{:S(2)}) collective-permute-start(bf16[4,128,2048]{2,1,0:T(8,128)(2,1)} %dynamic-slice_bitcast_fusion.1), channel_id=1, source_target_pairs={{0,4},{4,0},{8,12},{12,8},{16,20},{20,16},{24,28},{28,24},{1,5},{5... | collective-permute-start | bytes 6291464 | tf_op jit(solution)/shard_map/ppermute | solution.py:27
  340.5 149.0 %collective-permute-start.18 = (bf16[4,4,64,1024]{3,2,0,1:T(8,128)(2,1)}, bf16[4,4,64,1024]{3,2,0,1:T(8,128)(2,1)}, u32[]{:S(2)}, u32[]{:S(2)}) collective-permute-start(bf16[4,4,64,1024]{3,2,0,1:T(8,128)(2,1)} %dynamic-slice_bitcast_fusion.2), channel_id=1, source_target_pairs={{0,4},{4,0},{8,12},{12,8},{16,20},{20,16},{24,28},{28,24},{1,5},{5... | collective-permute-start | bytes 6291464 | tf_op jit(solution)/shard_map/ppermute | solution.py:27
  441.3 62.8 %collective-permute-start.22 = (bf16[4,4,64,1408]{3,2,0,1:T(8,128)(2,1)}, bf16[4,4,64,1408]{3,2,0,1:T(8,128)(2,1)S(1)}, u32[]{:S(2)}, u32[]{:S(2)}) collective-permute-start(bf16[4,4,64,1408]{3,2,0,1:T(8,128)(2,1)} %dynamic-slice_bitcast_fusion), channel_id=1, source_target_pairs={{0,4},{4,0},{8,12},{12,8},{16,20},{20,16},{24,28},{28,24},{1,5},{5... | collective-permute-start | bytes 8650760 | tf_op jit(solution)/shard_map/ppermute | solution.py:27
  460.4 228.0 %all-reduce.16.cloned.1.call-start = ((), (), s32[]{:S(2)}) async-start(), calls=%async_computation.7 | async-start | bytes 9961472
  506.6 228.1 %all-gather.10.cloned.1.call-start = ((), (), s32[]{:S(2)}) async-start(), calls=%async_computation.3 | async-start | bytes 2621440 | tf_op jit(solution)/shard_map/all_gather | solution.py:127
  523.3 167.7 %collective-permute-start.9 = (bf16[2,2,256,2048]{3,2,1,0:T(8,128)(2,1)}, bf16[2,2,256,2048]{3,2,1,0:T(8,128)(2,1)}, u32[]{:S(2)}, u32[]{:S(2)}) collective-permute-start(bf16[2,2,256,2048]{3,2,1,0:T(8,128)(2,1)} %slice_bitcast_fusion.2), channel_id=1, source_target_pairs={{0,1},{1,0},{2,3},{3,2},{4,5},{5,4},{6,7},{7,6},{8,9},{9,8},{10,11... | collective-permute-start | bytes 12582920 | tf_op jit(solution)/shard_map/ppermute | solution.py:27
  534.9 264.8 %all-gather.12.cloned.1.call-start = ((), (), s32[]{:S(2)}) async-start(), calls=%async_computation.4 | async-start | bytes 2621440 | tf_op jit(solution)/shard_map/all_gather | solution.py:127
  538.7 181.1 %collective-permute-start.12 = (bf16[1,2,256,2048]{3,2,1,0:T(8,128)(2,1)}, bf16[1,2,256,2048]{3,2,1,0:T(8,128)(2,1)}, u32[]{:S(2)}, u32[]{:S(2)}) collective-permute-start(bf16[1,2,256,2048]{3,2,1,0:T(8,128)(2,1)} %fusion.50), channel_id=1, source_target_pairs={{0,2},{1,3},{2,0},{3,1},{4,6},{5,7},{6,4},{7,5},{8,10},{9,11},{10,... | collective-permute-start | bytes 6291464 | tf_op jit(solution)/shard_map/ppermute | solution.py:27
  703.0 132.0 %all-gather.14.cloned.1.call-start = ((), (), s32[]{:S(2)}) async-start(), calls=%async_computation.5 | async-start | bytes 2867200 | tf_op jit(solution)/shard_map/all_gather | solution.py:127
  716.2 72.4 %collective-permute-start.10 = (bf16[1,2,256,2048]{3,2,1,0:T(8,128)(2,1)}, bf16[1,2,256,2048]{3,2,1,0:T(8,128)(2,1)}, u32[]{:S(2)}, u32[]{:S(2)}) collective-permute-start(bf16[1,2,256,2048]{3,2,1,0:T(8,128)(2,1)} %fusion.49), channel_id=1, source_target_pairs={{0,2},{1,3},{2,0},{3,1},{4,6},{5,7},{6,4},{7,5},{8,10},{9,11},{10,... | collective-permute-start | bytes 6291464 | tf_op jit(solution)/shard_map/ppermute | solution.py:27
  724.3 42.2 %collective-permute-start.13 = (f32[23808]{0:T(1024)S(1)}, f32[23808]{0:T(1024)S(1)}, u32[]{:S(2)}, u32[]{:S(2)}) collective-permute-start(f32[23808]{0:T(1024)S(1)} %pad_maximum_fusion.16), channel_id=1, source_target_pairs={{0,2},{1,3},{2,0},{3,1},{4,6},{5,7},{6,4},{7,5},{8,10},{9,11},{10,... | collective-permute-start | bytes 285704 | tf_op jit(solution)/shard_map/ppermute | solution.py:27
  734.7 101.7 %collective-permute-start.27 = (bf16[4,128,2048]{2,1,0:T(8,128)(2,1)}, bf16[4,128,2048]{2,1,0:T(8,128)(2,1)}, u32[]{:S(2)}, u32[]{:S(2)}) collective-permute-start(bf16[4,128,2048]{2,1,0:T(8,128)(2,1)} %all-gather.10.cloned.1.call-done), channel_id=1, source_target_pairs={{0,4},{4,0},{8,12},{12,8},{16,20},{20,16},{24,28},{28,24},{1,5},{5... | collective-permute-start | bytes 6291464 | tf_op jit(solution)/shard_map/ppermute | solution.py:27
  799.7 48.8 %collective-permute-start.21 = (bf16[4,64,4,1024]{3,1,0,2:T(8,128)(2,1)}, bf16[4,64,4,1024]{3,1,0,2:T(8,128)(2,1)S(1)}, u32[]{:S(2)}, u32[]{:S(2)}) collective-permute-start(bf16[4,64,4,1024]{3,1,0,2:T(8,128)(2,1)} %bitcast.307), channel_id=1, source_target_pairs={{0,4},{4,0},{8,12},{12,8},{16,20},{20,16},{24,28},{28,24},{1,5},{5... | collective-permute-start | bytes 6291464 | tf_op jit(solution)/shard_map/ppermute | solution.py:27
  835.0 59.0 %collective-permute-start.25 = (bf16[4,64,4416]{2,1,0:T(8,128)(2,1)}, bf16[4,64,4416]{2,1,0:T(8,128)(2,1)S(1)}, u32[]{:S(2)}, u32[]{:S(2)}) collective-permute-start(bf16[4,64,4416]{2,1,0:T(8,128)(2,1)} %bitcast.304), channel_id=1, source_target_pairs={{0,4},{4,0},{8,12},{12,8},{16,20},{20,16},{24,28},{28,24},{1,5},{5... | collective-permute-start | bytes 6782984 | tf_op jit(solution)/shard_map/ppermute | solution.py:27
  (52 other events, 978.0 us)
Sparse Core Ops, SparseCore 0:
  13.4 32.8 all-reduce.13
  47.9 27.3 all-gather.7
  460.5 43.7 reduce-scatter.7
  507.2 181.1 all-reduce.15
  689.8 44.9 all-gather.9
  736.2 48.9 all-gather.11
  786.8 48.1 all-gather.13

commit v2 on v1

v2 whole, which is shorter than its diff:
```python
from functools import partial

import jax
import jax.numpy as jnp
from jax import lax
from jax.experimental import pallas as pl
from jax.experimental.pallas import tpu as pltpu
from jax.sharding import PartitionSpec as P

INNER = 4096
HEADS = 64
HEADDIM = 64
STATE = 128
CONV = 4
XBC = 4352
LANES = 128
EPSILON = 1e-05
FAR = -1e30
HIGHEST = lax.Precision.HIGHEST
VMEM = 48 * 1024 * 1024
F32 = jnp.float32
BF16 = jnp.bfloat16


def swap(value, axis, bit):
    count = lax.axis_size(axis)
    return lax.ppermute(value, axis, [(i, i ^ bit) for i in range(count)])


def after(value, *earlier):
    return lax.optimization_barrier((value,) + earlier)[0] if earlier else value


def bits_of(count):
    return [1 << k for k in reversed(range(count.bit_length() - 1))]


def gather_far(piece):
    held = {0: piece}
    for bit in bits_of(lax.axis_size("fsdp"))[:-1]:
        for r, part in list(held.items()):
            held[r ^ bit] = swap(part, "fsdp", bit)
    return held


def gather_near(held, *later):
    for r, part in list(held.items()):
        held[r ^ 1] = swap(after(part, *later), "fsdp", 1)
    return [held[r] for r in range(len(held))]


def gathered(piece):
    return gather_near(gather_far(piece))


def permuted(parts, own):
    stacked = jnp.stack(parts)
    return [
        lax.dynamic_index_in_dim(stacked, own ^ i, 0, keepdims=False) for i in range(len(parts))
    ]


def absolute(parts):
    return permuted(parts, lax.axis_index("fsdp"))


def traded(blocks, send, arrived):
    held = {r: {0: block} for r, block in enumerate(blocks)}
    for bit in bits_of(len(blocks)):
        going = [r for r in sorted(held) if r & bit]
        sources = sorted(held[going[0]])
        got = send(jnp.stack([held[r][s] for r in going for s in sources]), bit)
        arrived.append(got)
        place = 0
        for r in going:
            for s in sources:
                held[r ^ bit][s ^ bit] = got[place]
                place += 1
            del held[r]
    return [held[0][s] for s in sorted(held[0])]


def traded_weights(in_rows, inner, between):
    own = lax.axis_index("fsdp")
    side = lax.axis_index("group") & 3
    rows = in_rows.shape[1]
    half = inner // 2
    parts = lax.axis_size("fsdp")

    def block(r, kind, first, size):
        at = kind * INNER + (own ^ r) * inner + first
        return lax.dynamic_slice(in_rows, (at, jnp.zeros_like(at)), (size, rows))

    def piece(r, s):
        if s in held[r]:
            return held[r][s]
        return jnp.stack([block(r, kind, 0, inner) for kind in (0, 1)]).reshape(4, half, rows)

    def quarter(r, s):
        if s in held[r]:
            return held[r][s][0]
        return block(r, side // 2, (side & 1) * half, half)

    held = {r: {} for r in range(parts)}
    sources = [0]
    pins = None
    for bit in bits_of(parts):
        going = [r for r in sorted(held) if r & bit]
        order = [(r, s) for r in going for s in sources]
        if bit > 1:
            sent = jnp.stack([quarter(r, s) for r, s in order])
            mine = swap(sent, "fsdp", bit)
            if pins is None:
                pins = between(sent, mine)
            by_x = swap(mine, "group", 1)
            by_z = swap(mine, "group", 2)
            cut = half // 2
            rest = [
                swap(after(by_z[:, :cut], *pins[0]), "group", 1),
                swap(after(by_x[:, cut:], *pins[0]), "group", 2),
            ]
            got = jnp.stack([mine, by_x, by_z, jnp.concatenate(rest, axis=1)], axis=1)
        else:
            got = [swap(after(piece(r, s), *pins[1]), "fsdp", bit) for r, s in order]
        for (r, s), part in zip(order, got):
            held[r ^ bit][s ^ bit] = part
        for r in going:
            del held[r]
        sources += [s ^ bit for s in sources]
    return [piece(0, s) for s in range(parts)]


def scattered(value, pins):
    bit = 1
    while value.shape[0] > 1:
        pairs = value.reshape((value.shape[0] // 2, 2) + value.shape[1:])
        got = swap(pairs[:, 1].astype(BF16), "fsdp", bit)
        got = after(got, *(pins[0] if pins else ()))
        pins = pins[1:]
        value = pairs[:, 0].astype(F32) + got.astype(F32)
        bit *= 2
    return value[0]


def summed(value, axis, kind=F32, pin=()):
    bits = bits_of(lax.axis_size(axis))[::-1]
    for bit in bits:
        got = swap(value.astype(kind), axis, bit)
        value = value + after(got, *(pin if bit == bits[0] else ())).astype(F32)
    return value


def lines():
    count = lax.axis_size("group")
    return [list(range(side, count, 2)) for side in (0, 1)]


class Lines:
    def __init__(self):
        self.last = None

    def order(self, value):
        return value if self.last is None else after(value, self.last)

    def scatter(self, value):
        self.last = lax.psum_scatter(
            self.order(value), "group", scatter_dimension=0, axis_index_groups=lines()
        )
        return self.last

    def gather(self, value):
        self.last = lax.all_gather(
            self.order(value), "group", axis=0, axis_index_groups=lines()
        )
        return self.last


class Chain:
    def __init__(self, part):
        self.count = lax.axis_size("group") // 2
        self.own = part
        self.up = []
        self.down = []

    def shifted(self, value, by):
        pairs = [(i, i + 2 * by) for i in range(2 * self.count) if 0 <= i + 2 * by < 2 * self.count]
        return lax.ppermute(value, "group", pairs)

    def step(self, *earlier):
        up, down = (self.up[-1], self.down[-1]) if self.up else (self.own, self.own)
        self.up.append(self.shifted(after(up, *earlier), 1))
        self.down.append(self.shifted(after(down, *earlier), -1))
        return self.up[-1], self.down[-1]

    def result(self):
        while len(self.up) < self.count - 1:
            self.step()
        place = lax.axis_index("group") // 2
        every = jnp.stack(self.down[::-1] + [self.own] + self.up)
        middle = self.count - 1
        return jnp.stack(
            [
                lax.dynamic_index_in_dim(every, middle + place - i, 0, keepdims=False)
                for i in range(self.count)
            ]
        )


def dot(a, b, contract=((1,), (0,)), precision=None):
    return lax.dot_general(a, b, (contract, ((), ())), precision=precision, preferred_element_type=F32)


def steps(dt_ref, head_ref, tri):
    raw = dt_ref[...] + head_ref[0:1, :]
    size = jnp.maximum(raw, 0.0) + jnp.log1p(jnp.exp(-jnp.abs(raw)))
    log_decay = size * head_ref[1:2, :]
    running = dot(tri, log_decay, precision=HIGHEST)
    return raw, size, log_decay, running


def columns(row, chunk):
    return jnp.broadcast_to(row, (LANES, chunk)).T


def squared(array, chunk):
    return array if chunk == LANES else array[:, :chunk]


def forward_kernel(
    chunk,
    own_ref,
    pre_ref,
    tail_ref,
    gate_ref,
    dt_ref,
    back_ref,
    row_ref,
    taps_ref,
    head_ref,
    skip_ref,
    gain_ref,
    act_ref,
    slope_ref,
    out_ref,
    gained_ref,
    enter_ref,
    stat_ref,
    state,
    window,
    carried,
    flown,
):
    where = pl.program_id(0)
    inner = gate_ref.shape[1]
    channels = act_ref.shape[1]

    @pl.when(where == 0)
    def _():
        state[...] = jnp.zeros_like(state)
        window[0:8, :] = jnp.zeros((8, channels), F32)

    start = (where * chunk).astype(F32)
    seg_row = row_ref[0:1, :]
    seg_col = columns(seg_row, chunk)
    time = lax.broadcasted_iota(jnp.int32, (chunk, LANES), 0).astype(F32) + start
    seen = [(seg_col <= time - back).astype(F32) for back in range(1, CONV)]
    window[8:, :inner] = pre_ref[...].astype(F32)
    window[8:, inner:] = tail_ref[...].astype(F32)
    for at in range(0, channels, LANES):
        lanes = slice(at, at + LANES)
        total = taps_ref[4:5, lanes] + taps_ref[3:4, lanes] * window[8 : 8 + chunk, lanes]
        for back in range(1, CONV):
            total += taps_ref[3 - back : 4 - back, lanes] * (
                window[8 - back : 8 - back + chunk, lanes] * seen[back - 1]
            )
        sig = jax.nn.sigmoid(total)
        act_ref[:, lanes] = (total * sig).astype(BF16)
        slope_ref[:, lanes] = (sig * (1.0 + total * (1.0 - sig))).astype(BF16)
    window[0:8, :] = window[chunk : chunk + 8, :]

    seg_last = seg_row[:, chunk - 1 : chunk]
    down = lax.broadcasted_iota(jnp.int32, (chunk, chunk), 0)
    across = lax.broadcasted_iota(jnp.int32, (chunk, chunk), 1)
    tri = (across <= down).astype(F32)
    _, size, _, running = steps(dt_ref, head_ref, tri)
    running_t = running.T
    size_t = size.T
    b_input = act_ref[:, inner : inner + STATE]
    c_output = act_ref[:, inner + STATE :]
    gram = dot(c_output, b_input, ((1,), (1,)))
    veil = jnp.where((squared(seg_col, chunk) == seg_row) & (across <= down), 0.0, FAR)
    crossing = (seg_col < start).astype(F32)
    ending = (seg_col == seg_last).astype(F32)
    passing = (seg_last < start).astype(F32)
    last = running[chunk - 1 : chunk, :]
    low = lax.broadcasted_iota(jnp.int32, (chunk, LANES), 1) < HEADDIM
    low_row = low[0:1, :]
    entering = state[...].astype(BF16)
    enter_ref[...] = entering
    carried[...] = dot(c_output, entering)
    squares = jnp.zeros((chunk, LANES), F32)
    products = jnp.zeros((chunk, LANES), F32)
    for pair in range(inner // LANES):
        lanes = slice(pair * LANES, (pair + 1) * LANES)
        heads = (2 * pair, 2 * pair + 1)
        x_pair = act_ref[:, lanes].astype(F32)
        run = [running[:, h : h + 1] for h in heads]
        mixing = [
            (jnp.exp(run[k] - running_t[h : h + 1, :] + veil) * gram * size_t[h : h + 1, :]).astype(
                BF16
            )
            for k, h in enumerate(heads)
        ]
        halves = [jnp.where(low, x_pair, 0.0).astype(BF16), jnp.where(low, 0.0, x_pair).astype(BF16)]
        inside = dot(jnp.concatenate(mixing, axis=1), jnp.concatenate(halves, axis=0))
        run_pair = jnp.where(low, run[0], run[1])
        size_pair = jnp.where(low, size[:, heads[0] : heads[0] + 1], size[:, heads[1] : heads[1] + 1])
        last_pair = jnp.where(
            low_row, last[:, heads[0] : heads[0] + 1], last[:, heads[1] : heads[1] + 1]
        )
        ssm = (
            inside
            + carried[:, lanes] * (jnp.exp(run_pair) * crossing)
            + skip_ref[:, lanes] * x_pair
        )
        outflow = jnp.exp(last_pair - run_pair) * ending * size_pair
        flown[:, lanes] = (x_pair * outflow).astype(BF16)
        state[:, lanes] = (jnp.exp(last_pair) * passing) * state[:, lanes]
        gate = gate_ref[:, lanes]
        gated = ssm * (gate * jax.nn.sigmoid(gate))
        out_ref[:, lanes] = ssm
        gained = gated * gain_ref[:, lanes]
        gained_ref[:, lanes] = gained.astype(BF16)
        squares += gated * gated
        products += gained * back_ref[:, lanes].astype(F32)
    state[...] += dot(b_input, flown[...], ((0,), (0,)))
    stat_ref[0:1, :] = jnp.sum(squares.T, axis=0, keepdims=True)
    stat_ref[1:2, :] = jnp.sum(products.T, axis=0, keepdims=True)
    stat_ref[2:8, :] = jnp.zeros((6, chunk), F32)


def gate_kernel(
    chunk,
    own_ref,
    out_ref,
    gate_ref,
    back_ref,
    stat_ref,
    gain_ref,
    grad_ssm_ref,
    grad_gate_ref,
    gated_ref,
    grad_gain_ref,
):
    inner = gate_ref.shape[1]

    @pl.when(pl.program_id(0) == 0)
    def _():
        grad_gain_ref[...] = jnp.zeros_like(grad_gain_ref)

    scale = lax.rsqrt(stat_ref[0:1, :] * (1.0 / INNER) + EPSILON)
    shift = scale * scale * scale * stat_ref[1:2, :] * (1.0 / INNER)
    scale = columns(scale, chunk)
    shift = columns(shift, chunk)
    for at in range(0, inner, LANES):
        lanes = slice(at, at + LANES)
        ssm = out_ref[:, lanes]
        gate = gate_ref[:, lanes]
        back = back_ref[:, lanes].astype(F32)
        sig = jax.nn.sigmoid(gate)
        silu = gate * sig
        gated = ssm * silu
        scaled = gated * scale
        gain = gain_ref[:, lanes]
        grad_gated = scale * (gain * back) - gated * shift
        grad_ssm_ref[:, lanes] = (grad_gated * silu).astype(BF16)
        grad_gate_ref[:, lanes] = (
            grad_gated * ssm * (sig * (1.0 + gate * (1.0 - sig)))
        ).astype(BF16)
        gated_ref[:, lanes] = (scaled * gain).astype(BF16)
        grad_gain_ref[0:1, lanes] += jnp.sum(scaled * back, axis=0, keepdims=True)


def backward_kernel(
    chunk,
    own_ref,
    act_ref,
    slope_ref,
    pre_ref,
    tail_ref,
    dt_ref,
    grad_ref,
    enter_ref,
    row_ref,
    taps_ref,
    head_ref,
    skip_ref,
    grad_pre_ref,
    grad_dt_ref,
    grad_taps_ref,
    grad_skip_ref,
    grad_head_ref,
    leaving,
    window,
    grad_act,
    row_sums,
    carried,
    fresh,
    into,
    flown,
):
    count = pl.num_programs(0)
    where = count - 1 - pl.program_id(0)
    inner = grad_ref.shape[1]
    channels = act_ref.shape[1]

    @pl.when(pl.program_id(0) == 0)
    def _():
        leaving[...] = jnp.zeros_like(leaving)
        window[chunk:, :] = jnp.zeros((8, channels), F32)
        grad_taps_ref[...] = jnp.zeros_like(grad_taps_ref)
        grad_skip_ref[...] = jnp.zeros_like(grad_skip_ref)
        grad_head_ref[...] = jnp.zeros_like(grad_head_ref)
        row_sums[...] = jnp.zeros_like(row_sums)

    start = (where * chunk).astype(F32)
    seg_row = row_ref[0:1, :]
    seg_col = columns(seg_row, chunk)
    seg_last = seg_row[:, chunk - 1 : chunk]
    down = lax.broadcasted_iota(jnp.int32, (chunk, chunk), 0)
    across = lax.broadcasted_iota(jnp.int32, (chunk, chunk), 1)
    tri = (across <= down).astype(F32)
    raw, size, log_decay, running = steps(dt_ref, head_ref, tri)
    running_t = running.T
    b_input = act_ref[:, inner : inner + STATE]
    c_output = act_ref[:, inner + STATE :]
    gram = dot(b_input, c_output, ((1,), (1,)))
    veil = jnp.where((squared(seg_col, chunk) == seg_row) & (down <= across), 0.0, FAR)
    crossing = (seg_col < start).astype(F32)
    ending = (seg_col == seg_last).astype(F32)
    passing = (seg_last < start).astype(F32)
    last = running[chunk - 1 : chunk, :]
    lane = lax.broadcasted_iota(jnp.int32, (chunk, LANES), 1)
    low = lane < HEADDIM
    low_row = low[0:1, :]
    lane_row = lane[0:1, :]
    left_low = leaving[...].astype(BF16)
    entering = enter_ref[...]
    carried[...] = dot(c_output, entering)
    fresh[...] = dot(b_input, left_low)
    grad_gram = jnp.zeros((chunk, chunk), F32)
    size_grad = jnp.zeros((chunk, LANES), F32)
    carry_grad = jnp.zeros((chunk, LANES), F32)
    total_grad = jnp.zeros((1, LANES), F32)
    for pair in range(inner // LANES):
        lanes = slice(pair * LANES, (pair + 1) * LANES)
        heads = (2 * pair, 2 * pair + 1)
        x_low = act_ref[:, lanes]
        x_pair = x_low.astype(F32)
        grad = grad_ref[:, lanes].astype(F32)
        halves = (low, jnp.logical_not(low))
        run = [running[:, h : h + 1] for h in heads]
        sizes = [size[:, h : h + 1] for h in heads]
        run_pair = jnp.where(low, run[0], run[1])
        size_pair = jnp.where(low, sizes[0], sizes[1])
        last_pair = jnp.where(
            low_row, last[:, heads[0] : heads[0] + 1], last[:, heads[1] : heads[1] + 1]
        )
        left = leaving[:, lanes]
        inflow = jnp.exp(run_pair) * crossing
        outflow = jnp.exp(last_pair - run_pair) * ending
        into_here = grad * inflow
        into[:, lanes] = into_here.astype(BF16)
        carry_here = into_here * carried[:, lanes]
        fresh_back = fresh[:, lanes] * outflow
        flown_here = x_pair * fresh_back
        flown[:, lanes] = (x_pair * outflow * size_pair).astype(BF16)
        whole = jnp.exp(last_pair) * passing
        kept = whole * jnp.sum(left * enter_ref[:, lanes].astype(F32), axis=0, keepdims=True)
        kept += jnp.sum(flown_here * size_pair, axis=0, keepdims=True)
        leaving[:, lanes] = whole * left
        both = jnp.concatenate(
            [jnp.where(low, grad, 0.0).astype(BF16), jnp.where(low, 0.0, grad).astype(BF16)], axis=0
        )
        back_both = dot(x_low, both, ((1,), (1,)))
        weights = []
        for k, h in enumerate(heads):
            mine = halves[k]
            decay = jnp.exp(running_t[h : h + 1, :] - run[k] + veil)
            weight = decay * gram
            weights.append((weight * sizes[k]).astype(BF16))
            back = back_both[:, k * chunk : (k + 1) * chunk]
            grad_gram += back * decay * sizes[k]
            straight = back * weight
            row_sums[h : h + 1, :] = jnp.sum(straight * sizes[k], axis=0, keepdims=True)
            flown_mine = jnp.where(mine, flown_here, 0.0)
            if chunk == LANES:
                size_here = jnp.sum(straight + flown_mine, axis=1, keepdims=True)
            else:
                size_here = jnp.sum(straight, axis=1, keepdims=True) + jnp.sum(
                    flown_mine, axis=1, keepdims=True
                )
            carry_mine = jnp.sum(jnp.where(mine, carry_here, 0.0), axis=1, keepdims=True)
            here = lane == h
            size_grad = jnp.where(here, size_here, size_grad)
            carry_grad = jnp.where(here, carry_mine, carry_grad)
            total_here = jnp.sum(jnp.where(mine[0:1, :], kept, 0.0), axis=1, keepdims=True)
            total_grad = jnp.where(lane_row == h, total_here, total_grad)
        grad_act[:, lanes] = (
            dot(jnp.concatenate(weights, axis=1), both)
            + fresh_back * size_pair
            + skip_ref[:, lanes] * grad
        )
        grad_skip_ref[0:1, lanes] += jnp.sum(grad * x_pair, axis=0, keepdims=True)
    grad_gram_low = grad_gram.astype(BF16)
    grad_act[:, inner : inner + STATE] = dot(grad_gram_low, c_output) + dot(
        flown[...], left_low, ((1,), (1,))
    )
    grad_act[:, inner + STATE :] = dot(grad_gram_low, b_input, ((0,), (0,))) + dot(
        into[...], entering, ((1,), (1,))
    )
    leaving[...] += dot(c_output, into[...], ((0,), (0,)))
    row_t = row_sums[...].T
    grad_run = row_t + carry_grad - size * size_grad
    upper = (across >= down).astype(F32)
    grad_decay = dot(upper, grad_run, precision=HIGHEST) + total_grad
    grad_size = grad_decay * head_ref[1:2, :] + size_grad
    grad_raw = jnp.where(lane < inner // HEADDIM, grad_size * jax.nn.sigmoid(raw), 0.0)
    grad_dt_ref[...] = grad_raw.astype(BF16)
    grad_head_ref[0:1, :] += jnp.sum(grad_raw, axis=0, keepdims=True)
    grad_head_ref[1:2, :] += jnp.sum(grad_decay * log_decay, axis=0, keepdims=True)

    same = [
        (columns(row_ref[ahead : ahead + 1, :], chunk) == seg_col).astype(F32)
        for ahead in range(1, CONV)
    ]
    for at in range(0, channels, LANES):
        lanes = slice(at, at + LANES)
        grad_sum = grad_act[:, lanes] * slope_ref[:, lanes].astype(F32)
        window[0:chunk, lanes] = grad_sum
        if at < inner:
            pre = pre_ref[:, lanes].astype(F32)
        else:
            pre = tail_ref[:, at - inner : at - inner + LANES].astype(F32)
        grad_pre = taps_ref[3:4, lanes] * grad_sum
        grad_taps_ref[3:4, lanes] += jnp.sum(pre * grad_sum, axis=0, keepdims=True)
        grad_taps_ref[4:5, lanes] += jnp.sum(grad_sum, axis=0, keepdims=True)
        for ahead in range(1, CONV):
            later = window[ahead : ahead + chunk, lanes] * same[ahead - 1]
            grad_pre += taps_ref[3 - ahead : 4 - ahead, lanes] * later
            grad_taps_ref[3 - ahead : 4 - ahead, lanes] += jnp.sum(
                pre * later, axis=0, keepdims=True
            )
        grad_pre_ref[:, lanes] = grad_pre.astype(BF16)
    window[chunk:, :] = window[0:8, :]


def scan_calls(parts, tok_count, inner):
    chunk = min(LANES, tok_count)
    per_part = tok_count // chunk
    count = parts * per_part
    channels = inner + 2 * STATE
    tokens = parts * tok_count

    def blocks(flip):
        def time(step):
            return count - 1 - step if flip else step

        def place(step, own):
            t = time(step)
            return lax.bitwise_xor(t // per_part, own[0]) * per_part + t % per_part

        def tok(width):
            return pl.BlockSpec((chunk, width), lambda step, own: (place(step, own), 0))

        row = pl.BlockSpec((None, 8, chunk), lambda step, own: (time(step), 0, 0))
        states = pl.BlockSpec((None, STATE, inner), lambda step, own: (time(step), 0, 0))

        def const(rows, width):
            return pl.BlockSpec((rows, width), lambda step, own: (0, 0))

        return tok, row, states, const

    def scan(kernel, ins, outs, shapes, scratch):
        return pl.pallas_call(
            partial(kernel, chunk),
            grid_spec=pltpu.PrefetchScalarGridSpec(
                num_scalar_prefetch=1,
                grid=(count,),
                in_specs=ins,
                out_specs=outs,
                scratch_shapes=scratch,
            ),
            out_shape=shapes,
            compiler_params=pltpu.CompilerParams(
                dimension_semantics=("arbitrary",), vmem_limit_bytes=VMEM
            ),
            cost_estimate=COST,
        )

    struct = jax.ShapeDtypeStruct
    tok, row, states, const = blocks(False)
    forward = scan(
        forward_kernel,
        [tok(inner), tok(2 * STATE), tok(inner), tok(LANES), tok(inner), row]
        + [const(8, channels), const(8, LANES), const(1, inner), const(1, inner)],
        [tok(channels), tok(channels), tok(inner), tok(inner), states, row],
        [
            struct((tokens, channels), BF16),
            struct((tokens, channels), BF16),
            struct((tokens, inner), F32),
            struct((tokens, inner), BF16),
            struct((count, STATE, inner), BF16),
            struct((count, 8, chunk), F32),
        ],
        [
            pltpu.VMEM((STATE, inner), F32),
            pltpu.VMEM((chunk + 8, channels), F32),
            pltpu.VMEM((chunk, inner), F32),
            pltpu.VMEM((chunk, inner), BF16),
        ],
    )
    gating = scan(
        gate_kernel,
        [tok(inner), tok(inner), tok(inner), row, const(1, inner)],
        [tok(inner), tok(inner), tok(inner), const(8, inner)],
        [struct((tokens, inner), BF16)] * 3 + [struct((8, inner), F32)],
        [],
    )
    tok, row, states, const = blocks(True)
    backward = scan(
        backward_kernel,
        [tok(channels), tok(channels), tok(inner), tok(2 * STATE), tok(LANES)]
        + [tok(inner), states, row]
        + [const(8, channels), const(8, LANES), const(1, inner)],
        [tok(channels), tok(LANES), const(8, channels), const(8, inner), const(8, LANES)],
        [
            struct((tokens, channels), BF16),
            struct((tokens, LANES), BF16),
            struct((8, channels), F32),
            struct((8, inner), F32),
            struct((8, LANES), F32),
        ],
        [
            pltpu.VMEM((STATE, inner), F32),
            pltpu.VMEM((chunk + 8, channels), F32),
            pltpu.VMEM((chunk, channels), F32),
            pltpu.VMEM((LANES, chunk), F32),
            pltpu.VMEM((chunk, inner), F32),
            pltpu.VMEM((chunk, inner), F32),
            pltpu.VMEM((chunk, inner), BF16),
            pltpu.VMEM((chunk, inner), BF16),
        ],
    )
    return forward, gating, backward


NN = ((1,), (0,))
NT = ((1,), (1,))
TN = ((0,), (0,))
COST = pl.CostEstimate(flops=1, bytes_accessed=1, transcendentals=0)


def call(kernel, grid, ins, outs, shapes, args, scratch=()):
    return pl.pallas_call(
        kernel,
        grid_spec=pltpu.PrefetchScalarGridSpec(
            num_scalar_prefetch=1,
            grid=grid,
            in_specs=ins,
            out_specs=outs,
            scratch_shapes=scratch,
        ),
        out_shape=shapes,
        compiler_params=pltpu.CompilerParams(
            dimension_semantics=("arbitrary",) * len(grid), vmem_limit_bytes=VMEM
        ),
        cost_estimate=COST,
    )(*args)


def fixed(shape):
    return pl.BlockSpec(shape, lambda i, own: (0,) * len(shape))


def own_heads(own, heads):
    head = lax.broadcasted_iota(jnp.int32, (HEADS, LANES), 0)
    lane = lax.broadcasted_iota(jnp.int32, (HEADS, LANES), 1)
    return ((head == own * heads + lane) & (lane < heads)).astype(F32)


def project_kernel(parts, own_ref, *refs):
    tok_refs, weights, tails = refs[:parts], refs[parts : 2 * parts], refs[2 * parts : 3 * parts]
    gain_ref, normed_ref, gate_ref, pre_ref, tail_ref, dt_ref, ordered = refs[3 * parts :]
    at = pl.program_id(0)
    rows = tails[0].shape[1]
    tok_count = tok_refs[0].shape[0]

    @pl.when(at == 0)
    def _():
        for r in range(parts):
            values = tok_refs[r][...].astype(F32)
            mean = jnp.mean(values * values, axis=-1, keepdims=True)
            normed_ref[r * tok_count : (r + 1) * tok_count, :] = (
                values * lax.rsqrt(mean + EPSILON) * gain_ref[...]
            ).astype(BF16)
        for s in range(parts):
            lanes = pl.ds(pl.multiple_of(lax.bitwise_xor(own_ref[0], s) * rows, LANES), rows)
            ordered[:, s * rows : (s + 1) * rows] = normed_ref[:, lanes]

    def total(refs):
        return dot(ordered[...], jnp.concatenate([ref[...] for ref in refs], axis=1), NT)

    @pl.when(at < 2)
    def _():
        gate_ref[...] = total(weights)

    @pl.when((at >= 2) & (at < 4))
    def _():
        pre_ref[...] = total(weights).astype(BF16)

    @pl.when(at == 4)
    def _():
        rest = total(tails)
        tail_ref[...] = rest[:, : 2 * STATE].astype(BF16)
        pick = own_heads(own_ref[0], HEADS // parts)
        dt_ref[...] = dot(rest[:, 2 * STATE :], pick, precision=HIGHEST)


def project(own_arg, tok_parts, weights, tails, gain):
    parts, (tok_count, width) = len(tok_parts), tok_parts[0].shape
    half, rows = weights[0].shape[1:]
    tokens = parts * tok_count

    def near(i, own):
        return (jnp.minimum(i, 3), 0, 0)

    def far(i, own):
        return (lax.bitwise_xor(jnp.minimum(i, 3), own[1]), 0, 0)

    struct = jax.ShapeDtypeStruct
    return call(
        partial(project_kernel, parts),
        (5,),
        [fixed((tok_count, width))] * parts
        + [pl.BlockSpec((None, half, rows), far if s > 1 else near) for s in range(parts)]
        + [fixed(tails[0].shape)] * parts
        + [fixed((1, width))],
        [
            fixed((tokens, width)),
            pl.BlockSpec((tokens, half), lambda i, own: (0, jnp.minimum(i, 1))),
            pl.BlockSpec((tokens, half), lambda i, own: (0, jnp.clip(i - 2, 0, 1))),
            fixed((tokens, 2 * STATE)),
            fixed((tokens, LANES)),
        ],
        [
            struct((tokens, width), BF16),
            struct((tokens, 2 * half), F32),
            struct((tokens, 2 * half), BF16),
            struct((tokens, 2 * STATE), BF16),
            struct((tokens, LANES), F32),
        ],
        (own_arg, *tok_parts, *weights, *tails, gain[None]),
        [pltpu.VMEM((tokens, width), BF16)],
    )


def back_kernel(parts, own_ref, *refs):
    weight_ref, all_ref, back_ref = refs[parts:]
    tok_count = refs[0].shape[0]

    @pl.when(pl.program_id(0) == 0)
    def _():
        for r in range(parts):
            all_ref[r * tok_count : (r + 1) * tok_count, :] = refs[r][...]

    back_ref[...] = dot(all_ref[...], weight_ref[...], NT).astype(BF16)


def project_back(own_arg, cot_parts, weight):
    parts, (tok_count, width) = len(cot_parts), cot_parts[0].shape
    inner = weight.shape[0]
    block = min(256, inner)
    tokens = parts * tok_count
    struct = jax.ShapeDtypeStruct
    return call(
        partial(back_kernel, parts),
        (inner // block,),
        [fixed((tok_count, width))] * parts
        + [pl.BlockSpec((block, width), lambda i, own: (i, 0))],
        [fixed((tokens, width)), pl.BlockSpec((tokens, block), lambda i, own: (0, i))],
        [struct((tokens, width), BF16), struct((tokens, inner), BF16)],
        (own_arg, *cot_parts, weight),
    )


def out_kernel(own_ref, a_ref, b_ref, out_ref):
    out_ref[...] = dot(a_ref[...], b_ref[...]).astype(BF16)


def project_out(own_arg, gained, weight):
    (tokens, inner), width = gained.shape, weight.shape[1]
    block = min(512, tokens)
    return call(
        out_kernel,
        (tokens // block,),
        [pl.BlockSpec((block, inner), lambda i, own: (i, 0)), fixed((inner, width))],
        [pl.BlockSpec((block, width), lambda i, own: (i, 0))],
        [jax.ShapeDtypeStruct((tokens, width), BF16)],
        (own_arg, gained, weight),
    )[0]


def into_kernel(parts, own_ref, gate_ref, pre_ref, dt_ref, *refs):
    weights, tails, out_ref = refs[:parts], refs[parts : 2 * parts], refs[-1]
    half, rows = weights[0].shape[1:]
    inner = 2 * half
    pick = own_heads(own_ref[0], HEADS // parts).astype(BF16)
    grad_dt = dot(dt_ref[...], pick, NT).astype(BF16)
    left = jnp.concatenate([gate_ref[...], pre_ref[...], grad_dt], axis=1)
    for s in range(parts):
        order = [lax.bitwise_xor(q, own_ref[1]) if s > 1 else q for q in range(4)]
        right = jnp.concatenate([weights[s][q] for q in order] + [tails[s][...]], axis=0)
        lanes = pl.ds(pl.multiple_of(lax.bitwise_xor(own_ref[0], s) * rows, LANES), rows)
        out_ref[:, lanes] = dot(left, right).astype(BF16)


def project_into(own_arg, grad_gate, grad_pre, grad_dt, weights, tails):
    parts = len(weights)
    (tokens, inner), channels = grad_gate.shape, grad_pre.shape[1]
    width = parts * weights[0].shape[2]
    block = min(512, tokens)

    def tok(size):
        return pl.BlockSpec((block, size), lambda i, own: (i, 0))

    return call(
        partial(into_kernel, parts),
        (tokens // block,),
        [tok(inner), tok(channels), tok(LANES)]
        + [fixed(w.shape) for w in weights]
        + [fixed(r.shape) for r in tails],
        [tok(width)],
        [jax.ShapeDtypeStruct((tokens, width), BF16)],
        (own_arg, grad_gate, grad_pre, grad_dt, *weights, *tails),
    )[0]


def weight_kernel(count, halves, own_ref, *refs):
    outs = refs[2 * count :]
    total = dot(refs[0][...], refs[count][...], TN)
    for m in range(1, count):
        total += dot(refs[m][...], refs[count + m][...], TN)
    if halves == 1:
        outs[0][...] = total
    else:
        first = pl.program_id(0) < pl.num_programs(0) // 2

        @pl.when(first)
        def _():
            outs[0][...] = total.astype(BF16)

        @pl.when(jnp.logical_not(first))
        def _():
            outs[1][...] = total.astype(BF16)


def weight_grad(own_arg, lefts, rights, inner):
    tokens, width = rights[0].shape
    block = min(256, inner // 2)
    per = inner // 2 // block

    def left(i, own):
        return (0, lax.bitwise_xor(i // per, 1 - (own[1] & 1)) * per + i % per)

    out = jax.ShapeDtypeStruct((inner // 2, width), BF16)
    return call(
        partial(weight_kernel, len(lefts), 2),
        (2 * per,),
        [pl.BlockSpec((tokens, block), left)] * len(lefts)
        + [fixed((tokens, width))] * len(rights),
        [
            pl.BlockSpec((block, width), lambda i, own: (jnp.minimum(i, per - 1), 0)),
            pl.BlockSpec((block, width), lambda i, own: (jnp.maximum(i - per, 0), 0)),
        ],
        [out, out],
        (own_arg, *lefts, *rights),
    )


def tail_grad(own_arg, lefts, first, rights):
    (tokens, width), columns = rights[0].shape, lefts[0].shape[1] - first
    block = LANES
    return call(
        partial(weight_kernel, len(lefts), 1),
        (columns // block,),
        [pl.BlockSpec((tokens, block), lambda i, own: (0, first // block + i))] * len(lefts)
        + [fixed((tokens, width))] * len(rights),
        [pl.BlockSpec((block, width), lambda i, own: (i, 0))],
        [jax.ShapeDtypeStruct((columns, width), F32)],
        (own_arg, *lefts, *rights),
    )[0]


def on_device(
    tokens,
    segment_ids,
    cotangent,
    norm_gain,
    in_weight,
    conv_weight,
    conv_bias,
    dt_bias,
    a_log,
    skip_d,
    inner_gain,
    out_weight,
):
    micro, _, tok_count, width = tokens.shape
    parts = lax.axis_size("fsdp")
    groups = lax.axis_size("group")
    own = lax.axis_index("fsdp")
    inner = INNER // parts
    heads = HEADS // parts
    channels = inner + 2 * STATE
    rows = width // parts
    seq = tok_count * parts
    chunk = min(LANES, tok_count)
    forward, gating, backward = scan_calls(parts, tok_count, inner)
    side = lax.axis_index("group") & 3
    own_arg = jnp.stack([own, side]).astype(jnp.int32)
    along = Lines()

    def small(sent):
        taps_here = jnp.concatenate([conv_weight, conv_bias[None]], axis=0).astype(F32)
        packed = jnp.concatenate(
            [
                norm_gain.astype(F32),
                taps_here.reshape(-1),
                segment_ids.astype(F32).reshape(-1),
            ]
        )
        held = gather_far(after(packed, sent))
        packed = jnp.stack(absolute(gather_near(held)))
        cut = norm_gain.shape[0]
        gain_norm = packed[:, :cut].reshape(-1)
        taps_size = taps_here.size
        taps = packed[:, cut : cut + taps_size].reshape(parts, CONV + 1, -1)
        taps = taps.transpose(1, 0, 2).reshape(CONV + 1, XBC)
        seg = packed[:, cut + taps_size :].reshape(parts, micro, tok_count)
        seg = seg.transpose(1, 0, 2).reshape(micro, seq)
        taps = jnp.concatenate(
            [lax.dynamic_slice_in_dim(taps, own * inner, inner, 1), taps[:, INNER:]], axis=1
        )
        taps = jnp.pad(taps, ((0, 8 - CONV - 1), (0, 0)))
        seg_rows = [seg] + [
            jnp.pad(seg[:, ahead:], ((0, 0), (0, ahead)), constant_values=-1.0)
            for ahead in range(1, CONV)
        ]
        seg_rows = jnp.stack([part.reshape(micro, -1, chunk) for part in seg_rows], axis=2)
        seg_rows = jnp.pad(seg_rows, ((0, 0), (0, 0), (0, 8 - CONV), (0, 0)))
        head_row = jnp.concatenate(
            [dt_bias.astype(F32)[None], -jnp.exp(a_log.astype(F32))[None]], axis=0
        )
        head_row = jnp.pad(head_row, ((0, 6), (0, LANES - heads)))
        skip_row = jnp.repeat(skip_d.astype(F32), HEADDIM)[None]
        gain_row = inner_gain.astype(F32)[None]
        return held[parts // 2], (gain_norm, taps, seg_rows, head_row, skip_row, gain_row)

    in_rows = in_weight.T
    started = {}

    def between(sent, got):
        packed, started["small"] = small(sent)
        started["tok"] = [gather_far(after(tokens[m, 0], got)) for m in range(micro)]
        first = started["tok"][0][parts // 2]
        last = started["tok"][-1][parts // 2]
        started["tail"] = gather_far(after(in_rows[2 * INNER :], first))
        started["cot"] = [gather_far(after(cotangent[0, 0], last))]
        return [first, packed], list(started["small"])

    weights = traded_weights(in_rows, inner, between)
    gain_norm, taps, seg_rows, head_row, skip_row, gain_row = started["small"]
    tails = gather_near(started["tail"], weights[1])
    tok_parts = [gather_near(held, weights[1]) for held in started["tok"]]

    tok_rows = tokens[:, 0].astype(F32)
    inverse = lax.rsqrt(jnp.mean(tok_rows * tok_rows, axis=-1, keepdims=True) + EPSILON)
    cot_here = cotangent[:, 0]

    projected = []
    last = started["tok"][-1][parts // 2]
    for m in range(micro):
        tok_here = [after(part, last, *[p[0] for p in projected[-1:]]) for part in tok_parts[m]]
        projected.append(project(own_arg, tok_here, weights, tails, gain_norm))
    normed_all = [p[0] for p in projected]
    for m in range(1, micro):
        started["cot"].append(
            gather_far(after(cotangent[m, 0], started["cot"][m - 1][parts // 2], normed_all[0]))
        )
    scans = []
    cot_all = []
    for m in range(micro):
        parts_here = gather_near(started["cot"][m], *(scans[m - 1][-1:] if m else normed_all[-1:]))
        cot, back = project_back(own_arg, parts_here, out_weight)
        _, gate, pre, tail, dt_raw = projected[m]
        outs = forward(
            own_arg, pre, tail, gate, dt_raw, back, seg_rows[m], taps, head_row, skip_row, gain_row
        )
        cot_all.append(cot)
        scans.append((gate, pre, tail, dt_raw, back) + tuple(outs))
    out_grads = []
    for m in range(micro):
        gate, _, _, _, back, _, _, ssm, gained, entering, stat = scans[m]
        stat = jnp.pad(summed(stat[:, :2], "fsdp"), ((0, 0), (0, 6), (0, 0)))
        out_grads.append((stat,) + tuple(gating(own_arg, ssm, gate, back, stat, gain_row)))

    def scan_back(m, *earlier):
        _, pre, tail, dt_raw, _, act, slope, _, _, entering, _ = scans[m]
        return backward(
            own_arg,
            act,
            slope,
            pre,
            tail,
            dt_raw,
            after(out_grads[m][1], *earlier),
            entering,
            seg_rows[m],
            taps,
            head_row,
            skip_row,
        )

    def across(away):
        return swap(away, "group", 1)

    def joined(keep, got):
        total = (keep.astype(F32) + got.astype(F32)).astype(BF16)
        return total.reshape(groups // 2, -1, width)

    def finish(half):
        arrived = []
        here = [lax.dynamic_slice_in_dim(half, (own ^ r) * rows, rows, 1) for r in range(parts)]
        here = traded(here, lambda value, bit: swap(value, "fsdp", bit), arrived)
        return jnp.stack(absolute(here)), arrived

    def by_part(value):
        return value.reshape(parts, tok_count, width)

    away_gate, keep_gate = weight_grad(own_arg, [g[2] for g in out_grads], normed_all, inner)
    got_gate = across(away_gate)
    gated = [after(g[3], keep_gate) for g in out_grads]
    away_out, keep_out = weight_grad(own_arg, gated, cot_all, inner)
    got_out = across(away_out)
    backs = [scan_back(0, keep_out)]
    mixed = [project_out(own_arg, after(scans[0][8], backs[0][0]), out_weight)]
    half_gate = joined(keep_gate, after(got_gate, mixed[0]))
    for m in range(1, micro):
        backs.append(scan_back(m, half_gate, *mixed[-1:]))
        mixed.append(project_out(own_arg, after(scans[m][8], backs[m][0]), out_weight))
    half_gate = along.scatter(half_gate)
    half_out = joined(keep_out, after(got_out, mixed[-1], half_gate))
    left = [after(b[0], half_out) for b in backs]
    away_x, keep_x = weight_grad(own_arg, left, normed_all, inner)
    got_x = across(away_x)
    half_out = along.scatter(half_out)
    gate_cols, arrived = finish(half_gate)

    def project_in(m, *earlier):
        grad_gate = after(out_grads[m][2], *earlier)
        return project_into(own_arg, grad_gate, *backs[m][:2], weights, tails)

    into = [project_in(0, keep_x, arrived[0])]
    chains = [Chain(gate_cols), Chain(half_out)]
    rights = [after(n, into[0], gate_cols, half_out) for n in normed_all]
    grad_tail = jnp.concatenate(
        [
            tail_grad(own_arg, [b[0] for b in backs], inner, rights),
            tail_grad(own_arg, [b[1] for b in backs], 0, rights),
        ],
        axis=0,
    )
    sent = [chains[0].step(keep_x)]
    into += [project_in(m, grad_tail, *sent[0], *into[-1:]) for m in range(1, micro)]
    chains[0].step(into[-1])
    chains[1].step(grad_tail)
    half_x = joined(keep_x, after(got_x, grad_tail, *into))
    for chain in (chains[0], chains[1], chains[1]):
        chain.step(half_x)
    mixed[0] = scattered(by_part(mixed[0]), [[backs[-1][0]], [keep_x]])
    mixed[1:] = [scattered(by_part(v), [[keep_x], [grad_tail]]) for v in mixed[1:]]
    into_sums = [
        scattered(by_part(v), [[grad_tail if m == 0 else half_x], [half_x]])
        for m, v in enumerate(into)
    ]
    step_part = lax.dynamic_update_slice_in_dim(
        jnp.zeros((HEADS, width), F32), grad_tail[2 * STATE : 2 * STATE + heads], own * heads, 0
    )
    grad_tail = jnp.concatenate([grad_tail[: 2 * STATE], step_part], axis=0)
    grad_tail = jnp.stack(
        [lax.dynamic_slice_in_dim(grad_tail, (own ^ r) * rows, rows, 1) for r in range(parts)]
    )
    grad_tail = scattered(grad_tail, [[into[-1]], [half_x]])
    scattered_x = along.scatter(half_x)
    half_x = scattered_x
    gate_lines = chains[0].result()
    out_lines = chains[1].result()
    x_lines = along.gather(finish(half_x)[0])
    grad_tail = summed(grad_tail, "group", BF16, [x_lines])

    def placed(whole, lines, kind, side):
        lines = lines.transpose(1, 0, 2, 3).reshape(parts, inner // 2, rows).astype(F32)
        for f in range(parts):
            at = kind * INNER + f * inner + side * (inner // 2)
            whole = lax.dynamic_update_slice(whole, lines[f], (at, jnp.zeros_like(at)))
        return whole

    lane = lax.axis_index("group") & 1
    got_lines = across(gate_lines)
    got_out = across(out_lines)
    got_x = across(x_lines)
    whole = jnp.zeros((2 * INNER + 2 * STATE + HEADS, rows), F32)
    whole = placed(whole, gate_lines, 0, lane)
    whole = placed(whole, after(got_lines, x_lines), 0, 1 - lane)
    whole = placed(whole, x_lines, 1, lane)
    whole = lax.dynamic_update_slice_in_dim(whole, grad_tail, 2 * INNER, 0)
    grad_in = placed(whole, got_x, 1, 1 - lane).T
    grad_out = jnp.stack(
        [
            jnp.where(lane == 0, out_lines, got_out),
            jnp.where(lane == 0, got_out, out_lines),
        ]
    )
    grad_out = grad_out.reshape(inner, width).astype(F32)

    for m in range(micro):
        stat = lax.dynamic_slice_in_dim(
            out_grads[m][0][:, 0].reshape(seq), own * tok_count, tok_count, 0
        )
        scale = lax.rsqrt(stat * (1.0 / INNER) + EPSILON)[:, None]
        mixed[m] = (tok_rows[m] + mixed[m] * scale).astype(BF16)

    grad_tok = []
    grad_norm = jnp.zeros((width,), F32)
    for m in range(micro):
        part = into_sums[m]
        hat = tok_rows[m] * inverse[m]
        through = part * gain_norm
        here = inverse[m] * (through - hat * jnp.mean(hat * through, axis=-1, keepdims=True))
        grad_tok.append((cot_here[m].astype(F32) + here).astype(BF16))
        grad_norm += jnp.sum(part * hat, axis=0)

    grad_taps = sum(b[2] for b in backs)[: CONV + 1]
    grad_skip = sum(b[3] for b in backs)[0]
    grad_head = sum(b[4] for b in backs)
    grad_inner = sum(g[4] for g in out_grads)[0]
    taps_all = lax.dynamic_update_slice_in_dim(
        jnp.zeros((CONV + 1, XBC), F32), grad_taps[:, :inner], own * inner, 1
    )
    taps_all = taps_all.at[:, INNER:].set(grad_taps[:, inner:])
    joint = summed(jnp.concatenate([taps_all.reshape(-1), grad_norm]), "fsdp")
    skip_sum = jnp.sum(grad_skip.reshape(heads, HEADDIM), axis=1)
    joint = summed(
        jnp.concatenate([joint, grad_inner, grad_head[0, :heads], grad_head[1, :heads], skip_sum]),
        "group",
        pin=[x_lines],
    )
    at = (CONV + 1) * XBC
    share = XBC // parts
    taps_all = lax.dynamic_slice_in_dim(joint[:at].reshape(CONV + 1, XBC), own * share, share, 1)
    grad_norm = lax.dynamic_slice_in_dim(joint, at + own * rows, rows, 0)
    at += width
    grad_inner = joint[at : at + inner]
    at += inner
    grad_bias, grad_rate, grad_skip = (
        joint[at + k * heads : at + (k + 1) * heads] for k in range(3)
    )
    return (
        jnp.stack(mixed)[:, None],
        jnp.stack(grad_tok)[:, None],
        grad_norm,
        grad_in,
        taps_all[:CONV],
        taps_all[CONV],
        grad_bias,
        grad_rate,
        grad_skip,
        grad_inner,
        grad_out,
    )


def solution(mesh):
    rows = P(None, "group", "fsdp", None)
    shard = P("fsdp")
    in_specs = (rows, P(None, "group", "fsdp"), rows, shard, P("fsdp", None), P(None, "fsdp"))
    in_specs += (shard,) * 5 + (P("fsdp", None),)
    out_specs = (rows, rows, shard, P("fsdp", None), P(None, "fsdp")) + (shard,) * 5
    out_specs += (P("fsdp", None),)
    return jax.shard_map(
        on_device, mesh=mesh, in_specs=in_specs, out_specs=out_specs, check_vma=False
    )
```

time: 940 us -> 735 us (0.78)
  waiting for transfers between devices: 410 us -> 187 us
  Pallas kernels: 134 us -> 288 us
  matrix products: 129 us -> 0 us
  starting transfers between devices: 23.8 us -> 71.2 us
  other arithmetic: 99.9 us -> 78.5 us
  local copies, waits for them, and re-layouts: 109 us -> 89.5 us
  blocking collectives: 11.6 us -> 0 us
    unnamed x9 -> x4, waiting for transfers between devices: 166 us -> 0.07 us
    pallas_call x2 -> x17, Pallas kernels: 116 us -> 270 us  [the longest x13 168 us: call(): pl.pallas_call(kernel, grid_spec=pltpu.PrefetchScalarGridSpec(num_scalar_...]
    dot_general x10 -> x0, matrix products: 129 us -> none  [the longest x6 87.5 us: dot(): lax.dot_general(a, b, (contract, ((), ())), precision=precision, preferre...]
    ppermute x28 -> x57, waiting for transfers between devices: 201 us -> 140 us  [swap(): return lax.ppermute(value, axis, [(i, i ^ bit) for i in range(count)])]
    ppermute x0 -> x12, waiting for transfers between devices: none -> 44 us  [shifted(): return lax.ppermute(value, 'group', pairs)]
    all_gather x4 -> x1, waiting for transfers between devices: 42.7 us -> 2.38 us  [gather(): lax.all_gather(self.order(value), 'group', axis=0, axis_index_groups=line...]
    ppermute x0 -> x12, starting transfers between devices: none -> 37.3 us  [shifted(): return lax.ppermute(value, 'group', pairs)]
    dynamic_update_slice x1 -> x18, local copies, waits for them, and re-layouts: 0.01 us -> 12.8 us  [the longest x16 12.8 us: placed(): whole = lax.dynamic_update_slice(whole, lines[f], (at, jnp.zeros_like(at)))]
  transfers between devices with their start and end apart: 35 -> 73, of which waited for: 15 -> 30; matrix products, arithmetic and copies ran while one was open for 25% -> 18% of each run, Pallas kernels for 8% -> 36%
where the time goes in v2:
time: 735 us; the launch traced here: 730 us
  Pallas kernels  288 us (39%)
  waiting for transfers between devices  187 us (25%)
  local copies, waits for them, and re-layouts  89.5 us (12%)
  other arithmetic  78.5 us (11%)
  starting transfers between devices  71.2 us (10%)
  between operations  15.9 us (2%)
    pallas_call x13, Pallas kernels, call(): pl.pallas_call(kernel, grid_spec=pltpu.PrefetchScalarGridSpec(num_scalar_...  168 us
    ppermute x57, waiting for transfers between devices, swap(): return lax.ppermute(value, axis, [(i, i ^ bit) for i in range(count)])  140 us
    pallas_call x2, Pallas kernels, scan_back(): backward(own_arg, act, slope, pre, tail, dt_raw, after(out_grads[m][1], *...  63 us
    ppermute x12, waiting for transfers between devices, shifted(): return lax.ppermute(value, 'group', pairs)  44 us
    pallas_call x2, Pallas kernels, on_device(): forward(own_arg, pre, tail, gate, dt_raw, back, seg_rows[m], taps, head_r...  38.5 us
    ppermute x12, starting transfers between devices, shifted(): return lax.ppermute(value, 'group', pairs)  37.3 us
    ppermute x57, starting transfers between devices, swap(): return lax.ppermute(value, axis, [(i, i ^ bit) for i in range(count)])  33.8 us
    unnamed x212, local copies, waits for them, and re-layouts  32.2 us
  transfers between devices with their start and end apart: 73, of which 30 were waited for; matrix products, arithmetic and copies ran while one was open for 18% of the time, Pallas kernels for 36%

profile of v2, /device:TPU:0, one launch (start us, length us, event | category | flops | bytes accessed | tf_op | source)
XLA Modules:
  0.0 729.9 jit_solution(10555982431211911089)
XLA Ops:
  19.1 16.4 %collective-permute-done.3 = f32[6464]{0:T(1024)S(1)} collective-permute-done((f32[6464]{0:T(1024)S(1)}, f32[6464]{0:T(1024)S(1)}, u32[]{:S(2)}, u32[]{:S(2)}) %collective-permute-start.3) | collective-permute-done | bytes 25888 | tf_op jit(solution)/shard_map/ppermute | solution.py:27
  43.5 20.9 %collective-permute-done.9 = bf16[2,512,512]{2,1,0:T(8,128)(2,1)} collective-permute-done((bf16[2,512,512]{2,1,0:T(8,128)(2,1)}, bf16[2,512,512]{2,1,0:T(8,128)(2,1)}, u32[]{:S(2)}, u32[]{:S(2)}) %collective-permute-start.9) | collective-permute-done | bytes 1048608 | tf_op jit(solution)/shard_map/ppermute | solution.py:27
  106.3 21.3 %shard_map.203 = (bf16[1024,2048]{1,0:T(8,128)(2,1)}, f32[1024,1024]{1,0:T(8,128)}, bf16[1024,1024]{1,0:T(8,128)(2,1)}, bf16[1024,256]{1,0:T(8,128)(2,1)S(1)}, f32[1024,128]{1,0:T(8,128)S(1)}) custom-call(s32[2]{0:T(128)S(1)} %pad_add_fusion.own_ref, bf16[256,2048]{1,0:T(8,128)(2,1)S(1)} %get-tuple-element.146.refs_0_, ...), custom_call_target="tpu_custom_call" | custom-call | flops 1 | bytes 1 | tf_op jit(solution)/shard_map/pallas_call | solution.py:665
  127.7 21.5 %shard_map.204 = (bf16[1024,2048]{1,0:T(8,128)(2,1)}, f32[1024,1024]{1,0:T(8,128)}, bf16[1024,1024]{1,0:T(8,128)(2,1)}, bf16[1024,256]{1,0:T(8,128)(2,1)S(1)}, f32[1024,128]{1,0:T(8,128)S(1)}) custom-call(s32[2]{0:T(128)S(1)} %pad_add_fusion.own_ref, bf16[256,2048]{1,0:T(8,128)(2,1)S(1)} %get-tuple-element.164.refs_0_, ...), custom_call_target="tpu_custom_call" | custom-call | flops 1 | bytes 1 | tf_op jit(solution)/shard_map/pallas_call | solution.py:665
  153.4 9.1 %shard_map.205 = (bf16[1024,2048]{1,0:T(8,128)(2,1)}, bf16[1024,1024]{1,0:T(8,128)(2,1)}) custom-call(s32[2]{0:T(128)S(1)} %pad_add_fusion.own_ref, bf16[256,2048]{1,0:T(8,128)(2,1)S(1)} %get-tuple-element.170.refs_0_, bf16[256,2048]{1,0:T(8,128)(2,1)S(1)} %collective-permute-done.19.refs_1_, bf16[256,2048]{1,0:T(8,128)(2,1)S(1)} %collective-permute-done.20.refs_2_, ...), custom_call_target="tpu_custom_call" | custom-call | flops 1 | bytes 1 | tf_op jit(solution)/shard_map/pallas_call | solution.py:665
  162.5 19.3 %shard_map.206 = (bf16[1024,1280]{1,0:T(8,128)(2,1)}, bf16[1024,1280]{1,0:T(8,128)(2,1)}, f32[1024,1024]{1,0:T(8,128)}, bf16[1024,1024]{1,0:T(8,128)(2,1)S(1)}, ...) custom-call(s32[2]{0:T(128)S(1)} %pad_add_fusion.own_ref, bf16[1024,1024]{1,0:T(8,128)(2,1)} %get-tuple-element.157.pre_ref, ...), custom_call_target="tpu_custom_call" | custom-call | flops 1 | bytes 1 | tf_op jit(solution)/shard_map/pallas_call | solution.py:1007
  188.6 9.2 %shard_map.208 = (bf16[1024,2048]{1,0:T(8,128)(2,1)}, bf16[1024,1024]{1,0:T(8,128)(2,1)}) custom-call(s32[2]{0:T(128)S(1)} %pad_add_fusion.own_ref, bf16[256,2048]{1,0:T(8,128)(2,1)S(1)} %get-tuple-element.186.refs_0_, bf16[256,2048]{1,0:T(8,128)(2,1)S(1)} %collective-permute-done.24.refs_1_, bf16[256,2048]{1,0:T(8,128)(2,1)S(1)} %collective-permute-done.25.refs_2_, ...), custom_call_target="tpu_custom_call" | custom-call | flops 1 | bytes 1 | tf_op jit(solution)/shard_map/pallas_call | solution.py:665
  197.9 19.2 %shard_map.209 = (bf16[1024,1280]{1,0:T(8,128)(2,1)}, bf16[1024,1280]{1,0:T(8,128)(2,1)}, f32[1024,1024]{1,0:T(8,128)}, bf16[1024,1024]{1,0:T(8,128)(2,1)S(1)}, ...) custom-call(s32[2]{0:T(128)S(1)} %pad_add_fusion.own_ref, bf16[1024,1024]{1,0:T(8,128)(2,1)} %get-tuple-element.181.pre_ref, ...), custom_call_target="tpu_custom_call" | custom-call | flops 1 | bytes 1 | tf_op jit(solution)/shard_map/pallas_call | solution.py:1007
  223.6 9.3 %shard_map.207 = (bf16[1024,1024]{1,0:T(8,128)(2,1)S(1)}, bf16[1024,1024]{1,0:T(8,128)(2,1)S(1)}, bf16[1024,1024]{1,0:T(8,128)(2,1)}, f32[8,1024]{1,0:T(8,128)S(1)}) custom-call(s32[2]{0:T(128)S(1)} %pad_add_fusion.own_ref, f32[1024,1024]{1,0:T(8,128)} %get-tuple-element.176.out_ref, f32[1024,1024]{1,0:T(8,128)} %get-tuple-element.159.gate_ref, ...), custom_call_target="tpu_custom_call" | custom-call | flops 1 | bytes 1 | tf_op jit(solution)/shard_map/pallas_call | solution.py:1016
  234.3 9.3 %shard_map.210 = (bf16[1024,1024]{1,0:T(8,128)(2,1)S(1)}, bf16[1024,1024]{1,0:T(8,128)(2,1)S(1)}, bf16[1024,1024]{1,0:T(8,128)(2,1)}, f32[8,1024]{1,0:T(8,128)S(1)}) custom-call(s32[2]{0:T(128)S(1)} %pad_add_fusion.own_ref, f32[1024,1024]{1,0:T(8,128)} %get-tuple-element.189.out_ref, f32[1024,1024]{1,0:T(8,128)} %get-tuple-element.183.gate_ref, ...), custom_call_target="tpu_custom_call" | custom-call | flops 1 | bytes 1 | tf_op jit(solution)/shard_map/pallas_call | solution.py:1016
  246.3 14.3 %shard_map.211 = (bf16[512,2048]{1,0:T(8,128)(2,1)S(1)}, bf16[512,2048]{1,0:T(8,128)(2,1)S(1)}) custom-call(s32[2]{0:T(128)S(1)} %pad_add_fusion.own_ref, bf16[1024,1024]{1,0:T(8,128)(2,1)} %copy-done.7, bf16[1024,1024]{1,0:T(8,128)(2,1)} %copy-done.5, bf16[1024,2048]{1,0:T(8,128)(2,1)} %get-tuple-element.224.refs_2_, ...), custom_call_target="tpu_custom_call" | custom-call | flops 1 | bytes 1 | tf_op jit(solution)/shard_map/pallas_call | solution.py:665
  261.3 15.4 %shard_map.212 = (bf16[512,2048]{1,0:T(8,128)(2,1)}, bf16[512,2048]{1,0:T(8,128)(2,1)S(1)}) custom-call(s32[2]{0:T(128)S(1)} %pad_add_fusion.own_ref, bf16[1024,1024]{1,0:T(8,128)(2,1)} %get-tuple-element.193.refs_0_, bf16[1024,1024]{1,0:T(8,128)(2,1)} %get-tuple-element.195.refs_1_, bf16[1024,2048]{1,0:T(8,128)(2,1)} %get-tuple-element.196.refs_2_, ...), custom_call_target="tpu_custom_call" | custom-call | flops 1 | bytes 1 | tf_op jit(solution)/shard_map/pallas_call | solution.py:665
  277.9 31.4 %shard_map.213 = (bf16[1024,1280]{1,0:T(8,128)(2,1)}, bf16[1024,128]{1,0:T(8,128)(2,1)S(1)}, f32[8,1280]{1,0:T(8,128)S(1)}, f32[8,1024]{1,0:T(8,128)S(1)}, f32[8,128]{1,0:T(8,128)S(1)}) custom-call(s32[2]{0:T(128)S(1)} %pad_add_fusion.own_ref, bf16[1024,1280]{1,0:T(8,128)(2,1)} %get-tuple-element.174.act_ref, ...), custom_call_target="tpu_custom_call" | custom-call | flops 1 | bytes 1 | tf_op jit(solution)/shard_map/pallas_call | solution.py:1020
  309.4 8.7 %shard_map.214 = bf16[1024,2048]{1,0:T(8,128)(2,1)} custom-call(s32[2]{0:T(128)S(1)} %pad_add_fusion.own_ref, bf16[1024,1024]{1,0:T(8,128)(2,1)S(1)} %copy-done.24, bf16[1024,2048]{1,0:T(8,128)(2,1)} %b_ref.3), custom_call_target="tpu_custom_call" | custom-call | flops 1 | bytes 1 | tf_op jit(solution)/shard_map/pallas_call | solution.py:665
  335.7 31.6 %shard_map.215 = (bf16[1024,1280]{1,0:T(8,128)(2,1)}, bf16[1024,128]{1,0:T(8,128)(2,1)S(1)}, f32[8,1280]{1,0:T(8,128)S(1)}, f32[8,1024]{1,0:T(8,128)S(1)}, f32[8,128]{1,0:T(8,128)S(1)}) custom-call(s32[2]{0:T(128)S(1)} %pad_add_fusion.own_ref, bf16[1024,1280]{1,0:T(8,128)(2,1)} %get-tuple-element.203.act_ref, ...), custom_call_target="tpu_custom_call" | custom-call | flops 1 | bytes 1 | tf_op jit(solution)/shard_map/pallas_call | solution.py:1020
  367.3 8.7 %shard_map.216 = bf16[1024,2048]{1,0:T(8,128)(2,1)} custom-call(s32[2]{0:T(128)S(1)} %pad_add_fusion.own_ref, bf16[1024,1024]{1,0:T(8,128)(2,1)S(1)} %copy-done.22, bf16[1024,2048]{1,0:T(8,128)(2,1)} %b_ref.3), custom_call_target="tpu_custom_call" | custom-call | flops 1 | bytes 1 | tf_op jit(solution)/shard_map/pallas_call | solution.py:665
  393.4 15.8 %shard_map.217 = (bf16[512,2048]{1,0:T(8,128)(2,1)}, bf16[512,2048]{1,0:T(8,128)(2,1)S(1)}) custom-call(s32[2]{0:T(128)S(1)} %pad_add_fusion.own_ref, bf16[1024,1280]{1,0:T(8,128)(2,1)} %get-tuple-element.216.refs_0_.pre_ref, bf16[1024,1280]{1,0:T(8,128)(2,1)} %get-tuple-element.217.refs_1_.pre_ref, bf16[1024,2048]{1,0:T(8,128)(2,1)} %get-tuple-element.224.refs_2_, ...), custom_call_target="tpu_custom_call" | custom-call | flops 1 | bytes 1 | tf_op jit(solution)/shard_map/pallas_call | solution.py:665
  414.5 16.4 %shard_map.218 = bf16[1024,2048]{1,0:T(8,128)(2,1)} custom-call(s32[2]{0:T(128)S(1)} %pad_add_fusion.own_ref, bf16[1024,1024]{1,0:T(8,128)(2,1)S(1)} %copy-done.8, bf16[1024,1280]{1,0:T(8,128)(2,1)} %get-tuple-element.216.refs_0_.pre_ref, bf16[1024,128]{1,0:T(8,128)(2,1)S(1)} %copy-done.26, bf16[4,512,512]{2,1,0:T(8,128)(2,1)S(1)} %bitcast.366, ...), custom_call_target="tpu_custom_call" | custom-call | flops 1 | bytes 1 | tf_op jit(solution)/shard_map/pallas_call | solution.py:665
  467.9 16.6 %shard_map.221 = bf16[1024,2048]{1,0:T(8,128)(2,1)} custom-call(s32[2]{0:T(128)S(1)} %pad_add_fusion.own_ref, bf16[1024,1024]{1,0:T(8,128)(2,1)S(1)} %copy-done.6, bf16[1024,1280]{1,0:T(8,128)(2,1)} %get-tuple-element.217.refs_1_.pre_ref, bf16[1024,128]{1,0:T(8,128)(2,1)S(1)} %copy-done.29, bf16[4,512,512]{2,1,0:T(8,128)(2,1)S(1)} %bitcast.367, ...), custom_call_target="tpu_custom_call" | custom-call | flops 1 | bytes 1 | tf_op jit(solution)/shard_map/pallas_call | solution.py:665
  504.0 24.1 %collective-permute-done.51 = bf16[4,128,512]{2,1,0:T(8,128)(2,1)S(1)} collective-permute-done((bf16[4,128,512]{2,1,0:T(8,128)(2,1)}, bf16[4,128,512]{2,1,0:T(8,128)(2,1)S(1)}, u32[]{:S(2)}, u32[]{:S(2)}) %collective-permute-start.51) | collective-permute-done | bytes 524320 | tf_op jit(solution)/shard_map/ppermute | solution.py:187
  542.6 14.0 %collective-permute-done.52 = bf16[4,128,512]{2,1,0:T(8,128)(2,1)S(1)} collective-permute-done((bf16[4,128,512]{2,1,0:T(8,128)(2,1)S(1)}, bf16[4,128,512]{2,1,0:T(8,128)(2,1)S(1)}, u32[]{:S(2)}, u32[]{:S(2)}) %collective-permute-start.52) | collective-permute-done | bytes 524320 | tf_op jit(solution)/shard_map/ppermute | solution.py:187
  592.3 18.3 %collective-permute-done.43 = bf16[1,256,2048]{2,1,0:T(8,128)(2,1)S(1)} collective-permute-done((bf16[1,256,2048]{2,1,0:T(8,128)(2,1)S(1)}, bf16[1,256,2048]{2,1,0:T(8,128)(2,1)S(1)}, u32[]{:S(2)}, u32[]{:S(2)}) %collective-permute-start.43) | collective-permute-done | bytes 1048608 | tf_op jit(solution)/shard_map/ppermute | solution.py:27
  636.8 22.4 %collective-permute-done.68 = bf16[4,128,2048]{2,1,0:T(8,128)(2,1)} collective-permute-done((bf16[4,128,2048]{2,1,0:T(8,128)(2,1)}, bf16[4,128,2048]{2,1,0:T(8,128)(2,1)}, u32[]{:S(2)}, u32[]{:S(2)}) %collective-permute-start.68) | collective-permute-done | bytes 2097184 | tf_op jit(solution)/shard_map/ppermute | solution.py:27
  698.6 11.3 %collective-permute-done.60 = bf16[320,512]{1,0:T(8,128)(2,1)S(1)} collective-permute-done((bf16[320,512]{1,0:T(8,128)(2,1)S(1)}, bf16[320,512]{1,0:T(8,128)(2,1)S(1)}, u32[]{:S(2)}, u32[]{:S(2)}) %collective-permute-start.60) | collective-permute-done | bytes 327712 | tf_op jit(solution)/shard_map/ppermute | solution.py:27
  (534 shorter events, 309.3 us)
Async XLA Ops:
  7.2 377.3 %reduce-scatter.4.cloned.1.call-start = ((), (), s32[]{:S(2)}) async-start(), calls=%async_computation.3 | async-start | bytes 2621440 | tf_op jit(solution)/shard_map/reduce_scatter | solution.py:166
  43.4 41.8 %collective-permute-start.5 = (bf16[4,512,512]{2,1,0:T(8,128)(2,1)}, bf16[4,512,512]{2,1,0:T(8,128)(2,1)S(1)}, u32[]{:S(2)}, u32[]{:S(2)}) collective-permute-start(bf16[4,512,512]{2,1,0:T(8,128)(2,1)} %bitcast.407), channel_id=1, source_target_pairs={{0,1},{1,0},{2,3},{3,2},{4,5},{5,4},{6,7},{7,6},{8,9},{9,8},{10,11... | collective-permute-start | bytes 6291464 | tf_op jit(solution)/shard_map/ppermute | solution.py:27
  101.1 48.1 %collective-permute-start.20 = (bf16[256,2048]{1,0:T(8,128)(2,1)S(1)}, bf16[256,2048]{1,0:T(8,128)(2,1)S(1)}, u32[]{:S(2)}, u32[]{:S(2)}) collective-permute-start(bf16[256,2048]{1,0:T(8,128)(2,1)S(1)} %get-tuple-element.170.refs_0_), channel_id=1, source_target_pairs={{0,2},{1,3},{2,0},{3,1},{4,6},{5,7},{6,4},{7,5},{8,10},{9,11},{10,... | collective-permute-start | bytes 3145736 | tf_op jit(solution)/shard_map/ppermute | solution.py:27
  149.8 34.7 %collective-permute-start.25 = (bf16[256,2048]{1,0:T(8,128)(2,1)S(1)}, bf16[256,2048]{1,0:T(8,128)(2,1)S(1)}, u32[]{:S(2)}, u32[]{:S(2)}) collective-permute-start(bf16[256,2048]{1,0:T(8,128)(2,1)S(1)} %get-tuple-element.186.refs_0_), channel_id=1, source_target_pairs={{0,2},{1,3},{2,0},{3,1},{4,6},{5,7},{6,4},{7,5},{8,10},{9,11},{10,... | collective-permute-start | bytes 3145736 | tf_op jit(solution)/shard_map/ppermute | solution.py:27
  185.0 34.9 %collective-permute-start.22 = (f32[8,2,128]{2,1,0:T(2,128)S(1)}, f32[8,2,128]{2,1,0:T(2,128)S(1)}, u32[]{:S(2)}, u32[]{:S(2)}) collective-permute-start(f32[8,2,128]{2,1,0:T(2,128)S(1)} %slice.324), channel_id=1, source_target_pairs={{0,1},{1,0},{2,3},{3,2},{4,5},{5,4},{6,7},{7,6},{8,9},{9,8},{10,11... | collective-permute-start | bytes 24584 | tf_op jit(solution)/shard_map/ppermute | solution.py:27
  260.7 57.5 %collective-permute-start.30 = (bf16[512,2048]{1,0:T(8,128)(2,1)S(1)}, bf16[512,2048]{1,0:T(8,128)(2,1)}, u32[]{:S(2)}, u32[]{:S(2)}) collective-permute-start(bf16[512,2048]{1,0:T(8,128)(2,1)S(1)} %get-tuple-element.206), channel_id=1, source_target_pairs={{0,4},{4,0},{8,12},{12,8},{16,20},{20,16},{24,28},{28,24},{1,5},{5... | collective-permute-start | bytes 6291464 | tf_op jit(solution)/shard_map/ppermute | solution.py:27
  322.0 125.7 %reduce-scatter.6.cloned.1.call-start = ((), (), s32[]{:S(2)}) async-start(), calls=%async_computation.4 | async-start | bytes 2621440 | tf_op jit(solution)/shard_map/reduce_scatter | solution.py:166
  325.4 54.2 %collective-permute-start.29 = (bf16[2,256,2048]{2,1,0:T(8,128)(2,1)}, bf16[2,256,2048]{2,1,0:T(8,128)(2,1)}, u32[]{:S(2)}, u32[]{:S(2)}) collective-permute-start(bf16[2,256,2048]{2,1,0:T(8,128)(2,1)} %slice_bitcast_fusion.10), channel_id=1, source_target_pairs={{0,1},{1,0},{2,3},{3,2},{4,5},{5,4},{6,7},{7,6},{8,9},{9,8},{10,11... | collective-permute-start | bytes 6291464 | tf_op jit(solution)/shard_map/ppermute | solution.py:27
  325.9 58.6 %collective-permute-start.32 = (bf16[512,2048]{1,0:T(8,128)(2,1)}, bf16[512,2048]{1,0:T(8,128)(2,1)}, u32[]{:S(2)}, u32[]{:S(2)}) collective-permute-start(bf16[512,2048]{1,0:T(8,128)(2,1)} %get-tuple-element.212), channel_id=1, source_target_pairs={{0,4},{4,0},{8,12},{12,8},{16,20},{20,16},{24,28},{28,24},{1,5},{5... | collective-permute-start | bytes 6291464 | tf_op jit(solution)/shard_map/ppermute | solution.py:27
  383.1 54.2 %collective-permute-start.31 = (bf16[1,256,2048]{2,1,0:T(8,128)(2,1)}, bf16[1,256,2048]{2,1,0:T(8,128)(2,1)}, u32[]{:S(2)}, u32[]{:S(2)}) collective-permute-start(bf16[1,256,2048]{2,1,0:T(8,128)(2,1)} %fusion.30), channel_id=1, source_target_pairs={{0,2},{1,3},{2,0},{3,1},{4,6},{5,7},{6,4},{7,5},{8,10},{9,11},{10,... | collective-permute-start | bytes 3145736 | tf_op jit(solution)/shard_map/ppermute | solution.py:27
  388.9 221.7 %reduce-scatter.8.cloned.1.call-start = ((), (), s32[]{:S(2)}) async-start(), calls=%async_computation.5 | async-start | bytes 2621440 | tf_op jit(solution)/shard_map/reduce_scatter | solution.py:166
  409.2 75.2 %collective-permute-start.39 = (bf16[512,2048]{1,0:T(8,128)(2,1)}, bf16[512,2048]{1,0:T(8,128)(2,1)}, u32[]{:S(2)}, u32[]{:S(2)}) collective-permute-start(bf16[512,2048]{1,0:T(8,128)(2,1)} %get-tuple-element.229), channel_id=1, source_target_pairs={{0,4},{4,0},{8,12},{12,8},{16,20},{20,16},{24,28},{28,24},{1,5},{5... | collective-permute-start | bytes 6291464 | tf_op jit(solution)/shard_map/ppermute | solution.py:27
  434.2 50.2 %collective-permute-start.37 = (bf16[2,256,2048]{2,1,0:T(8,128)(2,1)}, bf16[2,256,2048]{2,1,0:T(8,128)(2,1)}, u32[]{:S(2)}, u32[]{:S(2)}) collective-permute-start(bf16[2,256,2048]{2,1,0:T(8,128)(2,1)} %slice_bitcast_fusion.4), channel_id=1, source_target_pairs={{0,1},{1,0},{2,3},{3,2},{4,5},{5,4},{6,7},{7,6},{8,9},{9,8},{10,11... | collective-permute-start | bytes 6291464 | tf_op jit(solution)/shard_map/ppermute | solution.py:27
  437.0 59.0 %collective-permute-start.34 = (bf16[1,256,2048]{2,1,0:T(8,128)(2,1)}, bf16[1,256,2048]{2,1,0:T(8,128)(2,1)}, u32[]{:S(2)}, u32[]{:S(2)}) collective-permute-start(bf16[1,256,2048]{2,1,0:T(8,128)(2,1)} %fusion.31), channel_id=1, source_target_pairs={{0,2},{1,3},{2,0},{3,1},{4,6},{5,7},{6,4},{7,5},{8,10},{9,11},{10,... | collective-permute-start | bytes 3145736 | tf_op jit(solution)/shard_map/ppermute | solution.py:27
  460.6 73.1 %collective-permute-start.62 = (bf16[128,2048]{1,0:T(8,128)(2,1)}, bf16[128,2048]{1,0:T(8,128)(2,1)}, u32[]{:S(2)}, u32[]{:S(2)}) collective-permute-start(bf16[128,2048]{1,0:T(8,128)(2,1)} %bitcast.58), channel_id=1, source_target_pairs={{8,0},{12,4},{16,8},{20,12},{24,16},{28,20},{9,1},{13,5},{17,9},{2... | collective-permute-start | bytes 1572872 | tf_op jit(solution)/shard_map/ppermute | solution.py:187
  461.9 71.8 %collective-permute-start.65 = (bf16[128,2048]{1,0:T(8,128)(2,1)}, bf16[128,2048]{1,0:T(8,128)(2,1)}, u32[]{:S(2)}, u32[]{:S(2)}) collective-permute-start(bf16[128,2048]{1,0:T(8,128)(2,1)} %bitcast.58), channel_id=1, source_target_pairs={{0,8},{4,12},{8,16},{12,20},{16,24},{20,28},{1,9},{5,13},{9,17},{1... | collective-permute-start | bytes 1572872 | tf_op jit(solution)/shard_map/ppermute | solution.py:187
  486.7 42.7 %collective-permute-start.56 = (bf16[2,320,512]{2,1,0:T(8,128)(2,1)S(1)}, bf16[2,320,512]{2,1,0:T(8,128)(2,1)S(1)}, u32[]{:S(2)}, u32[]{:S(2)}) collective-permute-start(bf16[2,320,512]{2,1,0:T(8,128)(2,1)S(1)} %fusion.34), channel_id=1, source_target_pairs={{0,1},{1,0},{2,3},{3,2},{4,5},{5,4},{6,7},{7,6},{8,9},{9,8},{10,11... | collective-permute-start | bytes 1966088 | tf_op jit(solution)/shard_map/ppermute | solution.py:27
  496.1 172.5 %all-gather.3.cloned.1.call-start = ((), (), s32[]{:S(2)}) async-start(), calls=%async_computation.6 | async-start | bytes 2621440 | tf_op jit(solution)/shard_map/all_gather | solution.py:172
  497.7 33.9 %collective-permute-start.53 = (bf16[4,128,512]{2,1,0:T(8,128)(2,1)}, bf16[4,128,512]{2,1,0:T(8,128)(2,1)S(1)}, u32[]{:S(2)}, u32[]{:S(2)}) collective-permute-start(bf16[4,128,512]{2,1,0:T(8,128)(2,1)} %collective-permute-done.40), channel_id=1, source_target_pairs={{0,8},{4,12},{8,16},{12,20},{16,24},{20,28},{1,9},{5,13},{9,17},{1... | collective-permute-start | bytes 1572872 | tf_op jit(solution)/shard_map/ppermute | solution.py:187
  533.7 52.8 %collective-permute-start.42 = (bf16[2,256,2048]{2,1,0:T(8,128)(2,1)S(1)}, bf16[2,256,2048]{2,1,0:T(8,128)(2,1)S(1)}, u32[]{:S(2)}, u32[]{:S(2)}) collective-permute-start(bf16[2,256,2048]{2,1,0:T(8,128)(2,1)S(1)} %slice_bitcast_fusion.1), channel_id=1, source_target_pairs={{0,1},{1,0},{2,3},{3,2},{4,5},{5,4},{6,7},{7,6},{8,9},{9,8},{10,11... | collective-permute-start | bytes 6291464 | tf_op jit(solution)/shard_map/ppermute | solution.py:27
  563.2 112.7 %collective-permute-start.58 = (bf16[320,512]{1,0:T(8,128)(2,1)}, bf16[320,512]{1,0:T(8,128)(2,1)}, u32[]{:S(2)}, u32[]{:S(2)}) collective-permute-start(bf16[320,512]{1,0:T(8,128)(2,1)} %fusion.50), channel_id=1, source_target_pairs={{0,4},{4,0},{8,12},{12,8},{16,20},{20,16},{24,28},{28,24},{1,5},{5... | collective-permute-start | bytes 983048 | tf_op jit(solution)/shard_map/ppermute | solution.py:27
  565.9 107.3 %collective-permute-start.55 = (bf16[4,4,128,512]{3,2,1,0:T(8,128)(2,1)}, bf16[4,4,128,512]{3,2,1,0:T(8,128)(2,1)}, u32[]{:S(2)}, u32[]{:S(2)}) collective-permute-start(bf16[4,4,128,512]{3,2,1,0:T(8,128)(2,1)} %get-tuple-element.339), channel_id=1, source_target_pairs={{0,4},{4,0},{8,12},{12,8},{16,20},{20,16},{24,28},{28,24},{1,5},{5... | collective-permute-start | bytes 6291464 | tf_op jit(solution)/shard_map/ppermute | solution.py:27
  591.7 67.5 %collective-permute-start.68 = (bf16[4,128,2048]{2,1,0:T(8,128)(2,1)}, bf16[4,128,2048]{2,1,0:T(8,128)(2,1)}, u32[]{:S(2)}, u32[]{:S(2)}) collective-permute-start(bf16[4,128,2048]{2,1,0:T(8,128)(2,1)} %pad_maximum_fusion.7), channel_id=1, source_target_pairs={{0,4},{4,0},{8,12},{12,8},{16,20},{20,16},{24,28},{28,24},{1,5},{5... | collective-permute-start | bytes 6291464 | tf_op jit(solution)/shard_map/ppermute | solution.py:27
  668.5 47.7 %collective-permute-start.61 = (bf16[4,4,128,512]{3,2,1,0:T(8,128)(2,1)}, bf16[4,4,128,512]{3,2,1,0:T(8,128)(2,1)}, u32[]{:S(2)}, u32[]{:S(2)}) collective-permute-start(bf16[4,4,128,512]{3,2,1,0:T(8,128)(2,1)} %bitcast.405), channel_id=1, source_target_pairs={{0,4},{4,0},{8,12},{12,8},{16,20},{20,16},{24,28},{28,24},{1,5},{5... | collective-permute-start | bytes 6291464 | tf_op jit(solution)/shard_map/ppermute | solution.py:27
  (150 other events, 1938.0 us)
Sparse Core Ops, SparseCore 0:
  322.1 43.1 reduce-scatter.3
  389.0 42.2 reduce-scatter.5
  496.2 67.7 reduce-scatter.7
  621.4 47.1 all-gather.2

commit v3 on v2

--- a/solution.py
+++ b/solution.py
@@ -24,7 +24,8 @@
 
 def swap(value, axis, bit):
     count = lax.axis_size(axis)
-    return lax.ppermute(value, axis, [(i, i ^ bit) for i in range(count)])
+    with jax.named_scope(f"{axis}_{bit}"):
+        return lax.ppermute(value, axis, [(i, i ^ bit) for i in range(count)])
 
 
 def after(value, *earlier):
@@ -64,13 +65,12 @@
     return permuted(parts, lax.axis_index("fsdp"))
 
 
-def traded(blocks, send, arrived):
+def traded(blocks, send):
     held = {r: {0: block} for r, block in enumerate(blocks)}
     for bit in bits_of(len(blocks)):
         going = [r for r in sorted(held) if r & bit]
         sources = sorted(held[going[0]])
         got = send(jnp.stack([held[r][s] for r in going for s in sources]), bit)
-        arrived.append(got)
         place = 0
         for r in going:
             for s in sources:
@@ -130,23 +130,19 @@
     return [piece(0, s) for s in range(parts)]
 
 
-def scattered(value, pins):
+def scattered(value):
     bit = 1
     while value.shape[0] > 1:
         pairs = value.reshape((value.shape[0] // 2, 2) + value.shape[1:])
         got = swap(pairs[:, 1].astype(BF16), "fsdp", bit)
-        got = after(got, *(pins[0] if pins else ()))
-        pins = pins[1:]
         value = pairs[:, 0].astype(F32) + got.astype(F32)
         bit *= 2
     return value[0]
 
 
-def summed(value, axis, kind=F32, pin=()):
-    bits = bits_of(lax.axis_size(axis))[::-1]
-    for bit in bits:
-        got = swap(value.astype(kind), axis, bit)
-        value = value + after(got, *(pin if bit == bits[0] else ())).astype(F32)
+def summed(value, axis, kind=F32):
+    for bit in bits_of(lax.axis_size(axis))[::-1]:
+        value = value + swap(value.astype(kind), axis, bit).astype(F32)
     return value
 
 
@@ -162,48 +158,17 @@
     def order(self, value):
         return value if self.last is None else after(value, self.last)
 
-    def scatter(self, value):
+    def scatter(self, value, among=None):
         self.last = lax.psum_scatter(
-            self.order(value), "group", scatter_dimension=0, axis_index_groups=lines()
+            self.order(value), "group", scatter_dimension=0, axis_index_groups=among
         )
         return self.last
 
-    def gather(self, value):
+    def gather(self, value, among=None):
         self.last = lax.all_gather(
-            self.order(value), "group", axis=0, axis_index_groups=lines()
+            self.order(value), "group", axis=0, axis_index_groups=among
         )
         return self.last
-
-
-class Chain:
-    def __init__(self, part):
-        self.count = lax.axis_size("group") // 2
-        self.own = part
-        self.up = []
-        self.down = []
-
-    def shifted(self, value, by):
-        pairs = [(i, i + 2 * by) for i in range(2 * self.count) if 0 <= i + 2 * by < 2 * self.count]
-        return lax.ppermute(value, "group", pairs)
-
-    def step(self, *earlier):
-        up, down = (self.up[-1], self.down[-1]) if self.up else (self.own, self.own)
-        self.up.append(self.shifted(after(up, *earlier), 1))
-        self.down.append(self.shifted(after(down, *earlier), -1))
-        return self.up[-1], self.down[-1]
-
-    def result(self):
-        while len(self.up) < self.count - 1:
-            self.step()
-        place = lax.axis_index("group") // 2
-        every = jnp.stack(self.down[::-1] + [self.own] + self.up)
-        middle = self.count - 1
-        return jnp.stack(
-            [
-                lax.dynamic_index_in_dim(every, middle + place - i, 0, keepdims=False)
-                for i in range(self.count)
-            ]
-        )
 
 
 def dot(a, b, contract=((1,), (0,)), precision=None):
@@ -337,48 +302,6 @@
     stat_ref[0:1, :] = jnp.sum(squares.T, axis=0, keepdims=True)
     stat_ref[1:2, :] = jnp.sum(products.T, axis=0, keepdims=True)
     stat_ref[2:8, :] = jnp.zeros((6, chunk), F32)
-
-
-def gate_kernel(
-    chunk,
-    own_ref,
-    out_ref,
-    gate_ref,
-    back_ref,
-    stat_ref,
-    gain_ref,
-    grad_ssm_ref,
-    grad_gate_ref,
-    gated_ref,
-    grad_gain_ref,
-):
-    inner = gate_ref.shape[1]
-
-    @pl.when(pl.program_id(0) == 0)
-    def _():
-        grad_gain_ref[...] = jnp.zeros_like(grad_gain_ref)
-
-    scale = lax.rsqrt(stat_ref[0:1, :] * (1.0 / INNER) + EPSILON)
-    shift = scale * scale * scale * stat_ref[1:2, :] * (1.0 / INNER)
-    scale = columns(scale, chunk)
-    shift = columns(shift, chunk)
-    for at in range(0, inner, LANES):
-        lanes = slice(at, at + LANES)
-        ssm = out_ref[:, lanes]
-        gate = gate_ref[:, lanes]
-        back = back_ref[:, lanes].astype(F32)
-        sig = jax.nn.sigmoid(gate)
-        silu = gate * sig
-        gated = ssm * silu
-        scaled = gated * scale
-        gain = gain_ref[:, lanes]
-        grad_gated = scale * (gain * back) - gated * shift
-        grad_ssm_ref[:, lanes] = (grad_gated * silu).astype(BF16)
-        grad_gate_ref[:, lanes] = (
-            grad_gated * ssm * (sig * (1.0 + gate * (1.0 - sig)))
-        ).astype(BF16)
-        gated_ref[:, lanes] = (scaled * gain).astype(BF16)
-        grad_gain_ref[0:1, lanes] += jnp.sum(scaled * back, axis=0, keepdims=True)
 
 
 def backward_kernel(
@@ -620,13 +543,6 @@
             pltpu.VMEM((chunk, inner), BF16),
         ],
     )
-    gating = scan(
-        gate_kernel,
-        [tok(inner), tok(inner), tok(inner), row, const(1, inner)],
-        [tok(inner), tok(inner), tok(inner), const(8, inner)],
-        [struct((tokens, inner), BF16)] * 3 + [struct((8, inner), F32)],
-        [],
-    )
     tok, row, states, const = blocks(True)
     backward = scan(
         backward_kernel,
@@ -652,7 +568,7 @@
             pltpu.VMEM((chunk, inner), BF16),
         ],
     )
-    return forward, gating, backward
+    return forward, backward
 
 
 NN = ((1,), (0,))
@@ -794,27 +710,40 @@
     )
 
 
-def out_kernel(own_ref, a_ref, b_ref, out_ref):
-    out_ref[...] = dot(a_ref[...], b_ref[...]).astype(BF16)
-
-
-def project_out(own_arg, gained, weight):
+def split_rows(value, even_ref, odd_ref):
+    size = even_ref.shape[0]
+    even_ref[...] = value[:size].astype(BF16)
+    odd_ref[...] = value[size:].astype(BF16)
+
+
+def split_outs(tok_count, parts, width):
+    spec = pl.BlockSpec((None, tok_count, width), lambda i, own: (i, 0, 0))
+    shape = jax.ShapeDtypeStruct((parts // 2, tok_count, width), BF16)
+    return [spec, spec], [shape, shape]
+
+
+def out_kernel(own_ref, a_ref, b_ref, even_ref, odd_ref):
+    split_rows(dot(a_ref[...], b_ref[...]), even_ref, odd_ref)
+
+
+def project_out(own_arg, gained, weight, parts):
     (tokens, inner), width = gained.shape, weight.shape[1]
-    block = min(512, tokens)
+    tok_count = tokens // parts
+    specs, shapes = split_outs(tok_count, parts, width)
     return call(
         out_kernel,
-        (tokens // block,),
-        [pl.BlockSpec((block, inner), lambda i, own: (i, 0)), fixed((inner, width))],
-        [pl.BlockSpec((block, width), lambda i, own: (i, 0))],
-        [jax.ShapeDtypeStruct((tokens, width), BF16)],
+        (parts // 2,),
+        [pl.BlockSpec((2 * tok_count, inner), lambda i, own: (i, 0)), fixed((inner, width))],
+        specs,
+        shapes,
         (own_arg, gained, weight),
-    )[0]
+    )
 
 
 def into_kernel(parts, own_ref, gate_ref, pre_ref, dt_ref, *refs):
-    weights, tails, out_ref = refs[:parts], refs[parts : 2 * parts], refs[-1]
+    weights, tails = refs[:parts], refs[parts : 2 * parts]
+    even_ref, odd_ref = refs[2 * parts :]
     half, rows = weights[0].shape[1:]
-    inner = 2 * half
     pick = own_heads(own_ref[0], HEADS // parts).astype(BF16)
     grad_dt = dot(dt_ref[...], pick, NT).astype(BF16)
     left = jnp.concatenate([gate_ref[...], pre_ref[...], grad_dt], axis=1)
@@ -822,84 +751,415 @@
         order = [lax.bitwise_xor(q, own_ref[1]) if s > 1 else q for q in range(4)]
         right = jnp.concatenate([weights[s][q] for q in order] + [tails[s][...]], axis=0)
         lanes = pl.ds(pl.multiple_of(lax.bitwise_xor(own_ref[0], s) * rows, LANES), rows)
-        out_ref[:, lanes] = dot(left, right).astype(BF16)
+        split_rows(dot(left, right), even_ref.at[:, lanes], odd_ref.at[:, lanes])
 
 
 def project_into(own_arg, grad_gate, grad_pre, grad_dt, weights, tails):
     parts = len(weights)
     (tokens, inner), channels = grad_gate.shape, grad_pre.shape[1]
     width = parts * weights[0].shape[2]
-    block = min(512, tokens)
+    tok_count = tokens // parts
 
     def tok(size):
-        return pl.BlockSpec((block, size), lambda i, own: (i, 0))
-
+        return pl.BlockSpec((2 * tok_count, size), lambda i, own: (i, 0))
+
+    specs, shapes = split_outs(tok_count, parts, width)
     return call(
         partial(into_kernel, parts),
-        (tokens // block,),
+        (parts // 2,),
         [tok(inner), tok(channels), tok(LANES)]
         + [fixed(w.shape) for w in weights]
         + [fixed(r.shape) for r in tails],
-        [tok(width)],
-        [jax.ShapeDtypeStruct((tokens, width), BF16)],
+        specs,
+        shapes,
         (own_arg, grad_gate, grad_pre, grad_dt, *weights, *tails),
+    )
+
+
+def tail_kernel(count, parts, own_ref, *refs):
+    pres, dts, normed = refs[:count], refs[count : 2 * count], refs[2 * count : 3 * count]
+    even_ref, odd_ref = refs[3 * count :]
+    pick = own_heads(own_ref[0], HEADS // parts)
+
+    def total(lefts):
+        terms = [dot(a[...], b[...], TN) for a, b in zip(lefts, normed)]
+        return sum(terms[1:], terms[0])
+
+    value = [total(pres), dot(pick.astype(BF16), total(dts).astype(BF16))]
+    value = jnp.concatenate(value, axis=0).astype(BF16)
+
+    @pl.when(pl.program_id(0) % 2 == 0)
+    def _():
+        even_ref[...] = value
+
+    @pl.when(pl.program_id(0) % 2 == 1)
+    def _():
+        odd_ref[...] = value
+
+
+def tail_grad(own_arg, grad_pres, grad_dts, normed, parts):
+    (tokens, channels), width = grad_pres[0].shape, normed[0].shape[1]
+    count, columns, rows = len(normed), 2 * STATE + HEADS, width // parts
+    spec = pl.BlockSpec((None, columns, rows), lambda r, own: (r // 2, 0, 0))
+    shape = jax.ShapeDtypeStruct((parts // 2, columns, rows), BF16)
+    return call(
+        partial(tail_kernel, count, parts),
+        (parts,),
+        [pl.BlockSpec((tokens, 2 * STATE), lambda r, own: (0, channels // (2 * STATE) - 1))] * count
+        + [fixed((tokens, LANES))] * count
+        + [pl.BlockSpec((tokens, rows), lambda r, own: (0, lax.bitwise_xor(own[0], r)))] * count,
+        [spec, spec],
+        [shape, shape],
+        (own_arg, *grad_pres, *grad_dts, *normed),
+    )
+
+
+def add_kernel(own_ref, a_ref, b_ref, keep_ref, send_ref):
+    keep_ref[...] = a_ref[0].astype(F32) + b_ref[0].astype(F32)
+    send_ref[...] = (a_ref[1].astype(F32) + b_ref[1].astype(F32)).astype(BF16)
+
+
+def add_parts(own_arg, even, got):
+    _, size, width = even.shape
+    block = size // 2
+    both = pl.BlockSpec((2, block, width), lambda i, own: (0, i, 0))
+    one = pl.BlockSpec((block, width), lambda i, own: (i, 0))
+    struct = jax.ShapeDtypeStruct
+    return call(
+        add_kernel,
+        (2,),
+        [both, both],
+        [one, one],
+        [struct((size, width), F32), struct((size, width), BF16)],
+        (own_arg, even, got),
+    )
+
+
+class Split:
+    def __init__(self, own_arg, parts):
+        self.own_arg = own_arg
+        self.even, self.odd = parts
+        self.plain = self.even.shape[0] != 2
+        self.sent = self.even
+        if not self.plain:
+            self.got = swap(self.odd, "fsdp", 1)
+
+    def middle(self, *earlier):
+        if not self.plain:
+            got = after(self.got, *earlier)
+            self.keep, self.sent = add_parts(self.own_arg, self.even, got)
+            self.got = swap(self.sent, "fsdp", 2)
+        return self.sent
+
+    def final(self, *earlier):
+        if not self.plain:
+            return self.keep, after(self.got, *earlier)
+        every = jnp.stack([self.even, self.odd], axis=1)
+        every = every.reshape((-1,) + self.even.shape[1:])
+        total = scattered(after(every, *earlier))
+        return total, jnp.zeros(total.shape, BF16)
+
+
+def mixed_kernel(own_ref, tok_ref, scale_ref, keep_ref, got_ref, out_ref):
+    total = keep_ref[...] + got_ref[...].astype(F32)
+    out_ref[...] = (tok_ref[...].astype(F32) + total * scale_ref[...]).astype(BF16)
+
+
+def mixed_rows(own_arg, tok, scale, terms):
+    size, width = tok.shape
+    block = min(128, size)
+    one = pl.BlockSpec((block, width), lambda i, own: (i, 0))
+    return call(
+        mixed_kernel,
+        (size // block,),
+        [one, pl.BlockSpec((block, 1), lambda i, own: (i, 0)), one, one],
+        [one],
+        [jax.ShapeDtypeStruct((size, width), BF16)],
+        (own_arg, tok, scale, *terms),
     )[0]
 
 
-def weight_kernel(count, halves, own_ref, *refs):
-    outs = refs[2 * count :]
+def norm_kernel(own_ref, tok_ref, cot_ref, gain_ref, keep_ref, got_ref, out_ref, sum_ref):
+    @pl.when(pl.program_id(0) == 0)
+    def _():
+        sum_ref[...] = jnp.zeros_like(sum_ref)
+
+    tok = tok_ref[...].astype(F32)
+    inverse = lax.rsqrt(jnp.mean(tok * tok, axis=-1, keepdims=True) + EPSILON)
+    hat = tok * inverse
+    part = keep_ref[...] + got_ref[...].astype(F32)
+    through = part * gain_ref[...]
+    here = inverse * (through - hat * jnp.mean(hat * through, axis=-1, keepdims=True))
+    out_ref[...] = (cot_ref[...].astype(F32) + here).astype(BF16)
+    sum_ref[0:1, :] += jnp.sum(part * hat, axis=0, keepdims=True)
+
+
+def norm_rows(own_arg, tok, cot, gain, terms):
+    size, width = tok.shape
+    block = min(128, size)
+    one = pl.BlockSpec((block, width), lambda i, own: (i, 0))
+    return call(
+        norm_kernel,
+        (size // block,),
+        [one, one, fixed((1, width)), one, one],
+        [one, fixed((8, width))],
+        [jax.ShapeDtypeStruct((size, width), BF16), jax.ShapeDtypeStruct((8, width), F32)],
+        (own_arg, tok, cot, gain[None], *terms),
+    )
+
+
+def join_kernel(own_ref, a_ref, b_ref, out_ref):
+    out_ref[...] = (a_ref[...].astype(F32) + b_ref[...].astype(F32)).astype(BF16)
+
+
+def join(own_arg, keep, got):
+    size, width = keep.shape
+    one = pl.BlockSpec((size // 4, width), lambda i, own: (i, 0))
+    return call(
+        join_kernel,
+        (4,),
+        [one, one],
+        [one],
+        [jax.ShapeDtypeStruct((size, width), BF16)],
+        (own_arg, keep, got),
+    )[0]
+
+
+def pick_kernel(order, own_ref, *refs):
+    out_ref = refs[-1]
+    rows = out_ref.shape[-1]
+    for i, (ref, block, lane) in enumerate(order):
+        if lane:
+            lanes = pl.ds(pl.multiple_of(lax.bitwise_xor(own_ref[0], block) * rows, LANES), rows)
+            out_ref[i] = refs[ref][:, lanes]
+        else:
+            out_ref[i] = refs[ref][block]
+
+
+def picked(own_arg, order, args, rows):
+    shape = (len(order), args[0].shape[0], rows)
+    return call(
+        partial(pick_kernel, order),
+        (1,),
+        [fixed(arg.shape) for arg in args],
+        [fixed(shape)],
+        [jax.ShapeDtypeStruct(shape, BF16)],
+        (own_arg, *args),
+    )[0]
+
+
+def place_kernel(own_ref, half_ref, far_ref, near_ref, out_ref):
+    rows = out_ref.shape[-1]
+    own = own_ref[0]
+    lanes = pl.ds(pl.multiple_of(own * rows, LANES), rows)
+    out_ref[own] = half_ref[:, lanes]
+    out_ref[lax.bitwise_xor(own, 2)] = far_ref[0]
+    out_ref[lax.bitwise_xor(own, 1)] = near_ref[0]
+    out_ref[lax.bitwise_xor(own, 3)] = near_ref[1]
+
+
+class Trade:
+    def __init__(self, own_arg, half, parts):
+        self.own_arg, self.half, self.parts = own_arg, half, parts
+        self.rows = half.shape[1] // parts
+        self.sent = half
+        self.plain = parts != 4
+        if not self.plain:
+            self.sent = picked(own_arg, [(0, 2, True), (0, 3, True)], [half], self.rows)
+            self.far = swap(self.sent, "fsdp", 2)
+
+    def middle(self, *earlier):
+        if not self.plain:
+            self.far = after(self.far, *earlier)
+            order = [(0, 1, True), (1, 1, False)]
+            self.sent = picked(self.own_arg, order, [self.half, self.far], self.rows)
+            self.near = swap(self.sent, "fsdp", 1)
+        return self.sent
+
+    def final(self, *earlier):
+        if self.plain:
+            own = lax.axis_index("fsdp")
+            here = [
+                lax.dynamic_slice_in_dim(self.half, (own ^ r) * self.rows, self.rows, 1)
+                for r in range(self.parts)
+            ]
+            here = traded(here, lambda value, bit: swap(value, "fsdp", bit))
+            return jnp.stack(absolute(here))
+        near = after(self.near, *earlier)
+        shape = (self.parts, self.half.shape[0], self.rows)
+        return call(
+            place_kernel,
+            (1,),
+            [fixed(self.half.shape), fixed(self.far.shape), fixed(near.shape)],
+            [fixed(shape)],
+            [jax.ShapeDtypeStruct(shape, BF16)],
+            (self.own_arg, self.half, self.far, near),
+        )[0]
+
+
+def weight_kernel(count, own_ref, *refs):
+    out_ref = refs[-1]
     total = dot(refs[0][...], refs[count][...], TN)
     for m in range(1, count):
         total += dot(refs[m][...], refs[count + m][...], TN)
-    if halves == 1:
-        outs[0][...] = total
-    else:
-        first = pl.program_id(0) < pl.num_programs(0) // 2
-
-        @pl.when(first)
-        def _():
-            outs[0][...] = total.astype(BF16)
-
-        @pl.when(jnp.logical_not(first))
-        def _():
-            outs[1][...] = total.astype(BF16)
-
-
-def weight_grad(own_arg, lefts, rights, inner):
+    out_ref[...] = total.astype(out_ref.dtype)
+
+
+def half_of(own, kept):
+    return lax.bitwise_xor(own[1] & 1, 0 if kept else 1)
+
+
+def weight_grad(own_arg, lefts, rights, inner, kept):
     tokens, width = rights[0].shape
-    block = min(256, inner // 2)
-    per = inner // 2 // block
-
-    def left(i, own):
-        return (0, lax.bitwise_xor(i // per, 1 - (own[1] & 1)) * per + i % per)
-
-    out = jax.ShapeDtypeStruct((inner // 2, width), BF16)
+    half, block = inner // 2, 512
     return call(
-        partial(weight_kernel, len(lefts), 2),
-        (2 * per,),
-        [pl.BlockSpec((tokens, block), left)] * len(lefts)
-        + [fixed((tokens, width))] * len(rights),
-        [
-            pl.BlockSpec((block, width), lambda i, own: (jnp.minimum(i, per - 1), 0)),
-            pl.BlockSpec((block, width), lambda i, own: (jnp.maximum(i - per, 0), 0)),
-        ],
-        [out, out],
-        (own_arg, *lefts, *rights),
-    )
-
-
-def tail_grad(own_arg, lefts, first, rights):
-    (tokens, width), columns = rights[0].shape, lefts[0].shape[1] - first
-    block = LANES
-    return call(
-        partial(weight_kernel, len(lefts), 1),
-        (columns // block,),
-        [pl.BlockSpec((tokens, block), lambda i, own: (0, first // block + i))] * len(lefts)
-        + [fixed((tokens, width))] * len(rights),
-        [pl.BlockSpec((block, width), lambda i, own: (i, 0))],
-        [jax.ShapeDtypeStruct((columns, width), F32)],
+        partial(weight_kernel, len(lefts)),
+        (width // block,),
+        [pl.BlockSpec((tokens, half), lambda i, own: (0, half_of(own, kept)))] * len(lefts)
+        + [pl.BlockSpec((tokens, block), lambda i, own: (0, i))] * len(rights),
+        [pl.BlockSpec((half, block), lambda i, own: (0, i))],
+        [jax.ShapeDtypeStruct((half, width), BF16)],
         (own_arg, *lefts, *rights),
     )[0]
+
+
+def gate_kernel(micro, chunk, per_part, own_ref, *refs):
+    gain_ref, refs = refs[0], refs[1:]
+    ssm, gate, back, stat, normed = (refs[k * micro : (k + 1) * micro] for k in range(5))
+    outs = refs[5 * micro :]
+    grad_ssm, grad_gate, gated_all = (outs[k * micro : (k + 1) * micro] for k in range(3))
+    grad_gain_ref, out_ref = outs[3 * micro :]
+    count = stat[0].shape[0]
+    half = gain_ref.shape[1]
+
+    @pl.when(pl.program_id(1) == 0)
+    def _():
+        grad_gain_ref[...] = jnp.zeros_like(grad_gain_ref)
+
+        def step(t, carry):
+            place = lax.bitwise_xor(t // per_part, own_ref[0]) * per_part + t % per_part
+            rows = pl.ds(pl.multiple_of(place * chunk, chunk), chunk)
+            for m in range(micro):
+                sums = stat[m][t]
+                scale = lax.rsqrt(sums[0:1, :] * (1.0 / INNER) + EPSILON)
+                shift = scale * scale * scale * sums[1:2, :] * (1.0 / INNER)
+                scale = columns(scale, chunk)
+                shift = columns(shift, chunk)
+                for at in range(0, half, LANES):
+                    lanes = slice(at, at + LANES)
+                    out = ssm[m][rows, lanes]
+                    branch = gate[m][rows, lanes]
+                    grad = back[m][rows, lanes].astype(F32)
+                    sig = jax.nn.sigmoid(branch)
+                    silu = branch * sig
+                    gated = out * silu
+                    scaled = gated * scale
+                    gain = gain_ref[:, lanes]
+                    grad_gated = scale * (gain * grad) - gated * shift
+                    grad_ssm[m][rows, lanes] = (grad_gated * silu).astype(BF16)
+                    grad_gate[m][rows, lanes] = (
+                        grad_gated * out * (sig * (1.0 + branch * (1.0 - sig)))
+                    ).astype(BF16)
+                    gated_all[m][rows, lanes] = (scaled * gain).astype(BF16)
+                    grad_gain_ref[0:1, lanes] += jnp.sum(scaled * grad, axis=0, keepdims=True)
+            return carry
+
+        lax.fori_loop(0, count, step, 0)
+
+    terms = [dot(a[...], b[...], TN) for a, b in zip(grad_gate, normed)]
+    out_ref[...] = sum(terms[1:], terms[0]).astype(BF16).reshape(out_ref.shape)
+
+
+def gate_grads(own_arg, scans, stats, normed, gain, per_part, lines):
+    micro = len(scans)
+    (tokens, inner), width = scans[0][0].shape, normed[0].shape[1]
+    half, block = inner // 2, 512
+    chunk = stats[0].shape[2]
+    cols = pl.BlockSpec((tokens, half), lambda h, i, own: (0, h))
+    row = pl.BlockSpec((1, half), lambda h, i, own: (0, h))
+    sums = pl.BlockSpec((8, half), lambda h, i, own: (0, h))
+    lanes = pl.BlockSpec((tokens, block), lambda h, i, own: (0, i))
+    whole = pl.BlockSpec(stats[0].shape, lambda h, i, own: (0, 0, 0))
+    struct = jax.ShapeDtypeStruct
+    outs = call(
+        partial(gate_kernel, micro, chunk, per_part),
+        (2, width // block),
+        [row] + [cols] * (3 * micro) + [whole] * micro + [lanes] * micro,
+        [cols] * (3 * micro)
+        + [sums]
+        + [pl.BlockSpec((lines, None, half // lines, block), lambda h, i, own: (0, h, 0, i))],
+        [struct((tokens, inner), BF16)] * (3 * micro)
+        + [struct((8, inner), F32), struct((lines, 2, half // lines, width), BF16)],
+        (own_arg, gain, *[scan[k] for k in range(3) for scan in scans], *stats, *normed),
+    )
+    split = [outs[k * micro : (k + 1) * micro] for k in range(3)]
+    return split + list(outs[3 * micro :])
+
+
+def fill_kernel(own_ref, part_ref, *refs):
+    out_ref = refs[-1]
+    out_ref[...] = part_ref[...].reshape(out_ref.shape).astype(F32)
+
+
+def fill(own_arg, whole, rows, part, grid, part_spec, out_spec):
+    width = part.shape[-1]
+    return pl.pallas_call(
+        fill_kernel,
+        grid_spec=pltpu.PrefetchScalarGridSpec(
+            num_scalar_prefetch=1,
+            grid=grid,
+            in_specs=[part_spec] + [pl.BlockSpec(memory_space=pl.ANY)] * (whole is not None),
+            out_specs=out_spec,
+        ),
+        out_shape=jax.ShapeDtypeStruct((rows, width), F32),
+        input_output_aliases={} if whole is None else {2: 0},
+        compiler_params=pltpu.CompilerParams(
+            dimension_semantics=("arbitrary",) * len(grid), vmem_limit_bytes=VMEM
+        ),
+        cost_estimate=COST,
+    )(*([own_arg, part] + ([] if whole is None else [whole])))
+
+
+IN_ROWS = 2 * INNER + 2 * STATE + HEADS
+
+
+def fill_lines(own_arg, whole, part, kept):
+    lines, parts, share, rows = part.shape
+    return fill(
+        own_arg,
+        whole,
+        IN_ROWS,
+        part,
+        (parts,),
+        pl.BlockSpec((lines, None, share, rows), lambda f, own: (0, f, 0, 0)),
+        pl.BlockSpec((lines * share, rows), lambda f, own: (2 * f + half_of(own, kept), 0)),
+    )
+
+
+def fill_tail(own_arg, whole, part):
+    return fill(
+        own_arg,
+        whole,
+        IN_ROWS,
+        part,
+        (part.shape[0] // HEADS,),
+        pl.BlockSpec((HEADS, part.shape[1]), lambda i, own: (i, 0)),
+        pl.BlockSpec((HEADS, part.shape[1]), lambda i, own: (2 * INNER // HEADS + i, 0)),
+    )
+
+
+def fill_heads(own_arg, whole, part, first):
+    lines, _, parts, share, rows = part.shape
+    size = lines * share
+    return fill(
+        own_arg,
+        whole,
+        IN_ROWS,
+        part,
+        (parts, 2),
+        pl.BlockSpec((lines, None, None, share, rows), lambda f, k, own: (0, k, f, 0, 0)),
+        pl.BlockSpec((size, rows), lambda f, k, own: (first // size + 2 * f + k, 0)),
+    )
 
 
 def on_device(
@@ -926,7 +1186,7 @@
     rows = width // parts
     seq = tok_count * parts
     chunk = min(LANES, tok_count)
-    forward, gating, backward = scan_calls(parts, tok_count, inner)
+    forward, backward = scan_calls(parts, tok_count, inner)
     side = lax.axis_index("group") & 3
     own_arg = jnp.stack([own, side]).astype(jnp.int32)
     along = Lines()
@@ -972,31 +1232,26 @@
 
     def between(sent, got):
         packed, started["small"] = small(sent)
-        started["tok"] = [gather_far(after(tokens[m, 0], got)) for m in range(micro)]
+        started["tok"] = [gather_far(after(tokens[0, 0], got))]
+        started["tail"] = gather_far(after(in_rows[2 * INNER :], got))
         first = started["tok"][0][parts // 2]
-        last = started["tok"][-1][parts // 2]
-        started["tail"] = gather_far(after(in_rows[2 * INNER :], first))
-        started["cot"] = [gather_far(after(cotangent[0, 0], last))]
-        return [first, packed], list(started["small"])
-
-    weights = traded_weights(in_rows, inner, between)
+        started["tok"] += [gather_far(after(tokens[m, 0], first)) for m in range(1, micro)]
+        started["cot"] = [gather_far(after(cotangent[0, 0], first))]
+        return [first, packed], [started["tail"][parts // 2], *started["small"]]
+
+    with jax.named_scope("weights"):
+        weights = traded_weights(in_rows, inner, between)
     gain_norm, taps, seg_rows, head_row, skip_row, gain_row = started["small"]
     tails = gather_near(started["tail"], weights[1])
-    tok_parts = [gather_near(held, weights[1]) for held in started["tok"]]
-
-    tok_rows = tokens[:, 0].astype(F32)
-    inverse = lax.rsqrt(jnp.mean(tok_rows * tok_rows, axis=-1, keepdims=True) + EPSILON)
-    cot_here = cotangent[:, 0]
 
     projected = []
-    last = started["tok"][-1][parts // 2]
     for m in range(micro):
-        tok_here = [after(part, last, *[p[0] for p in projected[-1:]]) for part in tok_parts[m]]
+        tok_here = gather_near(started["tok"][m], weights[1], *[p[0] for p in projected[-1:]])
         projected.append(project(own_arg, tok_here, weights, tails, gain_norm))
     normed_all = [p[0] for p in projected]
     for m in range(1, micro):
         started["cot"].append(
-            gather_far(after(cotangent[m, 0], started["cot"][m - 1][parts // 2], normed_all[0]))
+            gather_far(after(cotangent[m, 0], started["tok"][m][parts // 2], normed_all[0]))
         )
     scans = []
     cot_all = []
@@ -1009,11 +1264,9 @@
         )
         cot_all.append(cot)
         scans.append((gate, pre, tail, dt_raw, back) + tuple(outs))
-    out_grads = []
-    for m in range(micro):
-        gate, _, _, _, back, _, _, ssm, gained, entering, stat = scans[m]
-        stat = jnp.pad(summed(stat[:, :2], "fsdp"), ((0, 0), (0, 6), (0, 0)))
-        out_grads.append((stat,) + tuple(gating(own_arg, ssm, gate, back, stat, gain_row)))
+    stats = [
+        jnp.pad(summed(scan[-1][:, :2], "fsdp"), ((0, 0), (0, 6), (0, 0))) for scan in scans
+    ]
 
     def scan_back(m, *earlier):
         _, pre, tail, dt_raw, _, act, slope, _, _, entering, _ = scans[m]
@@ -1024,7 +1277,7 @@
             pre,
             tail,
             dt_raw,
-            after(out_grads[m][1], *earlier),
+            after(grad_ssm[m], *earlier),
             entering,
             seg_rows[m],
             taps,
@@ -1035,97 +1288,124 @@
     def across(away):
         return swap(away, "group", 1)
 
+    lines_count = groups // 2
+    lane = lax.axis_index("group") & 1
+
     def joined(keep, got):
-        total = (keep.astype(F32) + got.astype(F32)).astype(BF16)
-        return total.reshape(groups // 2, -1, width)
-
-    def finish(half):
-        arrived = []
-        here = [lax.dynamic_slice_in_dim(half, (own ^ r) * rows, rows, 1) for r in range(parts)]
-        here = traded(here, lambda value, bit: swap(value, "fsdp", bit), arrived)
-        return jnp.stack(absolute(here)), arrived
-
-    def by_part(value):
-        return value.reshape(parts, tok_count, width)
-
-    away_gate, keep_gate = weight_grad(own_arg, [g[2] for g in out_grads], normed_all, inner)
-    got_gate = across(away_gate)
-    gated = [after(g[3], keep_gate) for g in out_grads]
-    away_out, keep_out = weight_grad(own_arg, gated, cot_all, inner)
-    got_out = across(away_out)
+        return join(own_arg, keep, got).reshape(lines_count, -1, width)
+
+    grad_ssm, grad_gates, gated, grad_inner, gate_out = gate_grads(
+        own_arg,
+        [(scan[7], scan[0], scan[4]) for scan in scans],
+        stats,
+        normed_all,
+        gain_row,
+        tok_count // chunk,
+        lines_count,
+    )
+    half_gate = along.scatter(gate_out.reshape(groups, -1, width))
+    gated = [after(g, gate_out) for g in gated]
+    away_out = weight_grad(own_arg, gated, cot_all, inner, False)
+    with jax.named_scope("away_out"):
+        got_out = across(away_out)
+    gated = [after(g, away_out) for g in gated]
+    keep_out = weight_grad(own_arg, gated, cot_all, inner, True)
     backs = [scan_back(0, keep_out)]
-    mixed = [project_out(own_arg, after(scans[0][8], backs[0][0]), out_weight)]
-    half_gate = joined(keep_gate, after(got_gate, mixed[0]))
+    half_out = joined(keep_out, after(got_out, backs[0][0]))
+    with jax.named_scope("trade_gate"):
+        trade = Trade(own_arg, after(half_gate, half_out), parts)
     for m in range(1, micro):
-        backs.append(scan_back(m, half_gate, *mixed[-1:]))
-        mixed.append(project_out(own_arg, after(scans[m][8], backs[m][0]), out_weight))
-    half_gate = along.scatter(half_gate)
-    half_out = joined(keep_out, after(got_out, mixed[-1], half_gate))
-    left = [after(b[0], half_out) for b in backs]
-    away_x, keep_x = weight_grad(own_arg, left, normed_all, inner)
-    got_x = across(away_x)
-    half_out = along.scatter(half_out)
-    gate_cols, arrived = finish(half_gate)
-
-    def project_in(m, *earlier):
-        grad_gate = after(out_grads[m][2], *earlier)
-        return project_into(own_arg, grad_gate, *backs[m][:2], weights, tails)
-
-    into = [project_in(0, keep_x, arrived[0])]
-    chains = [Chain(gate_cols), Chain(half_out)]
-    rights = [after(n, into[0], gate_cols, half_out) for n in normed_all]
-    grad_tail = jnp.concatenate(
-        [
-            tail_grad(own_arg, [b[0] for b in backs], inner, rights),
-            tail_grad(own_arg, [b[1] for b in backs], 0, rights),
-        ],
-        axis=0,
-    )
-    sent = [chains[0].step(keep_x)]
-    into += [project_in(m, grad_tail, *sent[0], *into[-1:]) for m in range(1, micro)]
-    chains[0].step(into[-1])
-    chains[1].step(grad_tail)
-    half_x = joined(keep_x, after(got_x, grad_tail, *into))
-    for chain in (chains[0], chains[1], chains[1]):
-        chain.step(half_x)
-    mixed[0] = scattered(by_part(mixed[0]), [[backs[-1][0]], [keep_x]])
-    mixed[1:] = [scattered(by_part(v), [[keep_x], [grad_tail]]) for v in mixed[1:]]
-    into_sums = [
-        scattered(by_part(v), [[grad_tail if m == 0 else half_x], [half_x]])
-        for m, v in enumerate(into)
-    ]
-    step_part = lax.dynamic_update_slice_in_dim(
-        jnp.zeros((HEADS, width), F32), grad_tail[2 * STATE : 2 * STATE + heads], own * heads, 0
-    )
-    grad_tail = jnp.concatenate([grad_tail[: 2 * STATE], step_part], axis=0)
-    grad_tail = jnp.stack(
-        [lax.dynamic_slice_in_dim(grad_tail, (own ^ r) * rows, rows, 1) for r in range(parts)]
-    )
-    grad_tail = scattered(grad_tail, [[into[-1]], [half_x]])
-    scattered_x = along.scatter(half_x)
-    half_x = scattered_x
-    gate_lines = chains[0].result()
-    out_lines = chains[1].result()
-    x_lines = along.gather(finish(half_x)[0])
-    grad_tail = summed(grad_tail, "group", BF16, [x_lines])
-
-    def placed(whole, lines, kind, side):
-        lines = lines.transpose(1, 0, 2, 3).reshape(parts, inner // 2, rows).astype(F32)
-        for f in range(parts):
-            at = kind * INNER + f * inner + side * (inner // 2)
-            whole = lax.dynamic_update_slice(whole, lines[f], (at, jnp.zeros_like(at)))
-        return whole
-
-    lane = lax.axis_index("group") & 1
-    got_lines = across(gate_lines)
-    got_out = across(out_lines)
-    got_x = across(x_lines)
-    whole = jnp.zeros((2 * INNER + 2 * STATE + HEADS, rows), F32)
-    whole = placed(whole, gate_lines, 0, lane)
-    whole = placed(whole, after(got_lines, x_lines), 0, 1 - lane)
-    whole = placed(whole, x_lines, 1, lane)
-    whole = lax.dynamic_update_slice_in_dim(whole, grad_tail, 2 * INNER, 0)
-    grad_in = placed(whole, got_x, 1, 1 - lane).T
+        backs.append(scan_back(m, half_out, trade.sent))
+    with jax.named_scope("trade_gate"):
+        trade.middle(backs[-1][0])
+        gate_cols = trade.final()
+    left = [after(b[0], gate_cols) for b in backs]
+    away_x = weight_grad(own_arg, left, normed_all, inner, False)
+    with jax.named_scope("away_heads"):
+        got_x = across(away_x)
+    left = [after(b[0], away_x) for b in backs]
+    keep_x = weight_grad(own_arg, left, normed_all, inner, True)
+    half_out = along.scatter(half_out, lines())
+    gate_lines = along.gather(after(gate_cols, away_x), lines())
+
+    into = []
+    for m in range(micro):
+        grad_gate = after(grad_gates[m], keep_x, *(part[0] for part in into[-1:]))
+        into.append(project_into(own_arg, grad_gate, *backs[m][:2], weights, tails))
+    half_x = joined(keep_x, after(got_x, into[-1][0]))
+    with jax.named_scope("gate_lines"):
+        got_lines = across(after(gate_lines, half_x))
+    rights = [after(n, half_x) for n in normed_all]
+    tail_part = tail_grad(own_arg, [b[0] for b in backs], [b[1] for b in backs], rights, parts)
+
+    def split(pair, name):
+        with jax.named_scope(name):
+            return Split(own_arg, [after(part, half_x) for part in pair])
+
+    into = [split(pair, "into") for pair in into]
+    tail_part = split(tail_part, "tail")
+    with jax.named_scope("into"):
+        for part in into:
+            part.middle()
+    with jax.named_scope("tail"):
+        tail_part.middle()
+    half_x = along.scatter(half_x, lines())
+    with jax.named_scope("trade_heads"):
+        trade = Trade(own_arg, half_x, parts)
+    sent = trade.sent
+    grad_tok = []
+    grad_norm = jnp.zeros((width,), F32)
+    for m in range(micro):
+        terms = into[m].final(sent, got_lines)
+        tok, gain = norm_rows(own_arg, tokens[m, 0], cotangent[m, 0], gain_norm, terms)
+        grad_tok.append(tok)
+        grad_norm += gain[0]
+        if m == 0:
+            with jax.named_scope("trade_heads"):
+                sent = trade.middle(tok)
+    with jax.named_scope("trade_heads"):
+        x_cols = trade.final(tok)
+    keep, got = tail_part.final()
+    grad_tail = keep + got.astype(F32)
+
+    grad_taps = sum(b[2] for b in backs)[: CONV + 1]
+    grad_skip = sum(b[3] for b in backs)[0]
+    grad_head = sum(b[4] for b in backs)
+    taps_all = lax.dynamic_update_slice_in_dim(
+        jnp.zeros((CONV + 1, XBC), F32), grad_taps[:, :inner], own * inner, 1
+    )
+    taps_all = taps_all.at[:, INNER:].set(grad_taps[:, inner:])
+    with jax.named_scope("small"):
+        joint = summed(jnp.concatenate([taps_all.reshape(-1), grad_norm]), "fsdp")
+    skip_sum = jnp.sum(grad_skip.reshape(heads, HEADDIM), axis=1)
+    joint = jnp.concatenate(
+        [joint, grad_inner[0], grad_head[0, :heads], grad_head[1, :heads], skip_sum]
+    )
+
+    with jax.named_scope("small"):
+        joint = summed(joint, "group")
+    with jax.named_scope("tail"):
+        grad_tail = summed(grad_tail, "group", BF16)
+    mixed = []
+    for m in range(micro):
+        gained = after(scans[m][8], x_cols, *(part.even for part in mixed[-1:]))
+        part = project_out(own_arg, gained, out_weight, parts)
+        with jax.named_scope("mixed"):
+            mixed.append(Split(own_arg, part))
+    out_lines = along.gather(half_out, lines())
+    with jax.named_scope("out_lines"):
+        got_out = across(after(out_lines, joint, grad_tail))
+    x_all = along.gather(after(x_cols, joint, grad_tail))
+    with jax.named_scope("mixed"):
+        for part in mixed:
+            part.middle(mixed[-1].even)
+
+    def all_lines(value):
+        return value.reshape(lines_count, 2, parts, -1, rows)
+
+    whole = fill_lines(own_arg, None, after(gate_lines, x_cols), True)
+    whole = fill_lines(own_arg, whole, after(got_lines, x_cols), False)
+    whole = fill_tail(own_arg, whole, grad_tail)
     grad_out = jnp.stack(
         [
             jnp.where(lane == 0, out_lines, got_out),
@@ -1136,36 +1416,11 @@
 
     for m in range(micro):
         stat = lax.dynamic_slice_in_dim(
-            out_grads[m][0][:, 0].reshape(seq), own * tok_count, tok_count, 0
+            stats[m][:, 0].reshape(seq), own * tok_count, tok_count, 0
         )
         scale = lax.rsqrt(stat * (1.0 / INNER) + EPSILON)[:, None]
-        mixed[m] = (tok_rows[m] + mixed[m] * scale).astype(BF16)
-
-    grad_tok = []
-    grad_norm = jnp.zeros((width,), F32)
-    for m in range(micro):
-        part = into_sums[m]
-        hat = tok_rows[m] * inverse[m]
-        through = part * gain_norm
-        here = inverse[m] * (through - hat * jnp.mean(hat * through, axis=-1, keepdims=True))
-        grad_tok.append((cot_here[m].astype(F32) + here).astype(BF16))
-        grad_norm += jnp.sum(part * hat, axis=0)
-
-    grad_taps = sum(b[2] for b in backs)[: CONV + 1]
-    grad_skip = sum(b[3] for b in backs)[0]
-    grad_head = sum(b[4] for b in backs)
-    grad_inner = sum(g[4] for g in out_grads)[0]
-    taps_all = lax.dynamic_update_slice_in_dim(
-        jnp.zeros((CONV + 1, XBC), F32), grad_taps[:, :inner], own * inner, 1
-    )
-    taps_all = taps_all.at[:, INNER:].set(grad_taps[:, inner:])
-    joint = summed(jnp.concatenate([taps_all.reshape(-1), grad_norm]), "fsdp")
-    skip_sum = jnp.sum(grad_skip.reshape(heads, HEADDIM), axis=1)
-    joint = summed(
-        jnp.concatenate([joint, grad_inner, grad_head[0, :heads], grad_head[1, :heads], skip_sum]),
-        "group",
-        pin=[x_lines],
-    )
+        mixed[m] = mixed_rows(own_arg, tokens[m, 0], scale, mixed[m].final(whole))
+
     at = (CONV + 1) * XBC
     share = XBC // parts
     taps_all = lax.dynamic_slice_in_dim(joint[:at].reshape(CONV + 1, XBC), own * share, share, 1)
@@ -1176,9 +1431,13 @@
     grad_bias, grad_rate, grad_skip = (
         joint[at + k * heads : at + (k + 1) * heads] for k in range(3)
     )
+    mixed = jnp.stack(mixed)[:, None]
+    grad_tok = jnp.stack(grad_tok)[:, None]
+    x_all = after(x_all, whole, grad_out, grad_norm, mixed, grad_tok)
+    grad_in = fill_heads(own_arg, whole, all_lines(x_all), INNER).T
     return (
-        jnp.stack(mixed)[:, None],
-        jnp.stack(grad_tok)[:, None],
+        mixed,
+        grad_tok,
         grad_norm,
         grad_in,
         taps_all[:CONV],

time: 735 us -> 696 us (0.947)
  other arithmetic: 78.5 us -> 30.3 us
  Pallas kernels: 288 us -> 335 us
  starting transfers between devices: 71.2 us -> 42.1 us
  local copies, waits for them, and re-layouts: 89.5 us -> 75.6 us
    pallas_call x13 -> x31, Pallas kernels: 168 us -> 218 us  [call(): pl.pallas_call(kernel, grid_spec=pltpu.PrefetchScalarGridSpec(num_scalar_...]
    ppermute x12 -> x0, waiting for transfers between devices: 44 us -> none  [shifted(): return lax.ppermute(value, 'group', pairs)]
    ppermute x12 -> x0, starting transfers between devices: 37.3 us -> none  [shifted(): return lax.ppermute(value, 'group', pairs)]
    reduce_scatter x3, waiting for transfers between devices: 0.01 us -> 34.1 us  [scatter(): lax.psum_scatter(self.order(value), 'group', scatter_dimension=0, axis_in...]
    convert_element_type x12 -> x3, other arithmetic: 31.8 us -> 5.06 us  [summed(): value = value + swap(value.astype(kind), axis, bit).astype(F32)]
    unnamed x212, local copies, waits for them, and re-layouts: 32.2 us -> 49.8 us
    ppermute x57 -> x55, waiting for transfers between devices: 140 us -> 156 us  [swap(): return lax.ppermute(value, axis, [(i, i ^ bit) for i in range(count)])]
    dynamic_update_slice x17 -> x0, local copies, waits for them, and re-layouts: 12.8 us -> none  [the longest x16 12.8 us: placed(): whole = lax.dynamic_update_slice(whole, lines[f], (at, jnp.zeros_like(at)))]
  transfers between devices with their start and end apart: 73 -> 61, of which waited for: 30 -> 31; matrix products, arithmetic and copies ran while one was open for 18% -> 8% of each run, Pallas kernels for 36% -> 43%
where the time goes in v3:
time: 696 us; the launch traced here: 691 us
  Pallas kernels  335 us (48%)
  waiting for transfers between devices  192 us (28%)
  local copies, waits for them, and re-layouts  75.6 us (11%)
  starting transfers between devices  42.1 us (6%)
  other arithmetic  30.3 us (4%)
  between operations  15.7 us (2%)
    pallas_call x31, Pallas kernels, call(): pl.pallas_call(kernel, grid_spec=pltpu.PrefetchScalarGridSpec(num_scalar_...  218 us
    ppermute x55, waiting for transfers between devices, swap(): return lax.ppermute(value, axis, [(i, i ^ bit) for i in range(count)])  156 us
    pallas_call x2, Pallas kernels, scan_back(): backward(own_arg, act, slope, pre, tail, dt_raw, after(grad_ssm[m], *earl...  62.6 us
    unnamed x212, local copies, waits for them, and re-layouts  49.8 us
    ppermute x55, starting transfers between devices, swap(): return lax.ppermute(value, axis, [(i, i ^ bit) for i in range(count)])  41.9 us
    pallas_call x2, Pallas kernels, on_device(): forward(own_arg, pre, tail, gate, dt_raw, back, seg_rows[m], taps, head_r...  38.6 us
    reduce_scatter x3, waiting for transfers between devices, scatter(): lax.psum_scatter(self.order(value), 'group', scatter_dimension=0, axis_in...  34.1 us
    pallas_call x4, Pallas kernels, fill(): pl.pallas_call(fill_kernel, grid_spec=pltpu.PrefetchScalarGridSpec(num_sc...  15.7 us
  transfers between devices with their start and end apart: 61, of which 31 were waited for; matrix products, arithmetic and copies ran while one was open for 8% of the time, Pallas kernels for 43%

profile of v3, /device:TPU:0, one launch (start us, length us, event | category | flops | bytes accessed | tf_op | source)
XLA Modules:
  0.0 690.7 jit_solution(1924991954659899909)
XLA Ops:
  20.7 15.9 %collective-permute-done.3 = f32[6464]{0:T(1024)S(1)} collective-permute-done((f32[6464]{0:T(1024)S(1)}, f32[6464]{0:T(1024)S(1)}, u32[]{:S(2)}, u32[]{:S(2)}) %collective-permute-start.3) | collective-permute-done | bytes 25888 | tf_op jit(solution)/shard_map/weights/fsdp_2/ppermute | solution.py:28
  45.2 20.3 %collective-permute-done.10 = bf16[2,512,512]{2,1,0:T(8,128)(2,1)} collective-permute-done((bf16[2,512,512]{2,1,0:T(8,128)(2,1)}, bf16[2,512,512]{2,1,0:T(8,128)(2,1)}, u32[]{:S(2)}, u32[]{:S(2)}) %collective-permute-start.10) | collective-permute-done | bytes 1048608 | tf_op jit(solution)/shard_map/weights/group_2/ppermute | solution.py:28
  71.8 8.1 %collective-permute-done.11 = bf16[2,256,512]{2,1,0:T(8,128)(2,1)S(1)} collective-permute-done((bf16[2,256,512]{2,1,0:T(8,128)(2,1)S(1)}, bf16[2,256,512]{2,1,0:T(8,128)(2,1)S(1)}, u32[]{:S(2)}, u32[]{:S(2)}) %collective-permute-start.11) | collective-permute-done | bytes 524320 | tf_op jit(solution)/shard_map/weights/group_1/ppermute | solution.py:28
  96.1 21.5 %shard_map.203 = (bf16[1024,2048]{1,0:T(8,128)(2,1)}, f32[1024,1024]{1,0:T(8,128)}, bf16[1024,1024]{1,0:T(8,128)(2,1)}, bf16[1024,256]{1,0:T(8,128)(2,1)S(1)}, f32[1024,128]{1,0:T(8,128)S(1)}) custom-call(s32[2]{0:T(128)S(1)} %pad_add_fusion.own_ref, bf16[256,2048]{1,0:T(8,128)(2,1)S(1)} %get-tuple-element.161.refs_0_.tok_ref, ...), custom_call_target="tpu_custom_call" | custom-call | flops 1 | bytes 1 | tf_op jit(solution)/shard_map/pallas_call | solution.py:581
  121.9 21.6 %shard_map.204 = (bf16[1024,2048]{1,0:T(8,128)(2,1)}, f32[1024,1024]{1,0:T(8,128)}, bf16[1024,1024]{1,0:T(8,128)(2,1)}, bf16[1024,256]{1,0:T(8,128)(2,1)S(1)}, f32[1024,128]{1,0:T(8,128)S(1)}) custom-call(s32[2]{0:T(128)S(1)} %pad_add_fusion.own_ref, bf16[256,2048]{1,0:T(8,128)(2,1)S(1)} %get-tuple-element.175.refs_0_.tok_ref, ...), custom_call_target="tpu_custom_call" | custom-call | flops 1 | bytes 1 | tf_op jit(solution)/shard_map/pallas_call | solution.py:581
  147.7 9.0 %shard_map.205 = (bf16[1024,2048]{1,0:T(8,128)(2,1)}, bf16[1024,1024]{1,0:T(8,128)(2,1)}) custom-call(s32[2]{0:T(128)S(1)} %pad_add_fusion.own_ref, bf16[256,2048]{1,0:T(8,128)(2,1)S(1)} %get-tuple-element.178.refs_0_.cot_ref, bf16[256,2048]{1,0:T(8,128)(2,1)S(1)} %collective-permute-done.19.refs_1_, bf16[256,2048]{1,0:T(8,128)(2,1)S(1)} %collective-permute-done.20.refs_2_, ...), custom_call_target="tpu_custom_call" | custom-call | flops 1 | bytes 1 | tf_op jit(solution)/shard_map/pallas_call | solution.py:581
  156.7 19.3 %shard_map.206 = (bf16[1024,1280]{1,0:T(8,128)(2,1)}, bf16[1024,1280]{1,0:T(8,128)(2,1)}, f32[1024,1024]{1,0:T(8,128)}, bf16[1024,1024]{1,0:T(8,128)(2,1)S(1)}, ...) custom-call(s32[2]{0:T(128)S(1)} %pad_add_fusion.own_ref, bf16[1024,1024]{1,0:T(8,128)(2,1)} %get-tuple-element.168.pre_ref, ...), custom_call_target="tpu_custom_call" | custom-call | flops 1 | bytes 1 | tf_op jit(solution)/shard_map/pallas_call | solution.py:1262
  182.9 9.6 %shard_map.207 = (bf16[1024,2048]{1,0:T(8,128)(2,1)}, bf16[1024,1024]{1,0:T(8,128)(2,1)}) custom-call(s32[2]{0:T(128)S(1)} %pad_add_fusion.own_ref, bf16[256,2048]{1,0:T(8,128)(2,1)S(1)} %get-tuple-element.191.refs_0_.cot_ref, bf16[256,2048]{1,0:T(8,128)(2,1)S(1)} %collective-permute-done.24.refs_1_, bf16[256,2048]{1,0:T(8,128)(2,1)S(1)} %collective-permute-done.25.refs_2_, ...), custom_call_target="tpu_custom_call" | custom-call | flops 1 | bytes 1 | tf_op jit(solution)/shard_map/pallas_call | solution.py:581
  192.5 19.3 %shard_map.208 = (bf16[1024,1280]{1,0:T(8,128)(2,1)}, bf16[1024,1280]{1,0:T(8,128)(2,1)}, f32[1024,1024]{1,0:T(8,128)}, bf16[1024,1024]{1,0:T(8,128)(2,1)S(1)}, ...) custom-call(s32[2]{0:T(128)S(1)} %pad_add_fusion.own_ref, bf16[1024,1024]{1,0:T(8,128)(2,1)} %get-tuple-element.186.pre_ref, ...), custom_call_target="tpu_custom_call" | custom-call | flops 1 | bytes 1 | tf_op jit(solution)/shard_map/pallas_call | solution.py:1262
  219.9 31.7 %shard_map.209 = (bf16[1024,1024]{1,0:T(8,128)(2,1)S(1)}, bf16[1024,1024]{1,0:T(8,128)(2,1)S(1)}, bf16[1024,1024]{1,0:T(8,128)(2,1)}, bf16[1024,1024]{1,0:T(8,12...) custom-call(s32[2]{0:T(128)S(1)} %pad_add_fusion.own_ref, ...), custom_call_target="tpu_custom_call" | custom-call | flops 1 | bytes 1 | tf_op jit(solution)/shard_map/pallas_call | solution.py:581
  255.9 8.2 %shard_map.210 = bf16[512,2048]{1,0:T(8,128)(2,1)S(1)} custom-call(s32[2]{0:T(128)S(1)} %pad_add_fusion.own_ref, bf16[1024,1024]{1,0:T(8,128)(2,1)S(1)} %copy-done.13, bf16[1024,1024]{1,0:T(8,128)(2,1)} %get-tuple-element.205.refs_1_, bf16[1024,2048]{1,0:T(8,128)(2,1)} %get-tuple-element.202.refs_2_, bf16[1024,2048]{1,0:T(8,128)(2,1)} %get-tuple-element.203.refs_3_), custom_call_target="tpu_custom_call" | custom-call | flops 1 | bytes 1 | tf_op jit(solution)/shard_map/pallas_call | solution.py:581
  264.6 8.5 %shard_map.211.a_ref = bf16[512,2048]{1,0:T(8,128)(2,1)S(1)} custom-call(s32[2]{0:T(128)S(1)} %pad_add_fusion.own_ref, bf16[1024,1024]{1,0:T(8,128)(2,1)S(1)} %copy-done.13, bf16[1024,1024]{1,0:T(8,128)(2,1)} %get-tuple-element.205.refs_1_, bf16[1024,2048]{1,0:T(8,128)(2,1)} %get-tuple-element.202.refs_2_, bf16[1024,2048]{1,0:T(8,128)(2,1)} %get-tuple-element.203.refs_3_), custom_call_target="tpu_custom_call" | custom-call | flops 1 | bytes 1 | tf_op jit(solution)/shard_map/pallas_call | solution.py:581
  273.2 31.3 %shard_map.212 = (bf16[1024,1280]{1,0:T(8,128)(2,1)}, bf16[1024,128]{1,0:T(8,128)(2,1)S(1)}, f32[8,1280]{1,0:T(8,128)S(1)}, f32[8,1024]{1,0:T(8,128)S(1)}, f32[8,128]{1,0:T(8,128)S(1)}) custom-call(s32[2]{0:T(128)S(1)} %pad_add_fusion.own_ref, bf16[1024,1280]{1,0:T(8,128)(2,1)} %get-tuple-element.183.act_ref, ...), custom_call_target="tpu_custom_call" | custom-call | flops 1 | bytes 1 | tf_op jit(solution)/shard_map/pallas_call | solution.py:1273
  306.3 24.7 %collective-permute-done.29.b_ref = bf16[512,2048]{1,0:T(8,128)(2,1)S(1)} collective-permute-done((bf16[512,2048]{1,0:T(8,128)(2,1)S(1)}, bf16[512,2048]{1,0:T(8,128)(2,1)S(1)}, u32[]{:S(2)}, u32[]{:S(2)}) %collective-permute-start.29) | collective-permute-done | bytes 2097184 | tf_op jit(solution)/shard_map/away_out/group_1/ppermute | solution.py:28
  336.9 18.6 %reduce-scatter.4.cloned.1.call-done = bf16[1,128,2048]{2,1,0:T(8,128)(2,1)} async-done(((bf16[8,128,2048]{2,1,0:T(8,128)(2,1)}), bf16[1,128,2048]{2,1,0:T(8,128)(2,1)}) %reduce-scatter.4.cloned.1.call-update) | async-done | bytes 524304 | tf_op jit(solution)/shard_map/reduce_scatter | solution.py:162
  363.7 31.3 %shard_map.214 = (bf16[1024,1280]{1,0:T(8,128)(2,1)}, bf16[1024,128]{1,0:T(8,128)(2,1)S(1)}, f32[8,1280]{1,0:T(8,128)S(1)}, f32[8,1024]{1,0:T(8,128)S(1)}, f32[8,128]{1,0:T(8,128)S(1)}) custom-call(s32[2]{0:T(128)S(1)} %pad_add_fusion.own_ref, bf16[1024,1280]{1,0:T(8,128)(2,1)} %get-tuple-element.211.act_ref, ...), custom_call_target="tpu_custom_call" | custom-call | flops 1 | bytes 1 | tf_op jit(solution)/shard_map/pallas_call | solution.py:1273
  398.6 8.0 %shard_map.215 = bf16[512,2048]{1,0:T(8,128)(2,1)S(1)} custom-call(s32[2]{0:T(128)S(1)} %pad_add_fusion.own_ref, bf16[1024,1280]{1,0:T(8,128)(2,1)S(1)} %copy-done, bf16[1024,1280]{1,0:T(8,128)(2,1)} %get-tuple-element.221.refs_1_.pre_ref, bf16[1024,2048]{1,0:T(8,128)(2,1)} %get-tuple-element.261.refs_9_.refs_2_.refs_4_, ...), custom_call_target="tpu_custom_call" | custom-call | flops 1 | bytes 1 | tf_op jit(solution)/shard_map/pallas_call | solution.py:581
  409.6 8.1 %shard_map.216.a_ref = bf16[512,2048]{1,0:T(8,128)(2,1)S(1)} custom-call(s32[2]{0:T(128)S(1)} %pad_add_fusion.own_ref, bf16[1024,1280]{1,0:T(8,128)(2,1)S(1)} %copy-done, bf16[1024,1280]{1,0:T(8,128)(2,1)} %get-tuple-element.221.refs_1_.pre_ref, bf16[1024,2048]{1,0:T(8,128)(2,1)} %get-tuple-element.261.refs_9_.refs_2_.refs_4_, ...), custom_call_target="tpu_custom_call" | custom-call | flops 1 | bytes 1 | tf_op jit(solution)/shard_map/pallas_call | solution.py:581
  417.8 16.0 %shard_map.217 = (bf16[2,256,2048]{2,1,0:T(8,128)(2,1)S(1)}, bf16[2,256,2048]{2,1,0:T(8,128)(2,1)S(1)}) custom-call(s32[2]{0:T(128)S(1)} %pad_add_fusion.own_ref, bf16[1024,1024]{1,0:T(8,128)(2,1)} %get-tuple-element.224.gate_ref, bf16[1024,1280]{1,0:T(8,128)(2,1)} %get-tuple-element.220.refs_0_.pre_ref, ...), custom_call_target="tpu_custom_call" | custom-call | flops 1 | bytes 1 | tf_op jit(solution)/shard_map/pallas_call | solution.py:581
  436.4 16.0 %shard_map.218 = (bf16[2,256,2048]{2,1,0:T(8,128)(2,1)S(1)}, bf16[2,256,2048]{2,1,0:T(8,128)(2,1)S(1)}) custom-call(s32[2]{0:T(128)S(1)} %pad_add_fusion.own_ref, bf16[1024,1024]{1,0:T(8,128)(2,1)} %get-tuple-element.227.gate_ref, bf16[1024,1280]{1,0:T(8,128)(2,1)} %get-tuple-element.221.refs_1_.pre_ref, bf16[1024,128]{1,0:T(8,128)(2,1)S(1)} %copy-done.50, ...), custom_call_target="tpu_custom_call" | custom-call | flops 1 | bytes 1 | tf_op jit(solution)/shard_map/pallas_call | solution.py:581
  489.4 15.4 %reduce-scatter.8.cloned.1.call-done = bf16[1,128,2048]{2,1,0:T(8,128)(2,1)} async-done(((bf16[4,128,2048]{2,1,0:T(8,128)(2,1)}), bf16[1,128,2048]{2,1,0:T(8,128)(2,1)}) %reduce-scatter.8.cloned.1.call-update) | async-done | bytes 524304 | tf_op jit(solution)/shard_map/reduce_scatter | solution.py:162
  520.6 10.4 %collective-permute-done.35.got_ref = bf16[256,2048]{1,0:T(8,128)(2,1)} collective-permute-done((bf16[256,2048]{1,0:T(8,128)(2,1)S(1)}, bf16[256,2048]{1,0:T(8,128)(2,1)}, u32[]{:S(2)}, u32[]{:S(2)}) %collective-permute-start.35) | collective-permute-done | bytes 1048608 | tf_op jit(solution)/shard_map/into/fsdp_2/ppermute | solution.py:28
  633.6 16.3 %collective-permute-done.48.got_ref = bf16[256,2048]{1,0:T(8,128)(2,1)} collective-permute-done((bf16[256,2048]{1,0:T(8,128)(2,1)}, bf16[256,2048]{1,0:T(8,128)(2,1)}, u32[]{:S(2)}, u32[]{:S(2)}) %collective-permute-start.48) | collective-permute-done | bytes 1048608 | tf_op jit(solution)/shard_map/mixed/fsdp_2/ppermute | solution.py:28
  653.4 13.1 %collective-permute-done.54 = bf16[4,128,2048]{2,1,0:T(8,128)(2,1)} collective-permute-done((bf16[4,128,2048]{2,1,0:T(8,128)(2,1)}, bf16[4,128,2048]{2,1,0:T(8,128)(2,1)}, u32[]{:S(2)}, u32[]{:S(2)}) %collective-permute-start.54) | collective-permute-done | bytes 2097184 | tf_op jit(solution)/shard_map/out_lines/group_1/ppermute | solution.py:28
  (458 shorter events, 272.6 us)
Async XLA Ops:
  7.2 348.4 %reduce-scatter.4.cloned.1.call-start = ((), (), s32[]{:S(2)}) async-start(), calls=%async_computation.3 | async-start | bytes 4718592 | tf_op jit(solution)/shard_map/reduce_scatter | solution.py:162
  9.7 28.4 %collective-permute-start = (bf16[2,512,512]{2,1,0:T(8,128)(2,1)}, bf16[2,512,512]{2,1,0:T(8,128)(2,1)}, u32[]{:S(2)}, u32[]{:S(2)}) collective-permute-start(bf16[2,512,512]{2,1,0:T(8,128)(2,1)} %pad_maximum_fusion.4), channel_id=1, source_target_pairs={{0,2},{1,3},{2,0},{3,1},{4,6},{5,7},{6,4},{7,5},{8,10},{9,11},{10,... | collective-permute-start | bytes 3145736 | tf_op jit(solution)/shard_map/weights/fsdp_2/ppermute | solution.py:28
  38.1 28.5 %collective-permute-start.7 = (bf16[256,2048]{1,0:T(8,128)(2,1)S(1)}, bf16[256,2048]{1,0:T(8,128)(2,1)}, u32[]{:S(2)}, u32[]{:S(2)}) collective-permute-start(bf16[256,2048]{1,0:T(8,128)(2,1)S(1)} %get-tuple-element.161.refs_0_.tok_ref), channel_id=1, source_target_pairs={{0,2},{1,3},{2,0},{3,1},{4,6},{5,7},{6,4},{7,5},{8,10},{9,11},{10,... | collective-permute-start | bytes 3145736 | tf_op jit(solution)/shard_map/weights/fsdp_2/ppermute | solution.py:28
  44.6 27.0 %collective-permute-start.1 = (bf16[320,512]{1,0:T(8,128)(2,1)S(1)}, bf16[320,512]{1,0:T(8,128)(2,1)S(1)}, u32[]{:S(2)}, u32[]{:S(2)}) collective-permute-start(bf16[320,512]{1,0:T(8,128)(2,1)S(1)} %slice.170.refs_8_.refs_4_), channel_id=1, source_target_pairs={{0,2},{1,3},{2,0},{3,1},{4,6},{5,7},{6,4},{7,5},{8,10},{9,11},{10,... | collective-permute-start | bytes 983048 | tf_op jit(solution)/shard_map/weights/fsdp_2/ppermute | solution.py:28
  87.3 30.4 %collective-permute-start.17 = (bf16[256,2048]{1,0:T(8,128)(2,1)S(1)}, bf16[256,2048]{1,0:T(8,128)(2,1)S(1)}, u32[]{:S(2)}, u32[]{:S(2)}) collective-permute-start(bf16[256,2048]{1,0:T(8,128)(2,1)S(1)} %get-tuple-element.175.refs_0_.tok_ref), channel_id=1, source_target_pairs={{0,2},{1,3},{2,0},{3,1},{4,6},{5,7},{6,4},{7,5},{8,10},{9,11},{10,... | collective-permute-start | bytes 3145736 | tf_op jit(solution)/shard_map/weights/fsdp_2/ppermute | solution.py:28
  144.1 34.6 %collective-permute-start.25 = (bf16[256,2048]{1,0:T(8,128)(2,1)S(1)}, bf16[256,2048]{1,0:T(8,128)(2,1)S(1)}, u32[]{:S(2)}, u32[]{:S(2)}) collective-permute-start(bf16[256,2048]{1,0:T(8,128)(2,1)S(1)} %get-tuple-element.191.refs_0_.cot_ref), channel_id=1, source_target_pairs={{0,2},{1,3},{2,0},{3,1},{4,6},{5,7},{6,4},{7,5},{8,10},{9,11},{10,... | collective-permute-start | bytes 3145736 | tf_op jit(solution)/shard_map/fsdp_2/ppermute | solution.py:28
  179.2 35.3 %collective-permute-start.22 = (f32[8,2,128]{2,1,0:T(2,128)S(1)}, f32[8,2,128]{2,1,0:T(2,128)S(1)}, u32[]{:S(2)}, u32[]{:S(2)}) collective-permute-start(f32[8,2,128]{2,1,0:T(2,128)S(1)} %slice.149), channel_id=1, source_target_pairs={{0,1},{1,0},{2,3},{3,2},{4,5},{5,4},{6,7},{7,6},{8,9},{9,8},{10,11... | collective-permute-start | bytes 24584 | tf_op jit(solution)/shard_map/fsdp_1/ppermute | solution.py:28
  254.9 153.1 %reduce-scatter.6.cloned.1.call-start = ((), (), s32[]{:S(2)}) async-start(), calls=%async_computation.4 | async-start | bytes 2621440 | tf_op jit(solution)/shard_map/reduce_scatter | solution.py:162
  264.2 66.8 %collective-permute-start.29 = (bf16[512,2048]{1,0:T(8,128)(2,1)S(1)}, bf16[512,2048]{1,0:T(8,128)(2,1)S(1)}, u32[]{:S(2)}, u32[]{:S(2)}) collective-permute-start(bf16[512,2048]{1,0:T(8,128)(2,1)S(1)} %shard_map.210), channel_id=1, source_target_pairs={{0,4},{4,0},{8,12},{12,8},{16,20},{20,16},{24,28},{28,24},{1,5},{5... | collective-permute-start | bytes 6291464 | tf_op jit(solution)/shard_map/away_out/group_1/ppermute | solution.py:28
  355.6 106.5 %all-gather.7.cloned.1.call-start = ((), (), s32[]{:S(2)}) async-start(), calls=%async_computation.6 | async-start | bytes 2621440 | tf_op jit(solution)/shard_map/all_gather | solution.py:168
  357.2 37.8 %collective-permute-start.30 = (bf16[2,128,512]{2,1,0:T(8,128)(2,1)S(1)}, bf16[2,128,512]{2,1,0:T(8,128)(2,1)S(1)}, u32[]{:S(2)}, u32[]{:S(2)}) collective-permute-start(bf16[2,128,512]{2,1,0:T(8,128)(2,1)S(1)} %trade_gate.3), channel_id=1, source_target_pairs={{0,2},{1,3},{2,0},{3,1},{4,6},{5,7},{6,4},{7,5},{8,10},{9,11},{10,... | collective-permute-start | bytes 786440 | tf_op jit(solution)/shard_map/trade_gate/fsdp_2/ppermute | solution.py:28
  408.0 96.8 %reduce-scatter.8.cloned.1.call-start = ((), (), s32[]{:S(2)}) async-start(), calls=%async_computation.5 | async-start | bytes 2621440 | tf_op jit(solution)/shard_map/reduce_scatter | solution.py:162
  408.1 47.9 %collective-permute-start.32 = (bf16[512,2048]{1,0:T(8,128)(2,1)}, bf16[512,2048]{1,0:T(8,128)(2,1)S(1)}, u32[]{:S(2)}, u32[]{:S(2)}) collective-permute-start(bf16[512,2048]{1,0:T(8,128)(2,1)} %copy-done.30), channel_id=1, source_target_pairs={{0,4},{4,0},{8,12},{12,8},{16,20},{20,16},{24,28},{28,24},{1,5},{5... | collective-permute-start | bytes 6291464 | tf_op jit(solution)/shard_map/away_heads/group_1/ppermute | solution.py:28
  462.1 117.8 %all-gather.9.cloned.1.call-start = ((), (), s32[]{:S(2)}) async-start(), calls=%async_computation.7 | async-start | bytes 2621440 | tf_op jit(solution)/shard_map/all_gather | solution.py:168
  462.7 68.4 %collective-permute-start.36 = (bf16[4,4,128,512]{3,2,1,0:T(8,128)(2,1)}, bf16[4,4,128,512]{3,2,1,0:T(8,128)(2,1)}, u32[]{:S(2)}, u32[]{:S(2)}) collective-permute-start(bf16[4,4,128,512]{3,2,1,0:T(8,128)(2,1)} %bitcast.124), channel_id=1, source_target_pairs={{0,4},{4,0},{8,12},{12,8},{16,20},{20,16},{24,28},{28,24},{1,5},{5... | collective-permute-start | bytes 6291464 | tf_op jit(solution)/shard_map/gate_lines/group_1/ppermute | solution.py:28
  475.5 29.4 %collective-permute-start.43 = (bf16[320,512]{1,0:T(8,128)(2,1)}, bf16[320,512]{1,0:T(8,128)(2,1)}, u32[]{:S(2)}, u32[]{:S(2)}) collective-permute-start(bf16[320,512]{1,0:T(8,128)(2,1)} %get-tuple-element.268), channel_id=1, source_target_pairs={{0,2},{1,3},{2,0},{3,1},{4,6},{5,7},{6,4},{7,5},{8,10},{9,11},{10,... | collective-permute-start | bytes 983048 | tf_op jit(solution)/shard_map/tail/fsdp_2/ppermute | solution.py:28
  482.2 56.1 %collective-permute-start.39 = (bf16[256,2048]{1,0:T(8,128)(2,1)}, bf16[256,2048]{1,0:T(8,128)(2,1)}, u32[]{:S(2)}, u32[]{:S(2)}) collective-permute-start(bf16[256,2048]{1,0:T(8,128)(2,1)} %get-tuple-element.248), channel_id=1, source_target_pairs={{0,2},{1,3},{2,0},{3,1},{4,6},{5,7},{6,4},{7,5},{8,10},{9,11},{10,... | collective-permute-start | bytes 3145736 | tf_op jit(solution)/shard_map/into/fsdp_2/ppermute | solution.py:28
  488.5 42.6 %collective-permute-start.35 = (bf16[256,2048]{1,0:T(8,128)(2,1)S(1)}, bf16[256,2048]{1,0:T(8,128)(2,1)}, u32[]{:S(2)}, u32[]{:S(2)}) collective-permute-start(bf16[256,2048]{1,0:T(8,128)(2,1)S(1)} %get-tuple-element.239), channel_id=1, source_target_pairs={{0,2},{1,3},{2,0},{3,1},{4,6},{5,7},{6,4},{7,5},{8,10},{9,11},{10,... | collective-permute-start | bytes 3145736 | tf_op jit(solution)/shard_map/into/fsdp_2/ppermute | solution.py:28
  504.9 171.3 %all-gather.11.cloned.1.call-start = ((), (), s32[]{:S(2)}) async-start(), calls=%async_computation.8 | async-start | bytes 4718592 | tf_op jit(solution)/shard_map/all_gather | solution.py:168
  510.4 26.7 %collective-permute-start.33 = (bf16[2,128,512]{2,1,0:T(8,128)(2,1)S(1)}, bf16[2,128,512]{2,1,0:T(8,128)(2,1)S(1)}, u32[]{:S(2)}, u32[]{:S(2)}) collective-permute-start(bf16[2,128,512]{2,1,0:T(8,128)(2,1)S(1)} %trade_heads.3), channel_id=1, source_target_pairs={{0,2},{1,3},{2,0},{3,1},{4,6},{5,7},{6,4},{7,5},{8,10},{9,11},{10,... | collective-permute-start | bytes 786440 | tf_op jit(solution)/shard_map/trade_heads/fsdp_2/ppermute | solution.py:28
  518.9 30.2 %collective-permute-start.45 = (bf16[320,512]{1,0:T(8,128)(2,1)S(1)}, bf16[320,512]{1,0:T(8,128)(2,1)S(1)}, u32[]{:S(2)}, u32[]{:S(2)}) collective-permute-start(bf16[320,512]{1,0:T(8,128)(2,1)S(1)} %fusion.4), channel_id=1, source_target_pairs={{0,8},{4,12},{8,0},{12,4},{16,24},{20,28},{24,16},{28,20},{1,9},{5... | collective-permute-start | bytes 983048 | tf_op jit(solution)/shard_map/tail/group_2/ppermute | solution.py:28
  596.2 70.4 %collective-permute-start.54 = (bf16[4,128,2048]{2,1,0:T(8,128)(2,1)}, bf16[4,128,2048]{2,1,0:T(8,128)(2,1)}, u32[]{:S(2)}, u32[]{:S(2)}) collective-permute-start(bf16[4,128,2048]{2,1,0:T(8,128)(2,1)} %bitcast.143), channel_id=1, source_target_pairs={{0,4},{4,0},{8,12},{12,8},{16,20},{20,16},{24,28},{28,24},{1,5},{5... | collective-permute-start | bytes 6291464 | tf_op jit(solution)/shard_map/out_lines/group_1/ppermute | solution.py:28
  602.2 28.8 %collective-permute-start.41 = (bf16[256,2048]{1,0:T(8,128)(2,1)}, bf16[256,2048]{1,0:T(8,128)(2,1)S(1)}, u32[]{:S(2)}, u32[]{:S(2)}) collective-permute-start(bf16[256,2048]{1,0:T(8,128)(2,1)} %get-tuple-element.260), channel_id=1, source_target_pairs={{0,2},{1,3},{2,0},{3,1},{4,6},{5,7},{6,4},{7,5},{8,10},{9,11},{10,... | collective-permute-start | bytes 3145736 | tf_op jit(solution)/shard_map/mixed/fsdp_2/ppermute | solution.py:28
  609.3 40.5 %collective-permute-start.48 = (bf16[256,2048]{1,0:T(8,128)(2,1)}, bf16[256,2048]{1,0:T(8,128)(2,1)}, u32[]{:S(2)}, u32[]{:S(2)}) collective-permute-start(bf16[256,2048]{1,0:T(8,128)(2,1)} %get-tuple-element.275), channel_id=1, source_target_pairs={{0,2},{1,3},{2,0},{3,1},{4,6},{5,7},{6,4},{7,5},{8,10},{9,11},{10,... | collective-permute-start | bytes 3145736 | tf_op jit(solution)/shard_map/mixed/fsdp_2/ppermute | solution.py:28
  (145 other events, 1748.8 us)
Sparse Core Ops, SparseCore 0:
  254.4 101.0 reduce-scatter.3
  358.0 43.6 reduce-scatter.5
  408.1 44.8 all-gather.6
  462.2 42.5 reduce-scatter.7
  506.3 53.2 all-gather.8
  580.0 96.1 all-gather.10

commit v4 on v3

--- a/solution.py
+++ b/solution.py
@@ -291,9 +291,9 @@
         outflow = jnp.exp(last_pair - run_pair) * ending * size_pair
         flown[:, lanes] = (x_pair * outflow).astype(BF16)
         state[:, lanes] = (jnp.exp(last_pair) * passing) * state[:, lanes]
-        gate = gate_ref[:, lanes]
+        gate = gate_ref[:, lanes].astype(F32)
         gated = ssm * (gate * jax.nn.sigmoid(gate))
-        out_ref[:, lanes] = ssm
+        out_ref[:, lanes] = ssm.astype(BF16)
         gained = gated * gain_ref[:, lanes]
         gained_ref[:, lanes] = gained.astype(BF16)
         squares += gated * gated
@@ -531,7 +531,7 @@
         [
             struct((tokens, channels), BF16),
             struct((tokens, channels), BF16),
-            struct((tokens, inner), F32),
+            struct((tokens, inner), BF16),
             struct((tokens, inner), BF16),
             struct((count, STATE, inner), BF16),
             struct((count, 8, chunk), F32),
@@ -629,7 +629,7 @@
 
     @pl.when(at < 2)
     def _():
-        gate_ref[...] = total(weights)
+        gate_ref[...] = total(weights).astype(BF16)
 
     @pl.when((at >= 2) & (at < 4))
     def _():
@@ -671,7 +671,7 @@
         ],
         [
             struct((tokens, width), BF16),
-            struct((tokens, 2 * half), F32),
+            struct((tokens, 2 * half), BF16),
             struct((tokens, 2 * half), BF16),
             struct((tokens, 2 * STATE), BF16),
             struct((tokens, LANES), F32),
@@ -1032,39 +1032,37 @@
     count = stat[0].shape[0]
     half = gain_ref.shape[1]
 
-    @pl.when(pl.program_id(1) == 0)
-    def _():
-        grad_gain_ref[...] = jnp.zeros_like(grad_gain_ref)
-
-        def step(t, carry):
-            place = lax.bitwise_xor(t // per_part, own_ref[0]) * per_part + t % per_part
-            rows = pl.ds(pl.multiple_of(place * chunk, chunk), chunk)
-            for m in range(micro):
-                sums = stat[m][t]
-                scale = lax.rsqrt(sums[0:1, :] * (1.0 / INNER) + EPSILON)
-                shift = scale * scale * scale * sums[1:2, :] * (1.0 / INNER)
-                scale = columns(scale, chunk)
-                shift = columns(shift, chunk)
-                for at in range(0, half, LANES):
-                    lanes = slice(at, at + LANES)
-                    out = ssm[m][rows, lanes]
-                    branch = gate[m][rows, lanes]
-                    grad = back[m][rows, lanes].astype(F32)
-                    sig = jax.nn.sigmoid(branch)
-                    silu = branch * sig
-                    gated = out * silu
-                    scaled = gated * scale
-                    gain = gain_ref[:, lanes]
-                    grad_gated = scale * (gain * grad) - gated * shift
-                    grad_ssm[m][rows, lanes] = (grad_gated * silu).astype(BF16)
-                    grad_gate[m][rows, lanes] = (
-                        grad_gated * out * (sig * (1.0 + branch * (1.0 - sig)))
-                    ).astype(BF16)
-                    gated_all[m][rows, lanes] = (scaled * gain).astype(BF16)
-                    grad_gain_ref[0:1, lanes] += jnp.sum(scaled * grad, axis=0, keepdims=True)
-            return carry
-
-        lax.fori_loop(0, count, step, 0)
+    grad_gain_ref[...] = jnp.zeros_like(grad_gain_ref)
+
+    def step(t, carry):
+        place = lax.bitwise_xor(t // per_part, own_ref[0]) * per_part + t % per_part
+        rows = pl.ds(pl.multiple_of(place * chunk, chunk), chunk)
+        for m in range(micro):
+            sums = stat[m][t]
+            scale = lax.rsqrt(sums[0:1, :] * (1.0 / INNER) + EPSILON)
+            shift = scale * scale * scale * sums[1:2, :] * (1.0 / INNER)
+            scale = columns(scale, chunk)
+            shift = columns(shift, chunk)
+            for at in range(0, half, LANES):
+                lanes = slice(at, at + LANES)
+                out = ssm[m][rows, lanes].astype(F32)
+                branch = gate[m][rows, lanes].astype(F32)
+                grad = back[m][rows, lanes].astype(F32)
+                sig = jax.nn.sigmoid(branch)
+                silu = branch * sig
+                gated = out * silu
+                scaled = gated * scale
+                gain = gain_ref[:, lanes]
+                grad_gated = scale * (gain * grad) - gated * shift
+                grad_ssm[m][rows, lanes] = (grad_gated * silu).astype(BF16)
+                grad_gate[m][rows, lanes] = (
+                    grad_gated * out * (sig * (1.0 + branch * (1.0 - sig)))
+                ).astype(BF16)
+                gated_all[m][rows, lanes] = (scaled * gain).astype(BF16)
+                grad_gain_ref[0:1, lanes] += jnp.sum(scaled * grad, axis=0, keepdims=True)
+        return carry
+
+    lax.fori_loop(0, count, step, 0)
 
     terms = [dot(a[...], b[...], TN) for a, b in zip(grad_gate, normed)]
     out_ref[...] = sum(terms[1:], terms[0]).astype(BF16).reshape(out_ref.shape)
@@ -1073,23 +1071,28 @@
 def gate_grads(own_arg, scans, stats, normed, gain, per_part, lines):
     micro = len(scans)
     (tokens, inner), width = scans[0][0].shape, normed[0].shape[1]
-    half, block = inner // 2, 512
+    share = inner // 2 // lines
+    taken = max(1, min(lines, 256 // share))
+    block = taken * share
     chunk = stats[0].shape[2]
-    cols = pl.BlockSpec((tokens, half), lambda h, i, own: (0, h))
-    row = pl.BlockSpec((1, half), lambda h, i, own: (0, h))
-    sums = pl.BlockSpec((8, half), lambda h, i, own: (0, h))
-    lanes = pl.BlockSpec((tokens, block), lambda h, i, own: (0, i))
-    whole = pl.BlockSpec(stats[0].shape, lambda h, i, own: (0, 0, 0))
+    cols = pl.BlockSpec((tokens, block), lambda i, own: (0, i))
+    row = pl.BlockSpec((1, block), lambda i, own: (0, i))
+    sums = pl.BlockSpec((8, block), lambda i, own: (0, i))
     struct = jax.ShapeDtypeStruct
     outs = call(
         partial(gate_kernel, micro, chunk, per_part),
-        (2, width // block),
-        [row] + [cols] * (3 * micro) + [whole] * micro + [lanes] * micro,
+        (inner // block,),
+        [row] + [cols] * (3 * micro) + [fixed(stats[0].shape)] * micro + [fixed((tokens, width))] * micro,
         [cols] * (3 * micro)
         + [sums]
-        + [pl.BlockSpec((lines, None, half // lines, block), lambda h, i, own: (0, h, 0, i))],
+        + [
+            pl.BlockSpec(
+                (taken, None, share, width),
+                lambda i, own: (i % (lines // taken), i // (lines // taken), 0, 0),
+            )
+        ],
         [struct((tokens, inner), BF16)] * (3 * micro)
-        + [struct((8, inner), F32), struct((lines, 2, half // lines, width), BF16)],
+        + [struct((8, inner), F32), struct((lines, 2, share, width), BF16)],
         (own_arg, gain, *[scan[k] for k in range(3) for scan in scans], *stats, *normed),
     )
     split = [outs[k * micro : (k + 1) * micro] for k in range(3)]

time: 696 us -> 689 us (0.990)
  Pallas kernels: 335 us -> 327 us
    pallas_call x31, Pallas kernels: 218 us -> 209 us  [call(): pl.pallas_call(kernel, grid_spec=pltpu.PrefetchScalarGridSpec(num_scalar_...]
    unnamed x212 -> x216, local copies, waits for them, and re-layouts: 49.8 us -> 51.1 us
  transfers between devices with their start and end apart: 61 -> 61, of which waited for: 31 -> 32; matrix products, arithmetic and copies ran while one was open for 8% -> 8% of each run, Pallas kernels for 43% -> 43%
where the time goes in v4:
time: 689 us; the launch traced here: 684 us
  Pallas kernels  327 us (47%)
  waiting for transfers between devices  192 us (28%)
  local copies, waits for them, and re-layouts  76.9 us (11%)
  starting transfers between devices  42.3 us (6%)
  other arithmetic  30.3 us (4%)
  between operations  15.7 us (2%)
    pallas_call x31, Pallas kernels, call(): pl.pallas_call(kernel, grid_spec=pltpu.PrefetchScalarGridSpec(num_scalar_...  209 us
    ppermute x55, waiting for transfers between devices, swap(): return lax.ppermute(value, axis, [(i, i ^ bit) for i in range(count)])  155 us
    pallas_call x2, Pallas kernels, scan_back(): backward(own_arg, act, slope, pre, tail, dt_raw, after(grad_ssm[m], *earl...  62.6 us
    unnamed x216, local copies, waits for them, and re-layouts  51.1 us
    ppermute x55, starting transfers between devices, swap(): return lax.ppermute(value, axis, [(i, i ^ bit) for i in range(count)])  42.1 us
    pallas_call x2, Pallas kernels, on_device(): forward(own_arg, pre, tail, gate, dt_raw, back, seg_rows[m], taps, head_r...  39.1 us
    reduce_scatter x3, waiting for transfers between devices, scatter(): lax.psum_scatter(self.order(value), 'group', scatter_dimension=0, axis_in...  34.2 us
    pallas_call x4, Pallas kernels, fill(): pl.pallas_call(fill_kernel, grid_spec=pltpu.PrefetchScalarGridSpec(num_sc...  15.7 us
  transfers between devices with their start and end apart: 61, of which 32 were waited for; matrix products, arithmetic and copies ran while one was open for 8% of the time, Pallas kernels for 43%

profile of v4, /device:TPU:0, one launch (start us, length us, event | category | flops | bytes accessed | tf_op | source)
XLA Modules:
  0.0 684.2 jit_solution(11069729175324057267)
XLA Ops:
  20.7 15.9 %collective-permute-done.3 = f32[6464]{0:T(1024)S(1)} collective-permute-done((f32[6464]{0:T(1024)S(1)}, f32[6464]{0:T(1024)S(1)}, u32[]{:S(2)}, u32[]{:S(2)}) %collective-permute-start.3) | collective-permute-done | bytes 25888 | tf_op jit(solution)/shard_map/weights/fsdp_2/ppermute | solution.py:28
  45.2 20.3 %collective-permute-done.10 = bf16[2,512,512]{2,1,0:T(8,128)(2,1)} collective-permute-done((bf16[2,512,512]{2,1,0:T(8,128)(2,1)}, bf16[2,512,512]{2,1,0:T(8,128)(2,1)}, u32[]{:S(2)}, u32[]{:S(2)}) %collective-permute-start.10) | collective-permute-done | bytes 1048608 | tf_op jit(solution)/shard_map/weights/group_2/ppermute | solution.py:28
  71.8 8.1 %collective-permute-done.11 = bf16[2,256,512]{2,1,0:T(8,128)(2,1)S(1)} collective-permute-done((bf16[2,256,512]{2,1,0:T(8,128)(2,1)S(1)}, bf16[2,256,512]{2,1,0:T(8,128)(2,1)S(1)}, u32[]{:S(2)}, u32[]{:S(2)}) %collective-permute-start.11) | collective-permute-done | bytes 524320 | tf_op jit(solution)/shard_map/weights/group_1/ppermute | solution.py:28
  96.1 21.1 %shard_map.203 = (bf16[1024,2048]{1,0:T(8,128)(2,1)}, bf16[1024,1024]{1,0:T(8,128)(2,1)}, bf16[1024,1024]{1,0:T(8,128)(2,1)}, bf16[1024,256]{1,0:T(8,128)(2,1)S(1)}, f32[1024,128]{1,0:T(8,128)S(1)}) custom-call(s32[2]{0:T(128)S(1)} %pad_add_fusion.own_ref, bf16[256,2048]{1,0:T(8,128)(2,1)S(1)} %get-tuple-element.161.refs_0_.tok_ref, ...), custom_call_target="tpu_custom_call" | custom-call | flops 1 | bytes 1 | tf_op jit(solution)/shard_map/pallas_call | solution.py:581
  121.4 21.1 %shard_map.204 = (bf16[1024,2048]{1,0:T(8,128)(2,1)}, bf16[1024,1024]{1,0:T(8,128)(2,1)}, bf16[1024,1024]{1,0:T(8,128)(2,1)}, bf16[1024,256]{1,0:T(8,128)(2,1)S(1)}, f32[1024,128]{1,0:T(8,128)S(1)}) custom-call(s32[2]{0:T(128)S(1)} %pad_add_fusion.own_ref, bf16[256,2048]{1,0:T(8,128)(2,1)S(1)} %get-tuple-element.175.refs_0_.tok_ref, ...), custom_call_target="tpu_custom_call" | custom-call | flops 1 | bytes 1 | tf_op jit(solution)/shard_map/pallas_call | solution.py:581
  147.1 9.1 %shard_map.205 = (bf16[1024,2048]{1,0:T(8,128)(2,1)}, bf16[1024,1024]{1,0:T(8,128)(2,1)}) custom-call(s32[2]{0:T(128)S(1)} %pad_add_fusion.own_ref, bf16[256,2048]{1,0:T(8,128)(2,1)S(1)} %get-tuple-element.178.refs_0_.cot_ref, bf16[256,2048]{1,0:T(8,128)(2,1)S(1)} %collective-permute-done.19.refs_1_, bf16[256,2048]{1,0:T(8,128)(2,1)S(1)} %collective-permute-done.20.refs_2_, ...), custom_call_target="tpu_custom_call" | custom-call | flops 1 | bytes 1 | tf_op jit(solution)/shard_map/pallas_call | solution.py:581
  156.1 19.6 %shard_map.206 = (bf16[1024,1280]{1,0:T(8,128)(2,1)}, bf16[1024,1280]{1,0:T(8,128)(2,1)}, bf16[1024,1024]{1,0:T(8,128)(2,1)S(1)}, bf16[1024,1024]{1,0:T(8,128)(2...) custom-call(s32[2]{0:T(128)S(1)} %pad_add_fusion.own_ref, ...), custom_call_target="tpu_custom_call" | custom-call | flops 1 | bytes 1 | tf_op jit(solution)/shard_map/pallas_call | solution.py:1265
  182.5 9.5 %shard_map.207 = (bf16[1024,2048]{1,0:T(8,128)(2,1)}, bf16[1024,1024]{1,0:T(8,128)(2,1)}) custom-call(s32[2]{0:T(128)S(1)} %pad_add_fusion.own_ref, bf16[256,2048]{1,0:T(8,128)(2,1)S(1)} %get-tuple-element.191.refs_0_.cot_ref, bf16[256,2048]{1,0:T(8,128)(2,1)S(1)} %collective-permute-done.24.refs_1_, bf16[256,2048]{1,0:T(8,128)(2,1)S(1)} %collective-permute-done.25.refs_2_, ...), custom_call_target="tpu_custom_call" | custom-call | flops 1 | bytes 1 | tf_op jit(solution)/shard_map/pallas_call | solution.py:581
  192.1 19.6 %shard_map.208 = (bf16[1024,1280]{1,0:T(8,128)(2,1)}, bf16[1024,1280]{1,0:T(8,128)(2,1)}, bf16[1024,1024]{1,0:T(8,128)(2,1)S(1)}, bf16[1024,1024]{1,0:T(8,128)(2...) custom-call(s32[2]{0:T(128)S(1)} %pad_add_fusion.own_ref, ...), custom_call_target="tpu_custom_call" | custom-call | flops 1 | bytes 1 | tf_op jit(solution)/shard_map/pallas_call | solution.py:1265
  219.9 25.6 %shard_map.209 = (bf16[1024,1024]{1,0:T(8,128)(2,1)S(1)}, bf16[1024,1024]{1,0:T(8,128)(2,1)S(1)}, bf16[1024,1024]{1,0:T(8,128)(2,1)}, bf16[1024,1024]{1,0:T(8,12...) custom-call(s32[2]{0:T(128)S(1)} %pad_add_fusion.own_ref, ...), custom_call_target="tpu_custom_call" | custom-call | flops 1 | bytes 1 | tf_op jit(solution)/shard_map/pallas_call | solution.py:581
  249.7 8.2 %shard_map.210 = bf16[512,2048]{1,0:T(8,128)(2,1)S(1)} custom-call(s32[2]{0:T(128)S(1)} %pad_add_fusion.own_ref, bf16[1024,1024]{1,0:T(8,128)(2,1)S(1)} %copy-done.14, bf16[1024,1024]{1,0:T(8,128)(2,1)} %get-tuple-element.205.refs_1_, bf16[1024,2048]{1,0:T(8,128)(2,1)} %get-tuple-element.202.refs_2_, bf16[1024,2048]{1,0:T(8,128)(2,1)} %get-tuple-element.203.refs_3_), custom_call_target="tpu_custom_call" | custom-call | flops 1 | bytes 1 | tf_op jit(solution)/shard_map/pallas_call | solution.py:581
  258.4 8.5 %shard_map.211.a_ref = bf16[512,2048]{1,0:T(8,128)(2,1)S(1)} custom-call(s32[2]{0:T(128)S(1)} %pad_add_fusion.own_ref, bf16[1024,1024]{1,0:T(8,128)(2,1)S(1)} %copy-done.14, bf16[1024,1024]{1,0:T(8,128)(2,1)} %get-tuple-element.205.refs_1_, bf16[1024,2048]{1,0:T(8,128)(2,1)} %get-tuple-element.202.refs_2_, bf16[1024,2048]{1,0:T(8,128)(2,1)} %get-tuple-element.203.refs_3_), custom_call_target="tpu_custom_call" | custom-call | flops 1 | bytes 1 | tf_op jit(solution)/shard_map/pallas_call | solution.py:581
  267.0 31.3 %shard_map.212 = (bf16[1024,1280]{1,0:T(8,128)(2,1)}, bf16[1024,128]{1,0:T(8,128)(2,1)S(1)}, f32[8,1280]{1,0:T(8,128)S(1)}, f32[8,1024]{1,0:T(8,128)S(1)}, f32[8,128]{1,0:T(8,128)S(1)}) custom-call(s32[2]{0:T(128)S(1)} %pad_add_fusion.own_ref, bf16[1024,1280]{1,0:T(8,128)(2,1)} %get-tuple-element.183.act_ref, ...), custom_call_target="tpu_custom_call" | custom-call | flops 1 | bytes 1 | tf_op jit(solution)/shard_map/pallas_call | solution.py:1276
  300.2 24.5 %collective-permute-done.29.b_ref = bf16[512,2048]{1,0:T(8,128)(2,1)S(1)} collective-permute-done((bf16[512,2048]{1,0:T(8,128)(2,1)S(1)}, bf16[512,2048]{1,0:T(8,128)(2,1)S(1)}, u32[]{:S(2)}, u32[]{:S(2)}) %collective-permute-start.29) | collective-permute-done | bytes 2097184 | tf_op jit(solution)/shard_map/away_out/group_1/ppermute | solution.py:28
  330.5 18.8 %reduce-scatter.4.cloned.1.call-done = bf16[1,128,2048]{2,1,0:T(8,128)(2,1)} async-done(((bf16[8,128,2048]{2,1,0:T(8,128)(2,1)}), bf16[1,128,2048]{2,1,0:T(8,128)(2,1)}) %reduce-scatter.4.cloned.1.call-update) | async-done | bytes 524304 | tf_op jit(solution)/shard_map/reduce_scatter | solution.py:162
  357.3 31.3 %shard_map.214 = (bf16[1024,1280]{1,0:T(8,128)(2,1)}, bf16[1024,128]{1,0:T(8,128)(2,1)S(1)}, f32[8,1280]{1,0:T(8,128)S(1)}, f32[8,1024]{1,0:T(8,128)S(1)}, f32[8,128]{1,0:T(8,128)S(1)}) custom-call(s32[2]{0:T(128)S(1)} %pad_add_fusion.own_ref, bf16[1024,1280]{1,0:T(8,128)(2,1)} %get-tuple-element.211.act_ref, ...), custom_call_target="tpu_custom_call" | custom-call | flops 1 | bytes 1 | tf_op jit(solution)/shard_map/pallas_call | solution.py:1276
  392.3 8.0 %shard_map.215 = bf16[512,2048]{1,0:T(8,128)(2,1)S(1)} custom-call(s32[2]{0:T(128)S(1)} %pad_add_fusion.own_ref, bf16[1024,1280]{1,0:T(8,128)(2,1)S(1)} %copy-done, bf16[1024,1280]{1,0:T(8,128)(2,1)} %get-tuple-element.221.refs_1_.pre_ref, bf16[1024,2048]{1,0:T(8,128)(2,1)} %get-tuple-element.261.refs_9_.refs_2_.refs_4_, ...), custom_call_target="tpu_custom_call" | custom-call | flops 1 | bytes 1 | tf_op jit(solution)/shard_map/pallas_call | solution.py:581
  403.2 8.1 %shard_map.216.a_ref = bf16[512,2048]{1,0:T(8,128)(2,1)S(1)} custom-call(s32[2]{0:T(128)S(1)} %pad_add_fusion.own_ref, bf16[1024,1280]{1,0:T(8,128)(2,1)S(1)} %copy-done, bf16[1024,1280]{1,0:T(8,128)(2,1)} %get-tuple-element.221.refs_1_.pre_ref, bf16[1024,2048]{1,0:T(8,128)(2,1)} %get-tuple-element.261.refs_9_.refs_2_.refs_4_, ...), custom_call_target="tpu_custom_call" | custom-call | flops 1 | bytes 1 | tf_op jit(solution)/shard_map/pallas_call | solution.py:581
  411.4 16.1 %shard_map.217 = (bf16[2,256,2048]{2,1,0:T(8,128)(2,1)S(1)}, bf16[2,256,2048]{2,1,0:T(8,128)(2,1)S(1)}) custom-call(s32[2]{0:T(128)S(1)} %pad_add_fusion.own_ref, bf16[1024,1024]{1,0:T(8,128)(2,1)} %get-tuple-element.224.gate_ref, bf16[1024,1280]{1,0:T(8,128)(2,1)} %get-tuple-element.220.refs_0_.pre_ref, ...), custom_call_target="tpu_custom_call" | custom-call | flops 1 | bytes 1 | tf_op jit(solution)/shard_map/pallas_call | solution.py:581
  430.2 16.0 %shard_map.218 = (bf16[2,256,2048]{2,1,0:T(8,128)(2,1)S(1)}, bf16[2,256,2048]{2,1,0:T(8,128)(2,1)S(1)}) custom-call(s32[2]{0:T(128)S(1)} %pad_add_fusion.own_ref, bf16[1024,1024]{1,0:T(8,128)(2,1)} %get-tuple-element.227.gate_ref, bf16[1024,1280]{1,0:T(8,128)(2,1)} %get-tuple-element.221.refs_1_.pre_ref, bf16[1024,128]{1,0:T(8,128)(2,1)S(1)} %copy-done.52, ...), custom_call_target="tpu_custom_call" | custom-call | flops 1 | bytes 1 | tf_op jit(solution)/shard_map/pallas_call | solution.py:581
  483.0 15.4 %reduce-scatter.8.cloned.1.call-done = bf16[1,128,2048]{2,1,0:T(8,128)(2,1)} async-done(((bf16[4,128,2048]{2,1,0:T(8,128)(2,1)}), bf16[1,128,2048]{2,1,0:T(8,128)(2,1)}) %reduce-scatter.8.cloned.1.call-update) | async-done | bytes 524304 | tf_op jit(solution)/shard_map/reduce_scatter | solution.py:162
  514.2 10.4 %collective-permute-done.35.got_ref = bf16[256,2048]{1,0:T(8,128)(2,1)} collective-permute-done((bf16[256,2048]{1,0:T(8,128)(2,1)S(1)}, bf16[256,2048]{1,0:T(8,128)(2,1)}, u32[]{:S(2)}, u32[]{:S(2)}) %collective-permute-start.35) | collective-permute-done | bytes 1048608 | tf_op jit(solution)/shard_map/into/fsdp_2/ppermute | solution.py:28
  627.1 16.2 %collective-permute-done.48.got_ref = bf16[256,2048]{1,0:T(8,128)(2,1)} collective-permute-done((bf16[256,2048]{1,0:T(8,128)(2,1)}, bf16[256,2048]{1,0:T(8,128)(2,1)}, u32[]{:S(2)}, u32[]{:S(2)}) %collective-permute-start.48) | collective-permute-done | bytes 1048608 | tf_op jit(solution)/shard_map/mixed/fsdp_2/ppermute | solution.py:28
  647.0 13.1 %collective-permute-done.54 = bf16[4,128,2048]{2,1,0:T(8,128)(2,1)} collective-permute-done((bf16[4,128,2048]{2,1,0:T(8,128)(2,1)}, bf16[4,128,2048]{2,1,0:T(8,128)(2,1)}, u32[]{:S(2)}, u32[]{:S(2)}) %collective-permute-start.54) | collective-permute-done | bytes 2097184 | tf_op jit(solution)/shard_map/out_lines/group_1/ppermute | solution.py:28
  (462 shorter events, 272.5 us)
Async XLA Ops:
  7.2 342.0 %reduce-scatter.4.cloned.1.call-start = ((), (), s32[]{:S(2)}) async-start(), calls=%async_computation.3 | async-start | bytes 4718592 | tf_op jit(solution)/shard_map/reduce_scatter | solution.py:162
  9.7 28.4 %collective-permute-start = (bf16[2,512,512]{2,1,0:T(8,128)(2,1)}, bf16[2,512,512]{2,1,0:T(8,128)(2,1)}, u32[]{:S(2)}, u32[]{:S(2)}) collective-permute-start(bf16[2,512,512]{2,1,0:T(8,128)(2,1)} %pad_maximum_fusion.4), channel_id=1, source_target_pairs={{0,2},{1,3},{2,0},{3,1},{4,6},{5,7},{6,4},{7,5},{8,10},{9,11},{10,... | collective-permute-start | bytes 3145736 | tf_op jit(solution)/shard_map/weights/fsdp_2/ppermute | solution.py:28
  38.1 28.5 %collective-permute-start.7 = (bf16[256,2048]{1,0:T(8,128)(2,1)S(1)}, bf16[256,2048]{1,0:T(8,128)(2,1)}, u32[]{:S(2)}, u32[]{:S(2)}) collective-permute-start(bf16[256,2048]{1,0:T(8,128)(2,1)S(1)} %get-tuple-element.161.refs_0_.tok_ref), channel_id=1, source_target_pairs={{0,2},{1,3},{2,0},{3,1},{4,6},{5,7},{6,4},{7,5},{8,10},{9,11},{10,... | collective-permute-start | bytes 3145736 | tf_op jit(solution)/shard_map/weights/fsdp_2/ppermute | solution.py:28
  44.6 27.0 %collective-permute-start.1 = (bf16[320,512]{1,0:T(8,128)(2,1)S(1)}, bf16[320,512]{1,0:T(8,128)(2,1)S(1)}, u32[]{:S(2)}, u32[]{:S(2)}) collective-permute-start(bf16[320,512]{1,0:T(8,128)(2,1)S(1)} %slice.170.refs_8_.refs_4_), channel_id=1, source_target_pairs={{0,2},{1,3},{2,0},{3,1},{4,6},{5,7},{6,4},{7,5},{8,10},{9,11},{10,... | collective-permute-start | bytes 983048 | tf_op jit(solution)/shard_map/weights/fsdp_2/ppermute | solution.py:28
  87.2 30.0 %collective-permute-start.17 = (bf16[256,2048]{1,0:T(8,128)(2,1)S(1)}, bf16[256,2048]{1,0:T(8,128)(2,1)S(1)}, u32[]{:S(2)}, u32[]{:S(2)}) collective-permute-start(bf16[256,2048]{1,0:T(8,128)(2,1)S(1)} %get-tuple-element.175.refs_0_.tok_ref), channel_id=1, source_target_pairs={{0,2},{1,3},{2,0},{3,1},{4,6},{5,7},{6,4},{7,5},{8,10},{9,11},{10,... | collective-permute-start | bytes 3145736 | tf_op jit(solution)/shard_map/weights/fsdp_2/ppermute | solution.py:28
  143.4 34.9 %collective-permute-start.25 = (bf16[256,2048]{1,0:T(8,128)(2,1)S(1)}, bf16[256,2048]{1,0:T(8,128)(2,1)S(1)}, u32[]{:S(2)}, u32[]{:S(2)}) collective-permute-start(bf16[256,2048]{1,0:T(8,128)(2,1)S(1)} %get-tuple-element.191.refs_0_.cot_ref), channel_id=1, source_target_pairs={{0,2},{1,3},{2,0},{3,1},{4,6},{5,7},{6,4},{7,5},{8,10},{9,11},{10,... | collective-permute-start | bytes 3145736 | tf_op jit(solution)/shard_map/fsdp_2/ppermute | solution.py:28
  178.9 35.6 %collective-permute-start.22 = (f32[8,2,128]{2,1,0:T(2,128)S(1)}, f32[8,2,128]{2,1,0:T(2,128)S(1)}, u32[]{:S(2)}, u32[]{:S(2)}) collective-permute-start(f32[8,2,128]{2,1,0:T(2,128)S(1)} %slice.149), channel_id=1, source_target_pairs={{0,1},{1,0},{2,3},{3,2},{4,5},{5,4},{6,7},{7,6},{8,9},{9,8},{10,11... | collective-permute-start | bytes 24584 | tf_op jit(solution)/shard_map/fsdp_1/ppermute | solution.py:28
  248.7 152.9 %reduce-scatter.6.cloned.1.call-start = ((), (), s32[]{:S(2)}) async-start(), calls=%async_computation.4 | async-start | bytes 2621440 | tf_op jit(solution)/shard_map/reduce_scatter | solution.py:162
  257.9 66.8 %collective-permute-start.29 = (bf16[512,2048]{1,0:T(8,128)(2,1)S(1)}, bf16[512,2048]{1,0:T(8,128)(2,1)S(1)}, u32[]{:S(2)}, u32[]{:S(2)}) collective-permute-start(bf16[512,2048]{1,0:T(8,128)(2,1)S(1)} %shard_map.210), channel_id=1, source_target_pairs={{0,4},{4,0},{8,12},{12,8},{16,20},{20,16},{24,28},{28,24},{1,5},{5... | collective-permute-start | bytes 6291464 | tf_op jit(solution)/shard_map/away_out/group_1/ppermute | solution.py:28
  349.3 106.4 %all-gather.7.cloned.1.call-start = ((), (), s32[]{:S(2)}) async-start(), calls=%async_computation.6 | async-start | bytes 2621440 | tf_op jit(solution)/shard_map/all_gather | solution.py:168
  350.9 37.7 %collective-permute-start.30 = (bf16[2,128,512]{2,1,0:T(8,128)(2,1)S(1)}, bf16[2,128,512]{2,1,0:T(8,128)(2,1)S(1)}, u32[]{:S(2)}, u32[]{:S(2)}) collective-permute-start(bf16[2,128,512]{2,1,0:T(8,128)(2,1)S(1)} %trade_gate.3), channel_id=1, source_target_pairs={{0,2},{1,3},{2,0},{3,1},{4,6},{5,7},{6,4},{7,5},{8,10},{9,11},{10,... | collective-permute-start | bytes 786440 | tf_op jit(solution)/shard_map/trade_gate/fsdp_2/ppermute | solution.py:28
  401.6 96.8 %reduce-scatter.8.cloned.1.call-start = ((), (), s32[]{:S(2)}) async-start(), calls=%async_computation.5 | async-start | bytes 2621440 | tf_op jit(solution)/shard_map/reduce_scatter | solution.py:162
  401.7 47.9 %collective-permute-start.32 = (bf16[512,2048]{1,0:T(8,128)(2,1)}, bf16[512,2048]{1,0:T(8,128)(2,1)S(1)}, u32[]{:S(2)}, u32[]{:S(2)}) collective-permute-start(bf16[512,2048]{1,0:T(8,128)(2,1)} %copy-done.32), channel_id=1, source_target_pairs={{0,4},{4,0},{8,12},{12,8},{16,20},{20,16},{24,28},{28,24},{1,5},{5... | collective-permute-start | bytes 6291464 | tf_op jit(solution)/shard_map/away_heads/group_1/ppermute | solution.py:28
  455.6 117.8 %all-gather.9.cloned.1.call-start = ((), (), s32[]{:S(2)}) async-start(), calls=%async_computation.7 | async-start | bytes 2621440 | tf_op jit(solution)/shard_map/all_gather | solution.py:168
  456.3 68.4 %collective-permute-start.36 = (bf16[4,4,128,512]{3,2,1,0:T(8,128)(2,1)}, bf16[4,4,128,512]{3,2,1,0:T(8,128)(2,1)}, u32[]{:S(2)}, u32[]{:S(2)}) collective-permute-start(bf16[4,4,128,512]{3,2,1,0:T(8,128)(2,1)} %bitcast.125), channel_id=1, source_target_pairs={{0,4},{4,0},{8,12},{12,8},{16,20},{20,16},{24,28},{28,24},{1,5},{5... | collective-permute-start | bytes 6291464 | tf_op jit(solution)/shard_map/gate_lines/group_1/ppermute | solution.py:28
  469.1 29.4 %collective-permute-start.43 = (bf16[320,512]{1,0:T(8,128)(2,1)}, bf16[320,512]{1,0:T(8,128)(2,1)}, u32[]{:S(2)}, u32[]{:S(2)}) collective-permute-start(bf16[320,512]{1,0:T(8,128)(2,1)} %get-tuple-element.268), channel_id=1, source_target_pairs={{0,2},{1,3},{2,0},{3,1},{4,6},{5,7},{6,4},{7,5},{8,10},{9,11},{10,... | collective-permute-start | bytes 983048 | tf_op jit(solution)/shard_map/tail/fsdp_2/ppermute | solution.py:28
  475.8 56.1 %collective-permute-start.39 = (bf16[256,2048]{1,0:T(8,128)(2,1)}, bf16[256,2048]{1,0:T(8,128)(2,1)}, u32[]{:S(2)}, u32[]{:S(2)}) collective-permute-start(bf16[256,2048]{1,0:T(8,128)(2,1)} %get-tuple-element.248), channel_id=1, source_target_pairs={{0,2},{1,3},{2,0},{3,1},{4,6},{5,7},{6,4},{7,5},{8,10},{9,11},{10,... | collective-permute-start | bytes 3145736 | tf_op jit(solution)/shard_map/into/fsdp_2/ppermute | solution.py:28
  482.0 42.6 %collective-permute-start.35 = (bf16[256,2048]{1,0:T(8,128)(2,1)S(1)}, bf16[256,2048]{1,0:T(8,128)(2,1)}, u32[]{:S(2)}, u32[]{:S(2)}) collective-permute-start(bf16[256,2048]{1,0:T(8,128)(2,1)S(1)} %get-tuple-element.239), channel_id=1, source_target_pairs={{0,2},{1,3},{2,0},{3,1},{4,6},{5,7},{6,4},{7,5},{8,10},{9,11},{10,... | collective-permute-start | bytes 3145736 | tf_op jit(solution)/shard_map/into/fsdp_2/ppermute | solution.py:28
  498.4 171.3 %all-gather.11.cloned.1.call-start = ((), (), s32[]{:S(2)}) async-start(), calls=%async_computation.8 | async-start | bytes 4718592 | tf_op jit(solution)/shard_map/all_gather | solution.py:168
  503.9 26.7 %collective-permute-start.33 = (bf16[2,128,512]{2,1,0:T(8,128)(2,1)S(1)}, bf16[2,128,512]{2,1,0:T(8,128)(2,1)S(1)}, u32[]{:S(2)}, u32[]{:S(2)}) collective-permute-start(bf16[2,128,512]{2,1,0:T(8,128)(2,1)S(1)} %trade_heads.3), channel_id=1, source_target_pairs={{0,2},{1,3},{2,0},{3,1},{4,6},{5,7},{6,4},{7,5},{8,10},{9,11},{10,... | collective-permute-start | bytes 786440 | tf_op jit(solution)/shard_map/trade_heads/fsdp_2/ppermute | solution.py:28
  512.4 30.2 %collective-permute-start.45 = (bf16[320,512]{1,0:T(8,128)(2,1)S(1)}, bf16[320,512]{1,0:T(8,128)(2,1)S(1)}, u32[]{:S(2)}, u32[]{:S(2)}) collective-permute-start(bf16[320,512]{1,0:T(8,128)(2,1)S(1)} %fusion.4), channel_id=1, source_target_pairs={{0,8},{4,12},{8,0},{12,4},{16,24},{20,28},{24,16},{28,20},{1,9},{5... | collective-permute-start | bytes 983048 | tf_op jit(solution)/shard_map/tail/group_2/ppermute | solution.py:28
  589.7 70.4 %collective-permute-start.54 = (bf16[4,128,2048]{2,1,0:T(8,128)(2,1)}, bf16[4,128,2048]{2,1,0:T(8,128)(2,1)}, u32[]{:S(2)}, u32[]{:S(2)}) collective-permute-start(bf16[4,128,2048]{2,1,0:T(8,128)(2,1)} %bitcast.144), channel_id=1, source_target_pairs={{0,4},{4,0},{8,12},{12,8},{16,20},{20,16},{24,28},{28,24},{1,5},{5... | collective-permute-start | bytes 6291464 | tf_op jit(solution)/shard_map/out_lines/group_1/ppermute | solution.py:28
  595.7 28.8 %collective-permute-start.41 = (bf16[256,2048]{1,0:T(8,128)(2,1)}, bf16[256,2048]{1,0:T(8,128)(2,1)S(1)}, u32[]{:S(2)}, u32[]{:S(2)}) collective-permute-start(bf16[256,2048]{1,0:T(8,128)(2,1)} %get-tuple-element.260), channel_id=1, source_target_pairs={{0,2},{1,3},{2,0},{3,1},{4,6},{5,7},{6,4},{7,5},{8,10},{9,11},{10,... | collective-permute-start | bytes 3145736 | tf_op jit(solution)/shard_map/mixed/fsdp_2/ppermute | solution.py:28
  602.9 40.5 %collective-permute-start.48 = (bf16[256,2048]{1,0:T(8,128)(2,1)}, bf16[256,2048]{1,0:T(8,128)(2,1)}, u32[]{:S(2)}, u32[]{:S(2)}) collective-permute-start(bf16[256,2048]{1,0:T(8,128)(2,1)} %get-tuple-element.275), channel_id=1, source_target_pairs={{0,2},{1,3},{2,0},{3,1},{4,6},{5,7},{6,4},{7,5},{8,10},{9,11},{10,... | collective-permute-start | bytes 3145736 | tf_op jit(solution)/shard_map/mixed/fsdp_2/ppermute | solution.py:28
  (147 other events, 1779.3 us)
Sparse Core Ops, SparseCore 0:
  248.2 100.9 reduce-scatter.3
  351.6 43.6 reduce-scatter.5
  401.7 44.9 all-gather.6
  455.7 42.5 reduce-scatter.7
  499.9 53.2 all-gather.8
  573.6 96.1 all-gather.10

commit v5 on v4

--- a/solution.py
+++ b/solution.py
@@ -140,9 +140,12 @@
     return value[0]
 
 
-def summed(value, axis, kind=F32):
-    for bit in bits_of(lax.axis_size(axis))[::-1]:
+def summed(value, axis, kind=F32, far_first=False, steps=None):
+    bits = bits_of(lax.axis_size(axis))
+    for bit in bits if far_first else bits[::-1]:
         value = value + swap(value.astype(kind), axis, bit).astype(F32)
+        if steps is not None:
+            steps.append(value)
     return value
 
 
@@ -1348,18 +1351,26 @@
     into = [split(pair, "into") for pair in into]
     tail_part = split(tail_part, "tail")
     with jax.named_scope("into"):
-        for part in into:
-            part.middle()
+        sent = [part.middle() for part in into]
     with jax.named_scope("tail"):
-        tail_part.middle()
+        sent.append(tail_part.middle())
+    keep, got = tail_part.final(*sent)
+    steps = [keep + got.astype(F32)]
+    with jax.named_scope("tail"):
+        grad_tail = summed(steps[0], "group", BF16, True, steps)
+    mixed = []
+    for m in range(micro):
+        gained = after(scans[m][8], steps[0], *sent, *(pair[0] for pair in mixed[-1:]))
+        mixed.append(project_out(own_arg, gained, out_weight, parts))
     half_x = along.scatter(half_x, lines())
     with jax.named_scope("trade_heads"):
-        trade = Trade(own_arg, half_x, parts)
+        trade = Trade(own_arg, after(half_x, mixed[-1][0]), parts)
+    out_pin = mixed[-1][0]
     sent = trade.sent
     grad_tok = []
     grad_norm = jnp.zeros((width,), F32)
     for m in range(micro):
-        terms = into[m].final(sent, got_lines)
+        terms = into[m].final(sent, got_lines, steps[min(m + 1, len(steps) - 1)])
         tok, gain = norm_rows(own_arg, tokens[m, 0], cotangent[m, 0], gain_norm, terms)
         grad_tok.append(tok)
         grad_norm += gain[0]
@@ -1368,9 +1379,6 @@
                 sent = trade.middle(tok)
     with jax.named_scope("trade_heads"):
         x_cols = trade.final(tok)
-    keep, got = tail_part.final()
-    grad_tail = keep + got.astype(F32)
-
     grad_taps = sum(b[2] for b in backs)[: CONV + 1]
     grad_skip = sum(b[3] for b in backs)[0]
     grad_head = sum(b[4] for b in backs)
@@ -1387,21 +1395,14 @@
 
     with jax.named_scope("small"):
         joint = summed(joint, "group")
-    with jax.named_scope("tail"):
-        grad_tail = summed(grad_tail, "group", BF16)
-    mixed = []
-    for m in range(micro):
-        gained = after(scans[m][8], x_cols, *(part.even for part in mixed[-1:]))
-        part = project_out(own_arg, gained, out_weight, parts)
-        with jax.named_scope("mixed"):
-            mixed.append(Split(own_arg, part))
-    out_lines = along.gather(half_out, lines())
+    out_lines = along.gather(after(half_out, out_pin), lines())
     with jax.named_scope("out_lines"):
         got_out = across(after(out_lines, joint, grad_tail))
     x_all = along.gather(after(x_cols, joint, grad_tail))
     with jax.named_scope("mixed"):
+        mixed = [Split(own_arg, [after(part, x_cols) for part in pair]) for pair in mixed]
         for part in mixed:
-            part.middle(mixed[-1].even)
+            part.middle()
 
     def all_lines(value):
         return value.reshape(lines_count, 2, parts, -1, rows)

time: 689 us -> 677 us (0.983)
    reduce_scatter x3, waiting for transfers between devices: 34.2 us -> 21.3 us  [scatter(): lax.psum_scatter(self.order(value), 'group', scatter_dimension=0, axis_in...]
    all_gather x3, waiting for transfers between devices: 2.63 us -> 11 us  [gather(): lax.all_gather(self.order(value), 'group', axis=0, axis_index_groups=among)]
    unnamed x216 -> x228, local copies, waits for them, and re-layouts: 51.1 us -> 53.7 us
  transfers between devices with their start and end apart: 61 -> 61, of which waited for: 32 -> 34; matrix products, arithmetic and copies ran while one was open for 8% -> 6% of each run, Pallas kernels for 43% -> 45%
where the time goes in v5:
time: 677 us; the launch traced here: 672 us
  Pallas kernels  330 us (49%)
  waiting for transfers between devices  187 us (28%)
  local copies, waits for them, and re-layouts  73.2 us (11%)
  starting transfers between devices  41.6 us (6%)
  other arithmetic  24.4 us (4%)
  between operations  15.8 us (2%)
    pallas_call x31, Pallas kernels, call(): pl.pallas_call(kernel, grid_spec=pltpu.PrefetchScalarGridSpec(num_scalar_...  211 us
    ppermute x55, waiting for transfers between devices, swap(): return lax.ppermute(value, axis, [(i, i ^ bit) for i in range(count)])  154 us
    pallas_call x2, Pallas kernels, scan_back(): backward(own_arg, act, slope, pre, tail, dt_raw, after(grad_ssm[m], *earl...  62.6 us
    unnamed x228, local copies, waits for them, and re-layouts  53.7 us
    ppermute x55, starting transfers between devices, swap(): return lax.ppermute(value, axis, [(i, i ^ bit) for i in range(count)])  41.4 us
    pallas_call x2, Pallas kernels, on_device(): forward(own_arg, pre, tail, gate, dt_raw, back, seg_rows[m], taps, head_r...  39.1 us
    reduce_scatter x3, waiting for transfers between devices, scatter(): lax.psum_scatter(self.order(value), 'group', scatter_dimension=0, axis_in...  21.3 us
    pallas_call x4, Pallas kernels, fill(): pl.pallas_call(fill_kernel, grid_spec=pltpu.PrefetchScalarGridSpec(num_sc...  17.4 us
  transfers between devices with their start and end apart: 61, of which 34 were waited for; matrix products, arithmetic and copies ran while one was open for 6% of the time, Pallas kernels for 45%

profile of v5, /device:TPU:0, one launch (start us, length us, event | category | flops | bytes accessed | tf_op | source)
XLA Modules:
  0.0 671.7 jit_solution(8612206853005290247)
XLA Ops:
  20.7 15.9 %collective-permute-done.3 = f32[6464]{0:T(1024)S(1)} collective-permute-done((f32[6464]{0:T(1024)S(1)}, f32[6464]{0:T(1024)S(1)}, u32[]{:S(2)}, u32[]{:S(2)}) %collective-permute-start.3) | collective-permute-done | bytes 25888 | tf_op jit(solution)/shard_map/weights/fsdp_2/ppermute | solution.py:28
  45.2 20.3 %collective-permute-done.10 = bf16[2,512,512]{2,1,0:T(8,128)(2,1)} collective-permute-done((bf16[2,512,512]{2,1,0:T(8,128)(2,1)}, bf16[2,512,512]{2,1,0:T(8,128)(2,1)}, u32[]{:S(2)}, u32[]{:S(2)}) %collective-permute-start.10) | collective-permute-done | bytes 1048608 | tf_op jit(solution)/shard_map/weights/group_2/ppermute | solution.py:28
  71.8 8.1 %collective-permute-done.11 = bf16[2,256,512]{2,1,0:T(8,128)(2,1)S(1)} collective-permute-done((bf16[2,256,512]{2,1,0:T(8,128)(2,1)S(1)}, bf16[2,256,512]{2,1,0:T(8,128)(2,1)S(1)}, u32[]{:S(2)}, u32[]{:S(2)}) %collective-permute-start.11) | collective-permute-done | bytes 524320 | tf_op jit(solution)/shard_map/weights/group_1/ppermute | solution.py:28
  96.2 21.1 %shard_map.203 = (bf16[1024,2048]{1,0:T(8,128)(2,1)}, bf16[1024,1024]{1,0:T(8,128)(2,1)}, bf16[1024,1024]{1,0:T(8,128)(2,1)}, bf16[1024,256]{1,0:T(8,128)(2,1)S(1)}, f32[1024,128]{1,0:T(8,128)S(1)}) custom-call(s32[2]{0:T(128)S(1)} %pad_add_fusion.own_ref, bf16[256,2048]{1,0:T(8,128)(2,1)S(1)} %get-tuple-element.166.refs_0_.tok_ref, ...), custom_call_target="tpu_custom_call" | custom-call | flops 1 | bytes 1 | tf_op jit(solution)/shard_map/pallas_call | solution.py:584
  121.6 21.1 %shard_map.204 = (bf16[1024,2048]{1,0:T(8,128)(2,1)}, bf16[1024,1024]{1,0:T(8,128)(2,1)}, bf16[1024,1024]{1,0:T(8,128)(2,1)}, bf16[1024,256]{1,0:T(8,128)(2,1)S(1)}, f32[1024,128]{1,0:T(8,128)S(1)}) custom-call(s32[2]{0:T(128)S(1)} %pad_add_fusion.own_ref, bf16[256,2048]{1,0:T(8,128)(2,1)S(1)} %get-tuple-element.180.refs_0_.tok_ref, ...), custom_call_target="tpu_custom_call" | custom-call | flops 1 | bytes 1 | tf_op jit(solution)/shard_map/pallas_call | solution.py:584
  147.3 9.1 %shard_map.205 = (bf16[1024,2048]{1,0:T(8,128)(2,1)}, bf16[1024,1024]{1,0:T(8,128)(2,1)}) custom-call(s32[2]{0:T(128)S(1)} %pad_add_fusion.own_ref, bf16[256,2048]{1,0:T(8,128)(2,1)S(1)} %get-tuple-element.183.refs_0_.cot_ref, bf16[256,2048]{1,0:T(8,128)(2,1)S(1)} %collective-permute-done.19.refs_1_, bf16[256,2048]{1,0:T(8,128)(2,1)S(1)} %collective-permute-done.20.refs_2_, ...), custom_call_target="tpu_custom_call" | custom-call | flops 1 | bytes 1 | tf_op jit(solution)/shard_map/pallas_call | solution.py:584
  156.4 19.6 %shard_map.206 = (bf16[1024,1280]{1,0:T(8,128)(2,1)}, bf16[1024,1280]{1,0:T(8,128)(2,1)}, bf16[1024,1024]{1,0:T(8,128)(2,1)S(1)}, bf16[1024,1024]{1,0:T(8,128)(2...) custom-call(s32[2]{0:T(128)S(1)} %pad_add_fusion.own_ref, ...), custom_call_target="tpu_custom_call" | custom-call | flops 1 | bytes 1 | tf_op jit(solution)/shard_map/pallas_call | solution.py:1268
  182.8 9.5 %shard_map.207 = (bf16[1024,2048]{1,0:T(8,128)(2,1)}, bf16[1024,1024]{1,0:T(8,128)(2,1)}) custom-call(s32[2]{0:T(128)S(1)} %pad_add_fusion.own_ref, bf16[256,2048]{1,0:T(8,128)(2,1)S(1)} %get-tuple-element.196.refs_0_.cot_ref, bf16[256,2048]{1,0:T(8,128)(2,1)S(1)} %collective-permute-done.24.refs_1_, bf16[256,2048]{1,0:T(8,128)(2,1)S(1)} %collective-permute-done.25.refs_2_, ...), custom_call_target="tpu_custom_call" | custom-call | flops 1 | bytes 1 | tf_op jit(solution)/shard_map/pallas_call | solution.py:584
  192.3 19.5 %shard_map.208 = (bf16[1024,1280]{1,0:T(8,128)(2,1)}, bf16[1024,1280]{1,0:T(8,128)(2,1)}, bf16[1024,1024]{1,0:T(8,128)(2,1)S(1)}, bf16[1024,1024]{1,0:T(8,128)(2...) custom-call(s32[2]{0:T(128)S(1)} %pad_add_fusion.own_ref, ...), custom_call_target="tpu_custom_call" | custom-call | flops 1 | bytes 1 | tf_op jit(solution)/shard_map/pallas_call | solution.py:1268
  220.0 25.6 %shard_map.209 = (bf16[1024,1024]{1,0:T(8,128)(2,1)S(1)}, bf16[1024,1024]{1,0:T(8,128)(2,1)S(1)}, bf16[1024,1024]{1,0:T(8,128)(2,1)}, bf16[1024,1024]{1,0:T(8,12...) custom-call(s32[2]{0:T(128)S(1)} %pad_add_fusion.own_ref, ...), custom_call_target="tpu_custom_call" | custom-call | flops 1 | bytes 1 | tf_op jit(solution)/shard_map/pallas_call | solution.py:584
  249.8 8.2 %shard_map.210 = bf16[512,2048]{1,0:T(8,128)(2,1)S(1)} custom-call(s32[2]{0:T(128)S(1)} %pad_add_fusion.own_ref, bf16[1024,1024]{1,0:T(8,128)(2,1)S(1)} %copy-done.14, bf16[1024,1024]{1,0:T(8,128)(2,1)} %get-tuple-element.210.refs_1_, bf16[1024,2048]{1,0:T(8,128)(2,1)} %get-tuple-element.207.refs_2_, bf16[1024,2048]{1,0:T(8,128)(2,1)} %get-tuple-element.208.refs_3_), custom_call_target="tpu_custom_call" | custom-call | flops 1 | bytes 1 | tf_op jit(solution)/shard_map/pallas_call | solution.py:584
  258.5 8.5 %shard_map.211.a_ref = bf16[512,2048]{1,0:T(8,128)(2,1)S(1)} custom-call(s32[2]{0:T(128)S(1)} %pad_add_fusion.own_ref, bf16[1024,1024]{1,0:T(8,128)(2,1)S(1)} %copy-done.14, bf16[1024,1024]{1,0:T(8,128)(2,1)} %get-tuple-element.210.refs_1_, bf16[1024,2048]{1,0:T(8,128)(2,1)} %get-tuple-element.207.refs_2_, bf16[1024,2048]{1,0:T(8,128)(2,1)} %get-tuple-element.208.refs_3_), custom_call_target="tpu_custom_call" | custom-call | flops 1 | bytes 1 | tf_op jit(solution)/shard_map/pallas_call | solution.py:584
  267.1 31.3 %shard_map.212 = (bf16[1024,1280]{1,0:T(8,128)(2,1)}, bf16[1024,128]{1,0:T(8,128)(2,1)S(1)}, f32[8,1280]{1,0:T(8,128)S(1)}, f32[8,1024]{1,0:T(8,128)S(1)}, f32[8,128]{1,0:T(8,128)S(1)}) custom-call(s32[2]{0:T(128)S(1)} %pad_add_fusion.own_ref, bf16[1024,1280]{1,0:T(8,128)(2,1)} %get-tuple-element.188.act_ref, ...), custom_call_target="tpu_custom_call" | custom-call | flops 1 | bytes 1 | tf_op jit(solution)/shard_map/pallas_call | solution.py:1279
  300.2 24.6 %collective-permute-done.29.b_ref = bf16[512,2048]{1,0:T(8,128)(2,1)S(1)} collective-permute-done((bf16[512,2048]{1,0:T(8,128)(2,1)S(1)}, bf16[512,2048]{1,0:T(8,128)(2,1)S(1)}, u32[]{:S(2)}, u32[]{:S(2)}) %collective-permute-start.29) | collective-permute-done | bytes 2097184 | tf_op jit(solution)/shard_map/away_out/group_1/ppermute | solution.py:28
  330.6 18.8 %reduce-scatter.4.cloned.1.call-done = bf16[1,128,2048]{2,1,0:T(8,128)(2,1)} async-done(((bf16[8,128,2048]{2,1,0:T(8,128)(2,1)}), bf16[1,128,2048]{2,1,0:T(8,128)(2,1)}) %reduce-scatter.4.cloned.1.call-update) | async-done | bytes 524304 | tf_op jit(solution)/shard_map/reduce_scatter | solution.py:165
  357.5 31.3 %shard_map.214 = (bf16[1024,1280]{1,0:T(8,128)(2,1)}, bf16[1024,128]{1,0:T(8,128)(2,1)S(1)}, f32[8,1280]{1,0:T(8,128)S(1)}, f32[8,1024]{1,0:T(8,128)S(1)}, f32[8,128]{1,0:T(8,128)S(1)}) custom-call(s32[2]{0:T(128)S(1)} %pad_add_fusion.own_ref, bf16[1024,1280]{1,0:T(8,128)(2,1)} %get-tuple-element.214.act_ref, ...), custom_call_target="tpu_custom_call" | custom-call | flops 1 | bytes 1 | tf_op jit(solution)/shard_map/pallas_call | solution.py:1279
  392.5 8.0 %shard_map.215 = bf16[512,2048]{1,0:T(8,128)(2,1)S(1)} custom-call(s32[2]{0:T(128)S(1)} %pad_add_fusion.own_ref, bf16[1024,1280]{1,0:T(8,128)(2,1)S(1)} %copy-done, bf16[1024,1280]{1,0:T(8,128)(2,1)} %get-tuple-element.228.refs_1_.pre_ref, bf16[1024,2048]{1,0:T(8,128)(2,1)} %get-tuple-element.236.refs_9_.refs_2_.refs_4_, ...), custom_call_target="tpu_custom_call" | custom-call | flops 1 | bytes 1 | tf_op jit(solution)/shard_map/pallas_call | solution.py:584
  403.5 8.2 %shard_map.216.a_ref = bf16[512,2048]{1,0:T(8,128)(2,1)S(1)} custom-call(s32[2]{0:T(128)S(1)} %pad_add_fusion.own_ref, bf16[1024,1280]{1,0:T(8,128)(2,1)S(1)} %copy-done, bf16[1024,1280]{1,0:T(8,128)(2,1)} %get-tuple-element.228.refs_1_.pre_ref, bf16[1024,2048]{1,0:T(8,128)(2,1)} %get-tuple-element.236.refs_9_.refs_2_.refs_4_, ...), custom_call_target="tpu_custom_call" | custom-call | flops 1 | bytes 1 | tf_op jit(solution)/shard_map/pallas_call | solution.py:584
  411.7 16.1 %shard_map.217 = (bf16[2,256,2048]{2,1,0:T(8,128)(2,1)S(1)}, bf16[2,256,2048]{2,1,0:T(8,128)(2,1)S(1)}) custom-call(s32[2]{0:T(128)S(1)} %pad_add_fusion.own_ref, bf16[1024,1024]{1,0:T(8,128)(2,1)} %get-tuple-element.231.gate_ref, bf16[1024,1280]{1,0:T(8,128)(2,1)} %get-tuple-element.227.refs_0_.pre_ref, ...), custom_call_target="tpu_custom_call" | custom-call | flops 1 | bytes 1 | tf_op jit(solution)/shard_map/pallas_call | solution.py:584
  430.4 16.0 %shard_map.218 = (bf16[2,256,2048]{2,1,0:T(8,128)(2,1)S(1)}, bf16[2,256,2048]{2,1,0:T(8,128)(2,1)S(1)}) custom-call(s32[2]{0:T(128)S(1)} %pad_add_fusion.own_ref, bf16[1024,1024]{1,0:T(8,128)(2,1)} %get-tuple-element.233.gate_ref, bf16[1024,1280]{1,0:T(8,128)(2,1)} %get-tuple-element.228.refs_1_.pre_ref, bf16[1024,128]{1,0:T(8,128)(2,1)S(1)} %copy-done.57, ...), custom_call_target="tpu_custom_call" | custom-call | flops 1 | bytes 1 | tf_op jit(solution)/shard_map/pallas_call | solution.py:584
  456.5 8.0 %shard_map.220 = (bf16[2,320,512]{2,1,0:T(8,128)(2,1)S(1)}, bf16[2,320,512]{2,1,0:T(8,128)(2,1)S(1)}) custom-call(s32[2]{0:T(128)S(1)} %pad_add_fusion.own_ref, bf16[1024,1280]{1,0:T(8,128)(2,1)S(1)} %copy-done.1, bf16[1024,1280]{1,0:T(8,128)(2,1)} %get-tuple-element.228.refs_1_.pre_ref, bf16[1024,128]{1,0:T(8,128)(2,1)S(1)} %get-tuple-element.222.dt_ref.refs_2_, ...), custom_call_target="tpu_custom_call" | custom-call | flops 1 | bytes 1 | tf_op jit(solution)/shard_map/pallas_call | solution.py:584
  482.6 7.8 %shard_map.221 = (bf16[2,256,2048]{2,1,0:T(8,128)(2,1)S(1)}, bf16[2,256,2048]{2,1,0:T(8,128)(2,1)S(1)}) custom-call(s32[2]{0:T(128)S(1)} %pad_add_fusion.own_ref, bf16[1024,1024]{1,0:T(8,128)(2,1)} %copy-done.25, bf16[1024,2048]{1,0:T(8,128)(2,1)} %b_ref.3), custom_call_target="tpu_custom_call" | custom-call | flops 1 | bytes 1 | tf_op jit(solution)/shard_map/pallas_call | solution.py:584
  610.4 18.0 %collective-permute-done.48.got_ref = bf16[256,2048]{1,0:T(8,128)(2,1)} collective-permute-done((bf16[256,2048]{1,0:T(8,128)(2,1)}, bf16[256,2048]{1,0:T(8,128)(2,1)}, u32[]{:S(2)}, u32[]{:S(2)}) %collective-permute-start.48) | collective-permute-done | bytes 1048608 | tf_op jit(solution)/shard_map/mixed/fsdp_2/ppermute | solution.py:28
  646.2 11.0 %all-gather.11.cloned.1.call-done = bf16[32,128,512]{2,1,0:T(8,128)(2,1)} async-done(((bf16[4,128,512]{2,1,0:T(8,128)(2,1)}), bf16[32,128,512]{2,1,0:T(8,128)(2,1)}) %all-gather.11.cloned.1.call-update) | async-done | bytes 4194320 | tf_op jit(solution)/shard_map/all_gather | solution.py:171
  (474 shorter events, 270.3 us)
Async XLA Ops:
  7.2 342.2 %reduce-scatter.4.cloned.1.call-start = ((), (), s32[]{:S(2)}) async-start(), calls=%async_computation.3 | async-start | bytes 4718592 | tf_op jit(solution)/shard_map/reduce_scatter | solution.py:165
  9.7 28.4 %collective-permute-start = (bf16[2,512,512]{2,1,0:T(8,128)(2,1)}, bf16[2,512,512]{2,1,0:T(8,128)(2,1)}, u32[]{:S(2)}, u32[]{:S(2)}) collective-permute-start(bf16[2,512,512]{2,1,0:T(8,128)(2,1)} %pad_maximum_fusion.4), channel_id=1, source_target_pairs={{0,2},{1,3},{2,0},{3,1},{4,6},{5,7},{6,4},{7,5},{8,10},{9,11},{10,... | collective-permute-start | bytes 3145736 | tf_op jit(solution)/shard_map/weights/fsdp_2/ppermute | solution.py:28
  38.1 28.5 %collective-permute-start.7 = (bf16[256,2048]{1,0:T(8,128)(2,1)S(1)}, bf16[256,2048]{1,0:T(8,128)(2,1)}, u32[]{:S(2)}, u32[]{:S(2)}) collective-permute-start(bf16[256,2048]{1,0:T(8,128)(2,1)S(1)} %get-tuple-element.166.refs_0_.tok_ref), channel_id=1, source_target_pairs={{0,2},{1,3},{2,0},{3,1},{4,6},{5,7},{6,4},{7,5},{8,10},{9,11},{10,... | collective-permute-start | bytes 3145736 | tf_op jit(solution)/shard_map/weights/fsdp_2/ppermute | solution.py:28
  39.9 25.6 %collective-permute-start.10 = (bf16[2,512,512]{2,1,0:T(8,128)(2,1)}, bf16[2,512,512]{2,1,0:T(8,128)(2,1)}, u32[]{:S(2)}, u32[]{:S(2)}) collective-permute-start(bf16[2,512,512]{2,1,0:T(8,128)(2,1)} %collective-permute-done), channel_id=1, source_target_pairs={{0,8},{4,12},{8,0},{12,4},{16,24},{20,28},{24,16},{28,20},{1,9},{5... | collective-permute-start | bytes 3145736 | tf_op jit(solution)/shard_map/weights/group_2/ppermute | solution.py:28
  41.5 26.7 %collective-permute-start.9 = (bf16[2,512,512]{2,1,0:T(8,128)(2,1)}, bf16[2,512,512]{2,1,0:T(8,128)(2,1)}, u32[]{:S(2)}, u32[]{:S(2)}) collective-permute-start(bf16[2,512,512]{2,1,0:T(8,128)(2,1)} %collective-permute-done), channel_id=1, source_target_pairs={{0,4},{4,0},{8,12},{12,8},{16,20},{20,16},{24,28},{28,24},{1,5},{5... | collective-permute-start | bytes 3145736 | tf_op jit(solution)/shard_map/weights/group_1/ppermute | solution.py:28
  44.6 27.0 %collective-permute-start.1 = (bf16[320,512]{1,0:T(8,128)(2,1)S(1)}, bf16[320,512]{1,0:T(8,128)(2,1)S(1)}, u32[]{:S(2)}, u32[]{:S(2)}) collective-permute-start(bf16[320,512]{1,0:T(8,128)(2,1)S(1)} %slice.170.refs_8_.refs_4_), channel_id=1, source_target_pairs={{0,2},{1,3},{2,0},{3,1},{4,6},{5,7},{6,4},{7,5},{8,10},{9,11},{10,... | collective-permute-start | bytes 983048 | tf_op jit(solution)/shard_map/weights/fsdp_2/ppermute | solution.py:28
  87.4 30.0 %collective-permute-start.17 = (bf16[256,2048]{1,0:T(8,128)(2,1)S(1)}, bf16[256,2048]{1,0:T(8,128)(2,1)S(1)}, u32[]{:S(2)}, u32[]{:S(2)}) collective-permute-start(bf16[256,2048]{1,0:T(8,128)(2,1)S(1)} %get-tuple-element.180.refs_0_.tok_ref), channel_id=1, source_target_pairs={{0,2},{1,3},{2,0},{3,1},{4,6},{5,7},{6,4},{7,5},{8,10},{9,11},{10,... | collective-permute-start | bytes 3145736 | tf_op jit(solution)/shard_map/weights/fsdp_2/ppermute | solution.py:28
  143.6 35.0 %collective-permute-start.25 = (bf16[256,2048]{1,0:T(8,128)(2,1)S(1)}, bf16[256,2048]{1,0:T(8,128)(2,1)S(1)}, u32[]{:S(2)}, u32[]{:S(2)}) collective-permute-start(bf16[256,2048]{1,0:T(8,128)(2,1)S(1)} %get-tuple-element.196.refs_0_.cot_ref), channel_id=1, source_target_pairs={{0,2},{1,3},{2,0},{3,1},{4,6},{5,7},{6,4},{7,5},{8,10},{9,11},{10,... | collective-permute-start | bytes 3145736 | tf_op jit(solution)/shard_map/fsdp_2/ppermute | solution.py:28
  179.1 35.5 %collective-permute-start.22 = (f32[8,2,128]{2,1,0:T(2,128)S(1)}, f32[8,2,128]{2,1,0:T(2,128)S(1)}, u32[]{:S(2)}, u32[]{:S(2)}) collective-permute-start(f32[8,2,128]{2,1,0:T(2,128)S(1)} %slice.149), channel_id=1, source_target_pairs={{0,1},{1,0},{2,3},{3,2},{4,5},{5,4},{6,7},{7,6},{8,9},{9,8},{10,11... | collective-permute-start | bytes 24584 | tf_op jit(solution)/shard_map/fsdp_1/ppermute | solution.py:28
  248.8 153.1 %reduce-scatter.6.cloned.1.call-start = ((), (), s32[]{:S(2)}) async-start(), calls=%async_computation.4 | async-start | bytes 2621440 | tf_op jit(solution)/shard_map/reduce_scatter | solution.py:165
  258.1 66.8 %collective-permute-start.29 = (bf16[512,2048]{1,0:T(8,128)(2,1)S(1)}, bf16[512,2048]{1,0:T(8,128)(2,1)S(1)}, u32[]{:S(2)}, u32[]{:S(2)}) collective-permute-start(bf16[512,2048]{1,0:T(8,128)(2,1)S(1)} %shard_map.210), channel_id=1, source_target_pairs={{0,4},{4,0},{8,12},{12,8},{16,20},{20,16},{24,28},{28,24},{1,5},{5... | collective-permute-start | bytes 6291464 | tf_op jit(solution)/shard_map/away_out/group_1/ppermute | solution.py:28
  349.4 106.4 %all-gather.7.cloned.1.call-start = ((), (), s32[]{:S(2)}) async-start(), calls=%async_computation.6 | async-start | bytes 2621440 | tf_op jit(solution)/shard_map/all_gather | solution.py:171
  351.1 37.8 %collective-permute-start.30 = (bf16[2,128,512]{2,1,0:T(8,128)(2,1)S(1)}, bf16[2,128,512]{2,1,0:T(8,128)(2,1)S(1)}, u32[]{:S(2)}, u32[]{:S(2)}) collective-permute-start(bf16[2,128,512]{2,1,0:T(8,128)(2,1)S(1)} %trade_gate.3), channel_id=1, source_target_pairs={{0,2},{1,3},{2,0},{3,1},{4,6},{5,7},{6,4},{7,5},{8,10},{9,11},{10,... | collective-permute-start | bytes 786440 | tf_op jit(solution)/shard_map/trade_gate/fsdp_2/ppermute | solution.py:28
  401.9 104.0 %reduce-scatter.8.cloned.1.call-start = ((), (), s32[]{:S(2)}) async-start(), calls=%async_computation.5 | async-start | bytes 2621440 | tf_op jit(solution)/shard_map/reduce_scatter | solution.py:165
  401.9 47.9 %collective-permute-start.32 = (bf16[512,2048]{1,0:T(8,128)(2,1)}, bf16[512,2048]{1,0:T(8,128)(2,1)S(1)}, u32[]{:S(2)}, u32[]{:S(2)}) collective-permute-start(bf16[512,2048]{1,0:T(8,128)(2,1)} %copy-done.33), channel_id=1, source_target_pairs={{0,4},{4,0},{8,12},{12,8},{16,20},{20,16},{24,28},{28,24},{1,5},{5... | collective-permute-start | bytes 6291464 | tf_op jit(solution)/shard_map/away_heads/group_1/ppermute | solution.py:28
  455.9 112.5 %all-gather.9.cloned.1.call-start = ((), (), s32[]{:S(2)}) async-start(), calls=%async_computation.7 | async-start | bytes 2621440 | tf_op jit(solution)/shard_map/all_gather | solution.py:171
  464.8 61.2 %collective-permute-start.39 = (bf16[4,4,128,512]{3,2,1,0:T(8,128)(2,1)}, bf16[4,4,128,512]{3,2,1,0:T(8,128)(2,1)}, u32[]{:S(2)}, u32[]{:S(2)}) collective-permute-start(bf16[4,4,128,512]{3,2,1,0:T(8,128)(2,1)} %bitcast.47.part_ref), channel_id=1, source_target_pairs={{0,4},{4,0},{8,12},{12,8},{16,20},{20,16},{24,28},{28,24},{1,5},{5... | collective-permute-start | bytes 6291464 | tf_op jit(solution)/shard_map/gate_lines/group_1/ppermute | solution.py:28
  477.5 33.6 %collective-permute-start.40 = (bf16[320,512]{1,0:T(8,128)(2,1)S(1)}, bf16[320,512]{1,0:T(8,128)(2,1)S(1)}, u32[]{:S(2)}, u32[]{:S(2)}) collective-permute-start(bf16[320,512]{1,0:T(8,128)(2,1)S(1)} %get-tuple-element.338), channel_id=1, source_target_pairs={{0,16},{4,20},{8,24},{12,28},{16,0},{20,4},{24,8},{28,12},{1,17},{... | collective-permute-start | bytes 983048 | tf_op jit(solution)/shard_map/tail/group_4/ppermute | solution.py:28
  479.8 46.2 %collective-permute-start.38 = (bf16[256,2048]{1,0:T(8,128)(2,1)}, bf16[256,2048]{1,0:T(8,128)(2,1)}, u32[]{:S(2)}, u32[]{:S(2)}) collective-permute-start(bf16[256,2048]{1,0:T(8,128)(2,1)} %get-tuple-element.247), channel_id=1, source_target_pairs={{0,2},{1,3},{2,0},{3,1},{4,6},{5,7},{6,4},{7,5},{8,10},{9,11},{10,... | collective-permute-start | bytes 3145736 | tf_op jit(solution)/shard_map/into/fsdp_2/ppermute | solution.py:28
  480.9 53.2 %collective-permute-start.42 = (bf16[256,2048]{1,0:T(8,128)(2,1)}, bf16[256,2048]{1,0:T(8,128)(2,1)}, u32[]{:S(2)}, u32[]{:S(2)}) collective-permute-start(bf16[256,2048]{1,0:T(8,128)(2,1)} %get-tuple-element.251), channel_id=1, source_target_pairs={{0,2},{1,3},{2,0},{3,1},{4,6},{5,7},{6,4},{7,5},{8,10},{9,11},{10,... | collective-permute-start | bytes 3145736 | tf_op jit(solution)/shard_map/into/fsdp_2/ppermute | solution.py:28
  505.9 151.3 %all-gather.11.cloned.1.call-start = ((), (), s32[]{:S(2)}) async-start(), calls=%async_computation.8 | async-start | bytes 4718592 | tf_op jit(solution)/shard_map/all_gather | solution.py:171
  569.0 70.2 %collective-permute-start.54 = (bf16[4,128,2048]{2,1,0:T(8,128)(2,1)}, bf16[4,128,2048]{2,1,0:T(8,128)(2,1)}, u32[]{:S(2)}, u32[]{:S(2)}) collective-permute-start(bf16[4,128,2048]{2,1,0:T(8,128)(2,1)} %bitcast.142), channel_id=1, source_target_pairs={{0,4},{4,0},{8,12},{12,8},{16,20},{20,16},{24,28},{28,24},{1,5},{5... | collective-permute-start | bytes 6291464 | tf_op jit(solution)/shard_map/out_lines/group_1/ppermute | solution.py:28
  580.4 26.3 %collective-permute-start.45 = (bf16[256,2048]{1,0:T(8,128)(2,1)}, bf16[256,2048]{1,0:T(8,128)(2,1)}, u32[]{:S(2)}, u32[]{:S(2)}) collective-permute-start(bf16[256,2048]{1,0:T(8,128)(2,1)} %get-tuple-element.276), channel_id=1, source_target_pairs={{0,2},{1,3},{2,0},{3,1},{4,6},{5,7},{6,4},{7,5},{8,10},{9,11},{10,... | collective-permute-start | bytes 3145736 | tf_op jit(solution)/shard_map/mixed/fsdp_2/ppermute | solution.py:28
  587.8 40.6 %collective-permute-start.48 = (bf16[256,2048]{1,0:T(8,128)(2,1)}, bf16[256,2048]{1,0:T(8,128)(2,1)}, u32[]{:S(2)}, u32[]{:S(2)}) collective-permute-start(bf16[256,2048]{1,0:T(8,128)(2,1)} %get-tuple-element.284), channel_id=1, source_target_pairs={{0,2},{1,3},{2,0},{3,1},{4,6},{5,7},{6,4},{7,5},{8,10},{9,11},{10,... | collective-permute-start | bytes 3145736 | tf_op jit(solution)/shard_map/mixed/fsdp_2/ppermute | solution.py:28
  (153 other events, 1775.1 us)
Sparse Core Ops, SparseCore 0:
  248.3 101.0 reduce-scatter.3
  351.8 43.6 reduce-scatter.5
  402.0 44.9 all-gather.6
  456.0 49.8 reduce-scatter.7
  507.4 50.8 all-gather.8
  568.5 88.6 all-gather.10

commit v6 on v5

--- a/solution.py
+++ b/solution.py
@@ -46,7 +46,7 @@
 
 def gather_near(held, *later):
     for r, part in list(held.items()):
-        held[r ^ 1] = swap(after(part, *later), "fsdp", 1)
+        held[r ^ 1] = swap(after(part, *later) if r else part, "fsdp", 1)
     return [held[r] for r in range(len(held))]
 
 
@@ -1037,7 +1037,7 @@
 
     grad_gain_ref[...] = jnp.zeros_like(grad_gain_ref)
 
-    def step(t, carry):
+    def step(t):
         place = lax.bitwise_xor(t // per_part, own_ref[0]) * per_part + t % per_part
         rows = pl.ds(pl.multiple_of(place * chunk, chunk), chunk)
         for m in range(micro):
@@ -1063,9 +1063,9 @@
                 ).astype(BF16)
                 gated_all[m][rows, lanes] = (scaled * gain).astype(BF16)
                 grad_gain_ref[0:1, lanes] += jnp.sum(scaled * grad, axis=0, keepdims=True)
-        return carry
-
-    lax.fori_loop(0, count, step, 0)
+
+    for t in range(count):
+        step(t)
 
     terms = [dot(a[...], b[...], TN) for a, b in zip(grad_gate, normed)]
     out_ref[...] = sum(terms[1:], terms[0]).astype(BF16).reshape(out_ref.shape)
@@ -1370,7 +1370,7 @@
     grad_tok = []
     grad_norm = jnp.zeros((width,), F32)
     for m in range(micro):
-        terms = into[m].final(sent, got_lines, steps[min(m + 1, len(steps) - 1)])
+        terms = into[m].final(sent, got_lines, *(steps[2:3] if m else []))
         tok, gain = norm_rows(own_arg, tokens[m, 0], cotangent[m, 0], gain_norm, terms)
         grad_tok.append(tok)
         grad_norm += gain[0]

time: 677 us -> 674 us (level)
  transfers between devices with their start and end apart: 61 -> 61, of which waited for: 34 -> 32; matrix products, arithmetic and copies ran while one was open for 6% -> 6% of each run, Pallas kernels for 45% -> 45%
where the time goes in v6:
time: 674 us; the launch traced here: 670 us
  Pallas kernels  329 us (49%)
  waiting for transfers between devices  184 us (27%)
  local copies, waits for them, and re-layouts  73.5 us (11%)
  starting transfers between devices  41.2 us (6%)
  other arithmetic  26 us (4%)
  between operations  15.9 us (2%)
    pallas_call x31, Pallas kernels, call(): pl.pallas_call(kernel, grid_spec=pltpu.PrefetchScalarGridSpec(num_scalar_...  210 us
    ppermute x55, waiting for transfers between devices, swap(): return lax.ppermute(value, axis, [(i, i ^ bit) for i in range(count)])  152 us
    pallas_call x2, Pallas kernels, scan_back(): backward(own_arg, act, slope, pre, tail, dt_raw, after(grad_ssm[m], *earl...  62.5 us
    unnamed x228, local copies, waits for them, and re-layouts  54 us
    ppermute x55, starting transfers between devices, swap(): return lax.ppermute(value, axis, [(i, i ^ bit) for i in range(count)])  41 us
    pallas_call x2, Pallas kernels, on_device(): forward(own_arg, pre, tail, gate, dt_raw, back, seg_rows[m], taps, head_r...  39.1 us
    reduce_scatter x3, waiting for transfers between devices, scatter(): lax.psum_scatter(self.order(value), 'group', scatter_dimension=0, axis_in...  20.9 us
    pallas_call x4, Pallas kernels, fill(): pl.pallas_call(fill_kernel, grid_spec=pltpu.PrefetchScalarGridSpec(num_sc...  17.4 us
  transfers between devices with their start and end apart: 61, of which 32 were waited for; matrix products, arithmetic and copies ran while one was open for 6% of the time, Pallas kernels for 45%

profile of v6, /device:TPU:0, one launch (start us, length us, event | category | flops | bytes accessed | tf_op | source)
XLA Modules:
  0.0 669.5 jit_solution(149801583240791743)
XLA Ops:
  20.7 15.9 %collective-permute-done.5 = f32[6464]{0:T(1024)S(1)} collective-permute-done((f32[6464]{0:T(1024)S(1)}, f32[6464]{0:T(1024)S(1)}, u32[]{:S(2)}, u32[]{:S(2)}) %collective-permute-start.5) | collective-permute-done | bytes 25888 | tf_op jit(solution)/shard_map/weights/fsdp_2/ppermute | solution.py:28
  43.6 21.9 %collective-permute-done.10 = bf16[2,512,512]{2,1,0:T(8,128)(2,1)} collective-permute-done((bf16[2,512,512]{2,1,0:T(8,128)(2,1)}, bf16[2,512,512]{2,1,0:T(8,128)(2,1)}, u32[]{:S(2)}, u32[]{:S(2)}) %collective-permute-start.10) | collective-permute-done | bytes 1048608 | tf_op jit(solution)/shard_map/weights/group_2/ppermute | solution.py:28
  73.1 7.9 %collective-permute-done.3.refs_10_.refs_6_ = bf16[320,512]{1,0:T(8,128)(2,1)S(1)} collective-permute-done((bf16[320,512]{1,0:T(8,128)(2,1)S(1)}, bf16[320,512]{1,0:T(8,128)(2,1)S(1)}, u32[]{:S(2)}, u32[]{:S(2)}) %collective-permute-start.3) | collective-permute-done | bytes 327712 | tf_op jit(solution)/shard_map/weights/fsdp_2/ppermute | solution.py:28
  98.5 21.1 %shard_map.203 = (bf16[1024,2048]{1,0:T(8,128)(2,1)}, bf16[1024,1024]{1,0:T(8,128)(2,1)}, bf16[1024,1024]{1,0:T(8,128)(2,1)}, bf16[1024,256]{1,0:T(8,128)(2,1)S(1)}, f32[1024,128]{1,0:T(8,128)S(1)}) custom-call(s32[2]{0:T(128)S(1)} %pad_add_fusion.own_ref, bf16[256,2048]{1,0:T(8,128)(2,1)S(1)} %get-tuple-element.157.refs_0_.tok_ref, ...), custom_call_target="tpu_custom_call" | custom-call | flops 1 | bytes 1 | tf_op jit(solution)/shard_map/pallas_call | solution.py:584
  123.3 21.1 %shard_map.204 = (bf16[1024,2048]{1,0:T(8,128)(2,1)}, bf16[1024,1024]{1,0:T(8,128)(2,1)}, bf16[1024,1024]{1,0:T(8,128)(2,1)}, bf16[1024,256]{1,0:T(8,128)(2,1)S(1)}, f32[1024,128]{1,0:T(8,128)S(1)}) custom-call(s32[2]{0:T(128)S(1)} %pad_add_fusion.own_ref, bf16[256,2048]{1,0:T(8,128)(2,1)S(1)} %get-tuple-element.171.refs_0_.tok_ref, ...), custom_call_target="tpu_custom_call" | custom-call | flops 1 | bytes 1 | tf_op jit(solution)/shard_map/pallas_call | solution.py:584
  147.9 9.1 %shard_map.205 = (bf16[1024,2048]{1,0:T(8,128)(2,1)}, bf16[1024,1024]{1,0:T(8,128)(2,1)}) custom-call(s32[2]{0:T(128)S(1)} %pad_add_fusion.own_ref, bf16[256,2048]{1,0:T(8,128)(2,1)S(1)} %get-tuple-element.170.refs_0_.cot_ref, bf16[256,2048]{1,0:T(8,128)(2,1)S(1)} %collective-permute-done.16.refs_1_, bf16[256,2048]{1,0:T(8,128)(2,1)S(1)} %collective-permute-done.17.refs_2_, ...), custom_call_target="tpu_custom_call" | custom-call | flops 1 | bytes 1 | tf_op jit(solution)/shard_map/pallas_call | solution.py:584
  157.0 19.6 %shard_map.206 = (bf16[1024,1280]{1,0:T(8,128)(2,1)}, bf16[1024,1280]{1,0:T(8,128)(2,1)}, bf16[1024,1024]{1,0:T(8,128)(2,1)S(1)}, bf16[1024,1024]{1,0:T(8,128)(2...) custom-call(s32[2]{0:T(128)S(1)} %pad_add_fusion.own_ref, ...), custom_call_target="tpu_custom_call" | custom-call | flops 1 | bytes 1 | tf_op jit(solution)/shard_map/pallas_call | solution.py:1268
  182.0 9.5 %shard_map.207 = (bf16[1024,2048]{1,0:T(8,128)(2,1)}, bf16[1024,1024]{1,0:T(8,128)(2,1)}) custom-call(s32[2]{0:T(128)S(1)} %pad_add_fusion.own_ref, bf16[256,2048]{1,0:T(8,128)(2,1)S(1)} %get-tuple-element.186.refs_0_.cot_ref, bf16[256,2048]{1,0:T(8,128)(2,1)S(1)} %collective-permute-done.24.refs_1_, bf16[256,2048]{1,0:T(8,128)(2,1)S(1)} %collective-permute-done.25.refs_2_, ...), custom_call_target="tpu_custom_call" | custom-call | flops 1 | bytes 1 | tf_op jit(solution)/shard_map/pallas_call | solution.py:584
  191.5 19.6 %shard_map.208 = (bf16[1024,1280]{1,0:T(8,128)(2,1)}, bf16[1024,1280]{1,0:T(8,128)(2,1)}, bf16[1024,1024]{1,0:T(8,128)(2,1)S(1)}, bf16[1024,1024]{1,0:T(8,128)(2...) custom-call(s32[2]{0:T(128)S(1)} %pad_add_fusion.own_ref, ...), custom_call_target="tpu_custom_call" | custom-call | flops 1 | bytes 1 | tf_op jit(solution)/shard_map/pallas_call | solution.py:1268
  219.2 24.4 %shard_map.209 = (bf16[1024,1024]{1,0:T(8,128)(2,1)S(1)}, bf16[1024,1024]{1,0:T(8,128)(2,1)S(1)}, bf16[1024,1024]{1,0:T(8,128)(2,1)}, bf16[1024,1024]{1,0:T(8,12...) custom-call(s32[2]{0:T(128)S(1)} %pad_add_fusion.own_ref, ...), custom_call_target="tpu_custom_call" | custom-call | flops 1 | bytes 1 | tf_op jit(solution)/shard_map/pallas_call | solution.py:584
  247.8 8.3 %shard_map.210 = bf16[512,2048]{1,0:T(8,128)(2,1)S(1)} custom-call(s32[2]{0:T(128)S(1)} %pad_add_fusion.own_ref, bf16[1024,1024]{1,0:T(8,128)(2,1)S(1)} %copy-done.14, bf16[1024,1024]{1,0:T(8,128)(2,1)} %get-tuple-element.200.refs_1_, bf16[1024,2048]{1,0:T(8,128)(2,1)} %get-tuple-element.197.refs_2_, bf16[1024,2048]{1,0:T(8,128)(2,1)} %get-tuple-element.198.refs_3_), custom_call_target="tpu_custom_call" | custom-call | flops 1 | bytes 1 | tf_op jit(solution)/shard_map/pallas_call | solution.py:584
  256.7 8.5 %shard_map.211.a_ref = bf16[512,2048]{1,0:T(8,128)(2,1)S(1)} custom-call(s32[2]{0:T(128)S(1)} %pad_add_fusion.own_ref, bf16[1024,1024]{1,0:T(8,128)(2,1)S(1)} %copy-done.14, bf16[1024,1024]{1,0:T(8,128)(2,1)} %get-tuple-element.200.refs_1_, bf16[1024,2048]{1,0:T(8,128)(2,1)} %get-tuple-element.197.refs_2_, bf16[1024,2048]{1,0:T(8,128)(2,1)} %get-tuple-element.198.refs_3_), custom_call_target="tpu_custom_call" | custom-call | flops 1 | bytes 1 | tf_op jit(solution)/shard_map/pallas_call | solution.py:584
  265.2 31.3 %shard_map.212 = (bf16[1024,1280]{1,0:T(8,128)(2,1)}, bf16[1024,128]{1,0:T(8,128)(2,1)S(1)}, f32[8,1280]{1,0:T(8,128)S(1)}, f32[8,1024]{1,0:T(8,128)S(1)}, f32[8,128]{1,0:T(8,128)S(1)}) custom-call(s32[2]{0:T(128)S(1)} %pad_add_fusion.own_ref, bf16[1024,1280]{1,0:T(8,128)(2,1)} %get-tuple-element.179.act_ref, ...), custom_call_target="tpu_custom_call" | custom-call | flops 1 | bytes 1 | tf_op jit(solution)/shard_map/pallas_call | solution.py:1279
  298.4 24.4 %collective-permute-done.29.b_ref = bf16[512,2048]{1,0:T(8,128)(2,1)S(1)} collective-permute-done((bf16[512,2048]{1,0:T(8,128)(2,1)S(1)}, bf16[512,2048]{1,0:T(8,128)(2,1)S(1)}, u32[]{:S(2)}, u32[]{:S(2)}) %collective-permute-start.29) | collective-permute-done | bytes 2097184 | tf_op jit(solution)/shard_map/away_out/group_1/ppermute | solution.py:28
  328.6 18.8 %reduce-scatter.4.cloned.1.call-done = bf16[1,128,2048]{2,1,0:T(8,128)(2,1)} async-done(((bf16[8,128,2048]{2,1,0:T(8,128)(2,1)}), bf16[1,128,2048]{2,1,0:T(8,128)(2,1)}) %reduce-scatter.4.cloned.1.call-update) | async-done | bytes 524304 | tf_op jit(solution)/shard_map/reduce_scatter | solution.py:165
  355.5 31.1 %shard_map.214 = (bf16[1024,1280]{1,0:T(8,128)(2,1)}, bf16[1024,128]{1,0:T(8,128)(2,1)S(1)}, f32[8,1280]{1,0:T(8,128)S(1)}, f32[8,1024]{1,0:T(8,128)S(1)}, f32[8,128]{1,0:T(8,128)S(1)}) custom-call(s32[2]{0:T(128)S(1)} %pad_add_fusion.own_ref, bf16[1024,1280]{1,0:T(8,128)(2,1)} %get-tuple-element.204.act_ref, ...), custom_call_target="tpu_custom_call" | custom-call | flops 1 | bytes 1 | tf_op jit(solution)/shard_map/pallas_call | solution.py:1279
  390.3 8.0 %shard_map.215 = bf16[512,2048]{1,0:T(8,128)(2,1)S(1)} custom-call(s32[2]{0:T(128)S(1)} %pad_add_fusion.own_ref, bf16[1024,1280]{1,0:T(8,128)(2,1)S(1)} %copy-done, bf16[1024,1280]{1,0:T(8,128)(2,1)} %get-tuple-element.218.refs_1_.pre_ref, bf16[1024,2048]{1,0:T(8,128)(2,1)} %get-tuple-element.226.refs_9_.refs_2_.refs_4_, ...), custom_call_target="tpu_custom_call" | custom-call | flops 1 | bytes 1 | tf_op jit(solution)/shard_map/pallas_call | solution.py:584
  401.2 8.4 %shard_map.216.a_ref = bf16[512,2048]{1,0:T(8,128)(2,1)S(1)} custom-call(s32[2]{0:T(128)S(1)} %pad_add_fusion.own_ref, bf16[1024,1280]{1,0:T(8,128)(2,1)S(1)} %copy-done, bf16[1024,1280]{1,0:T(8,128)(2,1)} %get-tuple-element.218.refs_1_.pre_ref, bf16[1024,2048]{1,0:T(8,128)(2,1)} %get-tuple-element.226.refs_9_.refs_2_.refs_4_, ...), custom_call_target="tpu_custom_call" | custom-call | flops 1 | bytes 1 | tf_op jit(solution)/shard_map/pallas_call | solution.py:584
  409.7 16.1 %shard_map.217 = (bf16[2,256,2048]{2,1,0:T(8,128)(2,1)S(1)}, bf16[2,256,2048]{2,1,0:T(8,128)(2,1)S(1)}) custom-call(s32[2]{0:T(128)S(1)} %pad_add_fusion.own_ref, bf16[1024,1024]{1,0:T(8,128)(2,1)} %get-tuple-element.221.gate_ref, bf16[1024,1280]{1,0:T(8,128)(2,1)} %get-tuple-element.217.refs_0_.pre_ref, ...), custom_call_target="tpu_custom_call" | custom-call | flops 1 | bytes 1 | tf_op jit(solution)/shard_map/pallas_call | solution.py:584
  428.4 16.0 %shard_map.218 = (bf16[2,256,2048]{2,1,0:T(8,128)(2,1)S(1)}, bf16[2,256,2048]{2,1,0:T(8,128)(2,1)S(1)}) custom-call(s32[2]{0:T(128)S(1)} %pad_add_fusion.own_ref, bf16[1024,1024]{1,0:T(8,128)(2,1)} %get-tuple-element.223.gate_ref, bf16[1024,1280]{1,0:T(8,128)(2,1)} %get-tuple-element.218.refs_1_.pre_ref, bf16[1024,128]{1,0:T(8,128)(2,1)S(1)} %copy-done.57, ...), custom_call_target="tpu_custom_call" | custom-call | flops 1 | bytes 1 | tf_op jit(solution)/shard_map/pallas_call | solution.py:584
  454.3 7.9 %shard_map.220 = (bf16[2,320,512]{2,1,0:T(8,128)(2,1)S(1)}, bf16[2,320,512]{2,1,0:T(8,128)(2,1)S(1)}) custom-call(s32[2]{0:T(128)S(1)} %pad_add_fusion.own_ref, bf16[1024,1280]{1,0:T(8,128)(2,1)S(1)} %copy-done.1, bf16[1024,1280]{1,0:T(8,128)(2,1)} %get-tuple-element.218.refs_1_.pre_ref, bf16[1024,128]{1,0:T(8,128)(2,1)S(1)} %get-tuple-element.212.dt_ref.refs_2_, ...), custom_call_target="tpu_custom_call" | custom-call | flops 1 | bytes 1 | tf_op jit(solution)/shard_map/pallas_call | solution.py:584
  480.3 7.8 %shard_map.221 = (bf16[2,256,2048]{2,1,0:T(8,128)(2,1)S(1)}, bf16[2,256,2048]{2,1,0:T(8,128)(2,1)S(1)}) custom-call(s32[2]{0:T(128)S(1)} %pad_add_fusion.own_ref, bf16[1024,1024]{1,0:T(8,128)(2,1)} %copy-done.25, bf16[1024,2048]{1,0:T(8,128)(2,1)} %b_ref.3), custom_call_target="tpu_custom_call" | custom-call | flops 1 | bytes 1 | tf_op jit(solution)/shard_map/pallas_call | solution.py:584
  608.2 18.0 %collective-permute-done.48.got_ref = bf16[256,2048]{1,0:T(8,128)(2,1)} collective-permute-done((bf16[256,2048]{1,0:T(8,128)(2,1)}, bf16[256,2048]{1,0:T(8,128)(2,1)}, u32[]{:S(2)}, u32[]{:S(2)}) %collective-permute-start.48) | collective-permute-done | bytes 1048608 | tf_op jit(solution)/shard_map/mixed/fsdp_2/ppermute | solution.py:28
  644.0 11.0 %all-gather.11.cloned.1.call-done = bf16[32,128,512]{2,1,0:T(8,128)(2,1)} async-done(((bf16[4,128,512]{2,1,0:T(8,128)(2,1)}), bf16[32,128,512]{2,1,0:T(8,128)(2,1)}) %all-gather.11.cloned.1.call-update) | async-done | bytes 4194320 | tf_op jit(solution)/shard_map/all_gather | solution.py:171
  (473 shorter events, 268.0 us)
Async XLA Ops:
  7.2 340.2 %reduce-scatter.4.cloned.1.call-start = ((), (), s32[]{:S(2)}) async-start(), calls=%async_computation.3 | async-start | bytes 4718592 | tf_op jit(solution)/shard_map/reduce_scatter | solution.py:165
  9.7 28.4 %collective-permute-start = (bf16[2,512,512]{2,1,0:T(8,128)(2,1)}, bf16[2,512,512]{2,1,0:T(8,128)(2,1)}, u32[]{:S(2)}, u32[]{:S(2)}) collective-permute-start(bf16[2,512,512]{2,1,0:T(8,128)(2,1)} %pad_maximum_fusion.4), channel_id=1, source_target_pairs={{0,2},{1,3},{2,0},{3,1},{4,6},{5,7},{6,4},{7,5},{8,10},{9,11},{10,... | collective-permute-start | bytes 3145736 | tf_op jit(solution)/shard_map/weights/fsdp_2/ppermute | solution.py:28
  38.1 28.5 %collective-permute-start.2 = (bf16[256,2048]{1,0:T(8,128)(2,1)S(1)}, bf16[256,2048]{1,0:T(8,128)(2,1)}, u32[]{:S(2)}, u32[]{:S(2)}) collective-permute-start(bf16[256,2048]{1,0:T(8,128)(2,1)S(1)} %get-tuple-element.157.refs_0_.tok_ref), channel_id=1, source_target_pairs={{0,2},{1,3},{2,0},{3,1},{4,6},{5,7},{6,4},{7,5},{8,10},{9,11},{10,... | collective-permute-start | bytes 3145736 | tf_op jit(solution)/shard_map/weights/fsdp_2/ppermute | solution.py:28
  41.5 26.7 %collective-permute-start.9 = (bf16[2,512,512]{2,1,0:T(8,128)(2,1)}, bf16[2,512,512]{2,1,0:T(8,128)(2,1)}, u32[]{:S(2)}, u32[]{:S(2)}) collective-permute-start(bf16[2,512,512]{2,1,0:T(8,128)(2,1)} %collective-permute-done), channel_id=1, source_target_pairs={{0,4},{4,0},{8,12},{12,8},{16,20},{20,16},{24,28},{28,24},{1,5},{5... | collective-permute-start | bytes 3145736 | tf_op jit(solution)/shard_map/weights/group_1/ppermute | solution.py:28
  89.6 30.0 %collective-permute-start.19 = (bf16[256,2048]{1,0:T(8,128)(2,1)S(1)}, bf16[256,2048]{1,0:T(8,128)(2,1)S(1)}, u32[]{:S(2)}, u32[]{:S(2)}) collective-permute-start(bf16[256,2048]{1,0:T(8,128)(2,1)S(1)} %get-tuple-element.171.refs_0_.tok_ref), channel_id=1, source_target_pairs={{0,2},{1,3},{2,0},{3,1},{4,6},{5,7},{6,4},{7,5},{8,10},{9,11},{10,... | collective-permute-start | bytes 3145736 | tf_op jit(solution)/shard_map/weights/fsdp_2/ppermute | solution.py:28
  120.1 25.8 %collective-permute-start.16 = (bf16[256,2048]{1,0:T(8,128)(2,1)S(1)}, bf16[256,2048]{1,0:T(8,128)(2,1)S(1)}, u32[]{:S(2)}, u32[]{:S(2)}) collective-permute-start(bf16[256,2048]{1,0:T(8,128)(2,1)S(1)} %get-tuple-element.170.refs_0_.cot_ref), channel_id=1, source_target_pairs={{0,1},{1,0},{2,3},{3,2},{4,5},{5,4},{6,7},{7,6},{8,9},{9,8},{10,11... | collective-permute-start | bytes 3145736 | tf_op jit(solution)/shard_map/fsdp_1/ppermute | solution.py:28
  145.3 34.0 %collective-permute-start.25 = (bf16[256,2048]{1,0:T(8,128)(2,1)S(1)}, bf16[256,2048]{1,0:T(8,128)(2,1)S(1)}, u32[]{:S(2)}, u32[]{:S(2)}) collective-permute-start(bf16[256,2048]{1,0:T(8,128)(2,1)S(1)} %get-tuple-element.186.refs_0_.cot_ref), channel_id=1, source_target_pairs={{0,2},{1,3},{2,0},{3,1},{4,6},{5,7},{6,4},{7,5},{8,10},{9,11},{10,... | collective-permute-start | bytes 3145736 | tf_op jit(solution)/shard_map/fsdp_2/ppermute | solution.py:28
  145.6 34.2 %collective-permute-start.24 = (bf16[256,2048]{1,0:T(8,128)(2,1)S(1)}, bf16[256,2048]{1,0:T(8,128)(2,1)S(1)}, u32[]{:S(2)}, u32[]{:S(2)}) collective-permute-start(bf16[256,2048]{1,0:T(8,128)(2,1)S(1)} %get-tuple-element.186.refs_0_.cot_ref), channel_id=1, source_target_pairs={{0,1},{1,0},{2,3},{3,2},{4,5},{5,4},{6,7},{7,6},{8,9},{9,8},{10,11... | collective-permute-start | bytes 3145736 | tf_op jit(solution)/shard_map/fsdp_1/ppermute | solution.py:28
  179.4 34.4 %collective-permute-start.22 = (f32[8,2,128]{2,1,0:T(2,128)S(1)}, f32[8,2,128]{2,1,0:T(2,128)S(1)}, u32[]{:S(2)}, u32[]{:S(2)}) collective-permute-start(f32[8,2,128]{2,1,0:T(2,128)S(1)} %slice.149), channel_id=1, source_target_pairs={{0,1},{1,0},{2,3},{3,2},{4,5},{5,4},{6,7},{7,6},{8,9},{9,8},{10,11... | collective-permute-start | bytes 24584 | tf_op jit(solution)/shard_map/fsdp_1/ppermute | solution.py:28
  246.8 152.8 %reduce-scatter.6.cloned.1.call-start = ((), (), s32[]{:S(2)}) async-start(), calls=%async_computation.4 | async-start | bytes 2621440 | tf_op jit(solution)/shard_map/reduce_scatter | solution.py:165
  256.1 66.7 %collective-permute-start.29 = (bf16[512,2048]{1,0:T(8,128)(2,1)S(1)}, bf16[512,2048]{1,0:T(8,128)(2,1)S(1)}, u32[]{:S(2)}, u32[]{:S(2)}) collective-permute-start(bf16[512,2048]{1,0:T(8,128)(2,1)S(1)} %shard_map.210), channel_id=1, source_target_pairs={{0,4},{4,0},{8,12},{12,8},{16,20},{20,16},{24,28},{28,24},{1,5},{5... | collective-permute-start | bytes 6291464 | tf_op jit(solution)/shard_map/away_out/group_1/ppermute | solution.py:28
  347.4 106.2 %all-gather.7.cloned.1.call-start = ((), (), s32[]{:S(2)}) async-start(), calls=%async_computation.6 | async-start | bytes 2621440 | tf_op jit(solution)/shard_map/all_gather | solution.py:171
  349.1 37.6 %collective-permute-start.30 = (bf16[2,128,512]{2,1,0:T(8,128)(2,1)S(1)}, bf16[2,128,512]{2,1,0:T(8,128)(2,1)S(1)}, u32[]{:S(2)}, u32[]{:S(2)}) collective-permute-start(bf16[2,128,512]{2,1,0:T(8,128)(2,1)S(1)} %trade_gate.3), channel_id=1, source_target_pairs={{0,2},{1,3},{2,0},{3,1},{4,6},{5,7},{6,4},{7,5},{8,10},{9,11},{10,... | collective-permute-start | bytes 786440 | tf_op jit(solution)/shard_map/trade_gate/fsdp_2/ppermute | solution.py:28
  399.6 103.7 %reduce-scatter.8.cloned.1.call-start = ((), (), s32[]{:S(2)}) async-start(), calls=%async_computation.5 | async-start | bytes 2621440 | tf_op jit(solution)/shard_map/reduce_scatter | solution.py:165
  399.7 47.9 %collective-permute-start.32 = (bf16[512,2048]{1,0:T(8,128)(2,1)}, bf16[512,2048]{1,0:T(8,128)(2,1)S(1)}, u32[]{:S(2)}, u32[]{:S(2)}) collective-permute-start(bf16[512,2048]{1,0:T(8,128)(2,1)} %copy-done.33), channel_id=1, source_target_pairs={{0,4},{4,0},{8,12},{12,8},{16,20},{20,16},{24,28},{28,24},{1,5},{5... | collective-permute-start | bytes 6291464 | tf_op jit(solution)/shard_map/away_heads/group_1/ppermute | solution.py:28
  453.7 112.4 %all-gather.9.cloned.1.call-start = ((), (), s32[]{:S(2)}) async-start(), calls=%async_computation.7 | async-start | bytes 2621440 | tf_op jit(solution)/shard_map/all_gather | solution.py:171
  462.5 60.5 %collective-permute-start.39 = (bf16[4,4,128,512]{3,2,1,0:T(8,128)(2,1)}, bf16[4,4,128,512]{3,2,1,0:T(8,128)(2,1)}, u32[]{:S(2)}, u32[]{:S(2)}) collective-permute-start(bf16[4,4,128,512]{3,2,1,0:T(8,128)(2,1)} %bitcast.47.part_ref), channel_id=1, source_target_pairs={{0,4},{4,0},{8,12},{12,8},{16,20},{20,16},{24,28},{28,24},{1,5},{5... | collective-permute-start | bytes 6291464 | tf_op jit(solution)/shard_map/gate_lines/group_1/ppermute | solution.py:28
  475.2 33.5 %collective-permute-start.42 = (bf16[320,512]{1,0:T(8,128)(2,1)S(1)}, bf16[320,512]{1,0:T(8,128)(2,1)S(1)}, u32[]{:S(2)}, u32[]{:S(2)}) collective-permute-start(bf16[320,512]{1,0:T(8,128)(2,1)S(1)} %get-tuple-element.326), channel_id=1, source_target_pairs={{0,16},{4,20},{8,24},{12,28},{16,0},{20,4},{24,8},{28,12},{1,17},{... | collective-permute-start | bytes 983048 | tf_op jit(solution)/shard_map/tail/group_4/ppermute | solution.py:28
  477.5 45.4 %collective-permute-start.38 = (bf16[256,2048]{1,0:T(8,128)(2,1)}, bf16[256,2048]{1,0:T(8,128)(2,1)}, u32[]{:S(2)}, u32[]{:S(2)}) collective-permute-start(bf16[256,2048]{1,0:T(8,128)(2,1)} %get-tuple-element.237), channel_id=1, source_target_pairs={{0,2},{1,3},{2,0},{3,1},{4,6},{5,7},{6,4},{7,5},{8,10},{9,11},{10,... | collective-permute-start | bytes 3145736 | tf_op jit(solution)/shard_map/into/fsdp_2/ppermute | solution.py:28
  478.7 53.1 %collective-permute-start.41 = (bf16[256,2048]{1,0:T(8,128)(2,1)}, bf16[256,2048]{1,0:T(8,128)(2,1)}, u32[]{:S(2)}, u32[]{:S(2)}) collective-permute-start(bf16[256,2048]{1,0:T(8,128)(2,1)} %get-tuple-element.241), channel_id=1, source_target_pairs={{0,2},{1,3},{2,0},{3,1},{4,6},{5,7},{6,4},{7,5},{8,10},{9,11},{10,... | collective-permute-start | bytes 3145736 | tf_op jit(solution)/shard_map/into/fsdp_2/ppermute | solution.py:28
  503.3 151.6 %all-gather.11.cloned.1.call-start = ((), (), s32[]{:S(2)}) async-start(), calls=%async_computation.8 | async-start | bytes 4718592 | tf_op jit(solution)/shard_map/all_gather | solution.py:171
  566.7 70.2 %collective-permute-start.54 = (bf16[4,128,2048]{2,1,0:T(8,128)(2,1)}, bf16[4,128,2048]{2,1,0:T(8,128)(2,1)}, u32[]{:S(2)}, u32[]{:S(2)}) collective-permute-start(bf16[4,128,2048]{2,1,0:T(8,128)(2,1)} %bitcast.142), channel_id=1, source_target_pairs={{0,4},{4,0},{8,12},{12,8},{16,20},{20,16},{24,28},{28,24},{1,5},{5... | collective-permute-start | bytes 6291464 | tf_op jit(solution)/shard_map/out_lines/group_1/ppermute | solution.py:28
  578.1 26.3 %collective-permute-start.45 = (bf16[256,2048]{1,0:T(8,128)(2,1)}, bf16[256,2048]{1,0:T(8,128)(2,1)}, u32[]{:S(2)}, u32[]{:S(2)}) collective-permute-start(bf16[256,2048]{1,0:T(8,128)(2,1)} %get-tuple-element.266), channel_id=1, source_target_pairs={{0,2},{1,3},{2,0},{3,1},{4,6},{5,7},{6,4},{7,5},{8,10},{9,11},{10,... | collective-permute-start | bytes 3145736 | tf_op jit(solution)/shard_map/mixed/fsdp_2/ppermute | solution.py:28
  585.4 40.7 %collective-permute-start.48 = (bf16[256,2048]{1,0:T(8,128)(2,1)}, bf16[256,2048]{1,0:T(8,128)(2,1)}, u32[]{:S(2)}, u32[]{:S(2)}) collective-permute-start(bf16[256,2048]{1,0:T(8,128)(2,1)} %get-tuple-element.274), channel_id=1, source_target_pairs={{0,2},{1,3},{2,0},{3,1},{4,6},{5,7},{6,4},{7,5},{8,10},{9,11},{10,... | collective-permute-start | bytes 3145736 | tf_op jit(solution)/shard_map/mixed/fsdp_2/ppermute | solution.py:28
  (152 other events, 1803.8 us)
Sparse Core Ops, SparseCore 0:
  246.3 100.9 reduce-scatter.3
  349.8 43.6 reduce-scatter.5
  399.8 44.8 all-gather.6
  453.8 49.4 reduce-scatter.7
  504.8 50.7 all-gather.8
  566.2 88.6 all-gather.10
